TPU v7x, 32 devices: a whole 2x2x4 slice. The times are simulated.
32 devices in a mesh: dp: 8 (over z, core), tensor: 4 (over y, x).
Axes of the slice: x: 2, y: 2, z: 4, core: 2. Of those that a mesh axis runs over, the one named last changes fastest.
Arguments:
- tokens: bfloat16 [8192, 2048], P(('dp', 'tensor')), may hold values from -6 to 6
- lengths: int32 [8, 3], P('dp'), may hold values from 1 to 1022, as said below
- gain_one: float32 [2048], replicated, may hold values from 0.1 to 1.9
- w_query: bfloat16 [2048, 2048], P(None, 'tensor'), may hold values from -0.125 to 0.125
- w_key: bfloat16 [2048, 512], P(None, 'tensor'), may hold values from -0.125 to 0.125
- w_value: bfloat16 [2048, 512], P(None, 'tensor'), may hold values from -0.125 to 0.125
- w_out: bfloat16 [2048, 2048], P('tensor'), may hold values from -1.5 to 1.5
- gain_two: float32 [2048], replicated, may hold values from 0.1 to 1.9
- w_gate: bfloat16 [2048, 8192], P(None, 'tensor'), may hold values from -0.125 to 0.125
- w_up: bfloat16 [2048, 8192], P(None, 'tensor'), may hold values from -0.125 to 0.125
- w_down: bfloat16 [8192, 2048], P('tensor'), may hold values from -0.0625 to 0.0625
- cotangent: bfloat16 [8192, 2048], P(('dp', 'tensor')), may hold values from -6 to 6
Outputs:
- output: bfloat16 [8192, 2048], P(('dp', 'tensor'))
- grad_tokens: bfloat16 [8192, 2048], P(('dp', 'tensor'))
- grad_gain_one: float32 [2048], P(('dp', 'tensor'))
- grad_w_query: float32 [2048, 2048], P('dp', 'tensor')
- grad_w_key: float32 [2048, 512], P('dp', 'tensor')
- grad_w_value: float32 [2048, 512], P('dp', 'tensor')
- grad_w_out: float32 [2048, 2048], P('tensor', 'dp')
- grad_gain_two: float32 [2048], P(('dp', 'tensor'))
- grad_w_gate: float32 [2048, 8192], P('dp', 'tensor')
- grad_w_up: float32 [2048, 8192], P('dp', 'tensor')
- grad_w_down: float32 [8192, 2048], P('tensor', 'dp')
Inputs may be any that keep to these rules, and one draw needn't show every extreme that they name: Each group's 3 lengths are positive and sum to between 768 and 1024; some group sums to exactly 1024, and its two shorter documents hold one token each; in every group one document holds at least 512 tokens and the others at most 128; the slots after the last document are padding.
All inputs are finite; a program needn't handle non-finite values.
Results may differ from a plain program's by a relative error of at most 0.023.
Values may be sent and summed in bfloat16 or wider, within the bound.
A program may use at most 256 MiB of HBM per device.

v0:
```python
import math

import jax
import jax.numpy as jnp
from jax import lax
from jax.sharding import PartitionSpec as P

HD = 64


EPSILON = 1e-05
MASKED = -1e30


def product(operand, weights):
    return jnp.dot(operand, weights, preferred_element_type=jnp.float32)


def against(operand, weights):
    return lax.dot_general(
        operand, weights, (((1,), (1,)), ((), ())), preferred_element_type=jnp.float32
    )


def contract_rows(operand, weights):
    return lax.dot_general(
        operand, weights, (((0,), (0,)), ((), ())), preferred_element_type=jnp.float32
    )


def layout(length_row, group_rows):
    boundary = jnp.cumsum(length_row)
    token_place = jnp.arange(group_rows, dtype=jnp.int32)
    segment = jnp.sum((token_place[:, None] >= boundary[None, :]).astype(jnp.int32), axis=1)
    starts = jnp.concatenate([jnp.zeros((1,), jnp.int32), boundary])
    labels = jnp.arange(starts.shape[0], dtype=jnp.int32)
    seg_start = jnp.sum(jnp.where(segment[:, None] == labels[None, :], starts[None, :], 0), axis=1)
    return (segment, token_place, token_place - seg_start)


def rope_table(position, head_dim):
    half_dim = head_dim // 2
    freq_index = jnp.arange(half_dim, dtype=jnp.float32)
    base_freq = jnp.exp(-math.log(500000.0) * 2.0 * freq_index / head_dim)
    wavelength = 2.0 * math.pi / base_freq
    smooth = (8192.0 / wavelength - 1.0) / 3.0
    blended = (1.0 - smooth) * base_freq / 32.0 + smooth * base_freq
    frequency = jnp.where(
        wavelength < 2048.0, base_freq, jnp.where(wavelength > 8192.0, base_freq / 32.0, blended)
    )
    angles = position.astype(jnp.float32)[:, None] * frequency[None, :]
    return (jnp.cos(angles), jnp.sin(angles))


def rotate(heads_in, cos_table, sin_table):
    half_dim = heads_in.shape[-1] // 2
    first_half = heads_in[..., :half_dim]
    second_half = heads_in[..., half_dim:]
    cos_wide = cos_table[:, None, :]
    sin_wide = sin_table[:, None, :]
    return jnp.concatenate(
        [
            first_half * cos_wide - second_half * sin_wide,
            second_half * cos_wide + first_half * sin_wide,
        ],
        axis=-1,
    )


def unrotate(grads_in, cos_table, sin_table):
    half_dim = grads_in.shape[-1] // 2
    first_half = grads_in[..., :half_dim]
    second_half = grads_in[..., half_dim:]
    cos_wide = cos_table[:, None, :]
    sin_wide = sin_table[:, None, :]
    return jnp.concatenate(
        [
            first_half * cos_wide + second_half * sin_wide,
            second_half * cos_wide - first_half * sin_wide,
        ],
        axis=-1,
    )


def norm_rows(values_in, gain_vec):
    row_scale = lax.rsqrt(jnp.mean(values_in * values_in, axis=-1, keepdims=True) + EPSILON)
    return (row_scale, (values_in * row_scale * gain_vec).astype(jnp.bfloat16))


def norm_back(values_in, row_scale, gain_vec, grad_normed):
    unit_rows = values_in * row_scale
    scaled_grad = grad_normed * gain_vec
    grad_input = row_scale * (
        scaled_grad - unit_rows * jnp.mean(scaled_grad * unit_rows, axis=-1, keepdims=True)
    )
    return (grad_input, jnp.sum(grad_normed * unit_rows, axis=0))


def score_block(query_block, key_heads, seg_block, place_block, segment, token_place):
    raw_scores = jnp.einsum(
        "qkrd,skd->krqs", query_block, key_heads, preferred_element_type=jnp.float32
    )
    allowed = (seg_block[:, None] == segment[None, :]) & (
        token_place[None, :] <= place_block[:, None]
    )
    return jnp.where(allowed[None, None], raw_scores * 0.125, MASKED)


def attend(query_heads, key_heads, value_heads, segment, token_place, block_rows):
    group_rows = query_heads.shape[0]
    blocks = group_rows // block_rows

    def one_block(inputs):
        query_block, seg_block, place_block = inputs
        scores = score_block(query_block, key_heads, seg_block, place_block, segment, token_place)
        row_max = jnp.max(scores, axis=-1, keepdims=True)
        weights = jnp.exp(scores - row_max)
        row_sum = jnp.sum(weights, axis=-1, keepdims=True)
        rounded = (weights / row_sum).astype(jnp.bfloat16)
        attended_block = jnp.einsum(
            "krqs,skd->qkrd", rounded, value_heads, preferred_element_type=jnp.float32
        )
        return (attended_block.astype(jnp.bfloat16), (row_max + jnp.log(row_sum))[..., 0])

    stacked = (
        query_heads.reshape((blocks, block_rows) + query_heads.shape[1:]),
        segment.reshape(blocks, block_rows),
        token_place.reshape(blocks, block_rows),
    )
    attended, log_total = lax.map(one_block, stacked)
    return (attended.reshape(query_heads.shape), log_total)


def attend_back(
    query_heads, key_heads, value_heads, grad_attended, log_total, segment, token_place, block_rows
):
    group_rows = query_heads.shape[0]
    blocks = group_rows // block_rows

    def one_block(running, inputs):
        key_grad, value_grad = running
        query_block, grad_block, total_block, seg_block, place_block = inputs
        scores = score_block(query_block, key_heads, seg_block, place_block, segment, token_place)
        softmax_out = jnp.exp(scores - total_block[..., None])
        rounded = softmax_out.astype(jnp.bfloat16)
        grad_probs = jnp.einsum(
            "qkrd,skd->krqs", grad_block, value_heads, preferred_element_type=jnp.float32
        )
        row_dot = jnp.sum(softmax_out * grad_probs, axis=-1, keepdims=True)
        grad_scores = (0.125 * softmax_out * (grad_probs - row_dot)).astype(jnp.bfloat16)
        query_grad = jnp.einsum(
            "krqs,skd->qkrd", grad_scores, key_heads, preferred_element_type=jnp.float32
        )
        key_grad = key_grad + jnp.einsum(
            "krqs,qkrd->skd", grad_scores, query_block, preferred_element_type=jnp.float32
        )
        value_grad = value_grad + jnp.einsum(
            "krqs,qkrd->skd", rounded, grad_block, preferred_element_type=jnp.float32
        )
        return ((key_grad, value_grad), query_grad)

    initial = (jnp.zeros(key_heads.shape, jnp.float32), jnp.zeros(value_heads.shape, jnp.float32))
    stacked = (
        query_heads.reshape((blocks, block_rows) + query_heads.shape[1:]),
        grad_attended.reshape((blocks, block_rows) + grad_attended.shape[1:]),
        log_total,
        segment.reshape(blocks, block_rows),
        token_place.reshape(blocks, block_rows),
    )
    (key_grad, value_grad), query_grad = lax.scan(one_block, initial, stacked)
    return (query_grad.reshape(query_heads.shape), key_grad, value_grad)


def local(
    tokens,
    lengths,
    gain_one,
    w_query,
    w_key,
    w_value,
    w_out,
    gain_two,
    w_gate,
    w_up,
    w_down,
    cotangent,
):
    local_rows = tokens.shape[0]
    group_rows = local_rows * lax.axis_size("tensor")
    block_rows = min(512, group_rows)
    heads_local = w_query.shape[1] // HD
    kv_local = w_key.shape[1] // HD
    repeat = heads_local // kv_local
    segment, token_place, position = layout(lengths[0], group_rows)
    cos_table, sin_table = rope_table(position, HD)
    x_rows = tokens.astype(jnp.float32)
    scale_one, normed_one = norm_rows(x_rows, gain_one)
    gathered_one = lax.all_gather(normed_one, "tensor", axis=0, tiled=True)
    query_raw = product(gathered_one, w_query).reshape(group_rows, heads_local, HD)
    key_raw = product(gathered_one, w_key).reshape(group_rows, kv_local, HD)
    query_heads = (
        rotate(query_raw, cos_table, sin_table)
        .astype(jnp.bfloat16)
        .reshape(group_rows, kv_local, repeat, HD)
    )
    key_heads = rotate(key_raw, cos_table, sin_table).astype(jnp.bfloat16)
    value_heads = (
        product(gathered_one, w_value).astype(jnp.bfloat16).reshape(group_rows, kv_local, HD)
    )
    attended, log_total = attend(
        query_heads, key_heads, value_heads, segment, token_place, block_rows
    )
    attended_flat = attended.reshape(group_rows, heads_local * HD)
    mixed = lax.psum_scatter(
        product(attended_flat, w_out).astype(jnp.bfloat16),
        "tensor",
        scatter_dimension=0,
        tiled=True,
    ).astype(jnp.float32)
    hidden_state = x_rows + mixed
    scale_two, normed_two = norm_rows(hidden_state, gain_two)
    gathered_two = lax.all_gather(normed_two, "tensor", axis=0, tiled=True)
    gate_proj = product(gathered_two, w_gate)
    up_proj = product(gathered_two, w_up)
    sigmoid_gate = jax.nn.sigmoid(gate_proj)
    activated = gate_proj * sigmoid_gate
    hidden = (activated * up_proj).astype(jnp.bfloat16)
    output_rows = hidden_state + lax.psum_scatter(
        product(hidden, w_down).astype(jnp.bfloat16), "tensor", scatter_dimension=0, tiled=True
    ).astype(jnp.float32)
    grad_gathered = lax.all_gather(cotangent, "tensor", axis=0, tiled=True)
    grad_w_down = contract_rows(hidden, grad_gathered)
    grad_hidden = against(grad_gathered, w_down)
    grad_gate = (
        grad_hidden * up_proj * sigmoid_gate * (1.0 + gate_proj * (1.0 - sigmoid_gate))
    ).astype(jnp.bfloat16)
    grad_up = (grad_hidden * activated).astype(jnp.bfloat16)
    grad_w_gate = contract_rows(gathered_two, grad_gate)
    grad_w_up = contract_rows(gathered_two, grad_up)
    grad_normed_two = lax.psum_scatter(
        (against(grad_gate, w_gate) + against(grad_up, w_up)).astype(jnp.bfloat16),
        "tensor",
        scatter_dimension=0,
        tiled=True,
    ).astype(jnp.float32)
    grad_state_norm, grad_gain_two = norm_back(hidden_state, scale_two, gain_two, grad_normed_two)
    grad_state = cotangent.astype(jnp.float32) + grad_state_norm
    grad_mixed = grad_state.astype(jnp.bfloat16)
    grad_mixed_all = lax.all_gather(grad_mixed, "tensor", axis=0, tiled=True)
    grad_w_out = contract_rows(attended_flat, grad_mixed_all)
    grad_attended = (
        against(grad_mixed_all, w_out)
        .astype(jnp.bfloat16)
        .reshape(group_rows, kv_local, repeat, HD)
    )
    grad_queries, grad_keys, grad_values = attend_back(
        query_heads,
        key_heads,
        value_heads,
        grad_attended,
        log_total,
        segment,
        token_place,
        block_rows,
    )
    grad_query_raw = (
        unrotate(grad_queries.reshape(group_rows, heads_local, HD), cos_table, sin_table)
        .astype(jnp.bfloat16)
        .reshape(group_rows, heads_local * HD)
    )
    grad_key_raw = (
        unrotate(grad_keys, cos_table, sin_table)
        .astype(jnp.bfloat16)
        .reshape(group_rows, kv_local * HD)
    )
    grad_value_raw = grad_values.astype(jnp.bfloat16).reshape(group_rows, kv_local * HD)
    grad_w_query = contract_rows(gathered_one, grad_query_raw)
    grad_w_key = contract_rows(gathered_one, grad_key_raw)
    grad_w_value = contract_rows(gathered_one, grad_value_raw)
    grad_normed_one = lax.psum_scatter(
        (
            against(grad_query_raw, w_query)
            + against(grad_key_raw, w_key)
            + against(grad_value_raw, w_value)
        ).astype(jnp.bfloat16),
        "tensor",
        scatter_dimension=0,
        tiled=True,
    ).astype(jnp.float32)
    grad_input_norm, grad_gain_one = norm_back(x_rows, scale_one, gain_one, grad_normed_one)
    grad_tokens = (grad_state + grad_input_norm).astype(jnp.bfloat16)
    gain_grads = lax.psum_scatter(
        jnp.stack([grad_gain_one, grad_gain_two]), ("dp", "tensor"), scatter_dimension=1, tiled=True
    )
    weight_grads = (
        lax.psum_scatter(
            grad_w_query.astype(jnp.bfloat16), "dp", scatter_dimension=0, tiled=True
        ).astype(jnp.float32),
        lax.psum_scatter(
            grad_w_key.astype(jnp.bfloat16), "dp", scatter_dimension=0, tiled=True
        ).astype(jnp.float32),
        lax.psum_scatter(
            grad_w_value.astype(jnp.bfloat16), "dp", scatter_dimension=0, tiled=True
        ).astype(jnp.float32),
        lax.psum_scatter(
            grad_w_out.astype(jnp.bfloat16), "dp", scatter_dimension=1, tiled=True
        ).astype(jnp.float32),
        lax.psum_scatter(
            grad_w_gate.astype(jnp.bfloat16), "dp", scatter_dimension=0, tiled=True
        ).astype(jnp.float32),
        lax.psum_scatter(
            grad_w_up.astype(jnp.bfloat16), "dp", scatter_dimension=0, tiled=True
        ).astype(jnp.float32),
        lax.psum_scatter(
            grad_w_down.astype(jnp.bfloat16), "dp", scatter_dimension=1, tiled=True
        ).astype(jnp.float32),
    )
    return (
        output_rows.astype(jnp.bfloat16),
        grad_tokens,
        gain_grads[0],
        weight_grads[0],
        weight_grads[1],
        weight_grads[2],
        weight_grads[3],
        gain_grads[1],
        weight_grads[4],
        weight_grads[5],
        weight_grads[6],
    )


def solution(mesh):
    return jax.shard_map(
        local,
        mesh=mesh,
        in_specs=(
            P(("dp", "tensor"), None),
            P("dp", None),
            P(),
            P(None, "tensor"),
            P(None, "tensor"),
            P(None, "tensor"),
            P("tensor", None),
            P(),
            P(None, "tensor"),
            P(None, "tensor"),
            P("tensor", None),
            P(("dp", "tensor"), None),
        ),
        out_specs=(
            P(("dp", "tensor"), None),
            P(("dp", "tensor"), None),
            P(("dp", "tensor")),
            P("dp", "tensor"),
            P("dp", "tensor"),
            P("dp", "tensor"),
            P("tensor", "dp"),
            P(("dp", "tensor")),
            P("dp", "tensor"),
            P("dp", "tensor"),
            P("tensor", "dp"),
        ),
        check_vma=False,
    )
```

profile of v0, /device:TPU:0, one launch (start us, length us, event | category | flops | bytes accessed | tf_op | source)
XLA Modules:
  0.0 1258.8 jit_solution(6947928369219775657)
XLA Ops:
  12.6 54.4 %all-gather.5.cloned.1.call-done = bf16[1024,2048]{1,0:T(8,128)(2,1)} async-done(((bf16[256,2048]{1,0:T(8,128)(2,1)}), bf16[1024,2048]{1,0:T(8,128)(2,1)}) %all-gather.5.cloned.1.call-update) | async-done | bytes 4194320 | tf_op jit(solution)/shard_map/all_gather | solution.py:198
  84.1 30.1 %while.28 = (s32[]{:T(128)}, bf16[2,512,2,4,64]{1,4,3,2,0:T(8,128)(2,1)}, f32[2,2,4,512]{3,2,1,0:T(4,128)S(1)}, s32[2,512]{1,0:T(2,128)S(1)}, s32[1024]{0:T(1024...) while((s32[]{:T(128)}, ...), condition=%wide.region_7.8_spmd.clone, body=%wide.region_4.7_spmd.clone.sunk | while | flops 1125904384 | bytes 62537908 | solution.py:130
  122.2 52.8 %reduce-scatter.15.cloned.1.call-done = bf16[256,2048]{1,0:T(8,128)(2,1)} async-done(((bf16[1024,2048]{1,0:T(8,128)(2,1)}), bf16[256,2048]{1,0:T(8,128)(2,1)}) %reduce-scatter.15.cloned.1.call-update) | async-done | bytes 1048592 | tf_op jit(solution)/shard_map/reduce_scatter | solution.py:214
  180.5 52.2 %all-gather.7.cloned.1.call-done = bf16[1024,2048]{1,0:T(8,128)(2,1)} async-done(((bf16[256,2048]{1,0:T(8,128)(2,1)}), bf16[1024,2048]{1,0:T(8,128)(2,1)}) %all-gather.7.cloned.1.call-update) | async-done | bytes 4194320 | tf_op jit(solution)/shard_map/all_gather | solution.py:222
  232.8 15.9 %fusion.79 = f32[1024,2048]{1,0:T(8,128)} fusion(bf16[1024,2048]{1,0:T(8,128)(2,1)} %all-gather.7.cloned.1.call-done, bf16[2048,2048]{1,0:T(8,128)(2,1)} %param.25), kind=kOutput, calls=%fused_computation.143 | convolution fusion | flops 8589934592 | bytes 20971520 | tf_op jit(solution)/shard_map/dot_general | solution.py:16
  262.0 25.4 %all-gather.9.cloned.1.call-done = bf16[1024,2048]{1,0:T(8,128)(2,1)} async-done(((bf16[256,2048]{1,0:T(8,128)(2,1)}), bf16[1024,2048]{1,0:T(8,128)(2,1)}) %all-gather.9.cloned.1.call-update) | async-done | bytes 4194320 | tf_op jit(solution)/shard_map/all_gather | solution.py:231
  287.4 21.8 %multiply_convert_fusion = (bf16[1024,2048]{1,0:T(8,128)(2,1)}, bf16[1024,2048]{1,0:T(8,128)(2,1)}, bf16[1024,2048]{1,0:T(8,128)(2,1)}) fusion(f32[1024,2048]{1,0:T(8,128)} %fusion.78, f32[1024,2048]{1,0:T(8,128)} %fusion.79, bf16[1024,2048]{1,0:T(8,128)(2,1)} %all-gather.9.cloned.1.call-done, bf16[2048,2048]{1,0:T(8,128)(2,1)} %param.26), kind=kOutput, calls=%fused_computation.66 | convolution fusion | flops 8621391872 | bytes 41943040 | tf_op jit(solution)/shard_map/dot_general | solution.py:20
  335.0 52.8 %reduce-scatter.19.cloned.1.call-done = bf16[256,2048]{1,0:T(8,128)(2,1)} async-done(((bf16[1024,2048]{1,0:T(8,128)(2,1)}), bf16[256,2048]{1,0:T(8,128)(2,1)}) %reduce-scatter.19.cloned.1.call-update) | async-done | bytes 1048592 | tf_op jit(solution)/shard_map/reduce_scatter | solution.py:240
  395.5 52.8 %all-gather.11.cloned.1.call-done = bf16[1024,2048]{1,0:T(8,128)(2,1)} async-done(((bf16[256,2048]{1,0:T(8,128)(2,1)}), bf16[1024,2048]{1,0:T(8,128)(2,1)}) %all-gather.11.cloned.1.call-update) | async-done | bytes 4194320 | tf_op jit(solution)/shard_map/all_gather | solution.py:249
  460.1 130.3 %while.29 = (s32[]{:T(128)}, f32[1024,2,64]{0,2,1:T(8,128)}, f32[1024,2,64]{0,2,1:T(8,128)}, f32[2,512,2,4,64]{1,0,4,3,2:T(2,128)}, bf16[2,512,2,4,64]{1,4,3,2,0...) while((s32[]{:T(128)}, f32[1024,2,64]{0,2,1:T(8,128)}, ...), condition=%wide.region_15.16_spmd.clone, body=%wide.region_13.15_spmd.clone.sunk | while | flops 2753556480 | bytes 144572672 | solution.py:170
  505.3 19.6 %dynamic_update_slice.22 = f32[2,512,2,4,64]{1,0,4,3,2:T(2,128)} dynamic-update-slice(f32[2,512,2,4,64]{1,0,4,3,2:T(2,128)} %get-tuple-element.536, f32[1,512,2,4,64]{1,0,4,3,2:T(1,128)S(1)} %copy.64, s32[]{:T(128)S(6)} %copy.81, s32[]{:T(128)} %constant.74.clone.1..sunk, s32[]{:T(128)} %constant.74.clone.1..sunk, s32[]{:T(128)} %constant.74.clone.1..sunk, s32[]{:T(128)} %constant.74.clone.1..sunk) | dynamic-update-slice | bytes 2097156 | tf_op jit(solution)/shard_map/while/body/jit(dynamic_update_index_in_dim)/dynamic_update_slice | solution.py:170
  570.7 19.6 %dynamic_update_slice.22 = f32[2,512,2,4,64]{1,0,4,3,2:T(2,128)} dynamic-update-slice(f32[2,512,2,4,64]{1,0,4,3,2:T(2,128)} %get-tuple-element.536, f32[1,512,2,4,64]{1,0,4,3,2:T(1,128)S(1)} %copy.64, s32[]{:T(128)S(6)} %copy.81, s32[]{:T(128)} %constant.74.clone.1..sunk, s32[]{:T(128)} %constant.74.clone.1..sunk, s32[]{:T(128)} %constant.74.clone.1..sunk, s32[]{:T(128)} %constant.74.clone.1..sunk) | dynamic-update-slice | bytes 2097156 | tf_op jit(solution)/shard_map/while/body/jit(dynamic_update_index_in_dim)/dynamic_update_slice | solution.py:170
  601.5 14.1 %convolution_convert_fusion = bf16[2048,2048]{1,0:T(8,128)(2,1)} fusion(bf16[1024,2048]{1,0:T(8,128)(2,1)} %get-tuple-element.330, bf16[1024,2048]{1,0:T(8,128)(2,1)} %all-gather.9.cloned.1.call-done), kind=kOutput, calls=%fused_computation.71 | convolution fusion | flops 8594128896 | bytes 16777216 | tf_op jit(solution)/shard_map/dot_general | solution.py:26
  615.6 14.1 %convolution_convert_fusion.1 = bf16[2048,2048]{1,0:T(8,128)(2,1)} fusion(bf16[1024,2048]{1,0:T(8,128)(2,1)} %all-gather.7.cloned.1.call-done, bf16[1024,2048]{1,0:T(8,128)(2,1)} %get-tuple-element.328), kind=kOutput, calls=%fused_computation.72 | convolution fusion | flops 8594128896 | bytes 16777216 | tf_op jit(solution)/shard_map/dot_general | solution.py:26
  629.8 14.3 %convolution_convert_fusion.2 = bf16[2048,2048]{1,0:T(8,128)(2,1)} fusion(bf16[1024,2048]{1,0:T(8,128)(2,1)} %all-gather.7.cloned.1.call-done, bf16[1024,2048]{1,0:T(8,128)(2,1)} %get-tuple-element.329), kind=kOutput, calls=%fused_computation.73 | convolution fusion | flops 8594128896 | bytes 16777216 | tf_op jit(solution)/shard_map/dot_general | solution.py:26
  668.1 13.9 %convolution_convert_fusion.3 = bf16[1024,2048]{1,0:T(8,128)(2,1)} fusion(bf16[1024,2048]{1,0:T(8,128)(2,1)} %get-tuple-element.330, bf16[2048,2048]{1,0:T(8,128)(2,1)} %param.26), kind=kOutput, calls=%fused_computation.74 | convolution fusion | flops 8592031744 | bytes 16777216 | tf_op jit(solution)/shard_map/dot_general | solution.py:16
  685.1 64.3 %reduce-scatter.35.cloned.1.call-done = bf16[2048,256]{1,0:T(8,128)(2,1)} async-done(((bf16[2048,2048]{1,0:T(8,128)(2,1)}), bf16[2048,256]{1,0:T(8,128)(2,1)}) %reduce-scatter.35.cloned.1.call-update) | async-done | bytes 1048592 | tf_op jit(solution)/shard_map/reduce_scatter | solution.py:314
  752.1 87.4 %reduce-scatter.33.cloned.1.call-done = bf16[256,2048]{1,0:T(8,128)(2,1)} async-done(((bf16[2048,2048]{1,0:T(8,128)(2,1)}), bf16[256,2048]{1,0:T(8,128)(2,1)}) %reduce-scatter.33.cloned.1.call-update) | async-done | bytes 1048592 | tf_op jit(solution)/shard_map/reduce_scatter | solution.py:311
  842.3 87.5 %reduce-scatter.31.cloned.1.call-done = bf16[256,2048]{1,0:T(8,128)(2,1)} async-done(((bf16[2048,2048]{1,0:T(8,128)(2,1)}), bf16[256,2048]{1,0:T(8,128)(2,1)}) %reduce-scatter.31.cloned.1.call-update) | async-done | bytes 1048592 | tf_op jit(solution)/shard_map/reduce_scatter | solution.py:308
  932.6 33.5 %reduce-scatter.29.cloned.1.call-done = bf16[512,256]{1,0:T(8,128)(2,1)} async-done(((bf16[512,2048]{1,0:T(8,128)(2,1)}), bf16[512,256]{1,0:T(8,128)(2,1)}) %reduce-scatter.29.cloned.1.call-update) | async-done | bytes 262160 | tf_op jit(solution)/shard_map/reduce_scatter | solution.py:305
  967.9 35.0 %reduce-scatter.23.cloned.1.call-done = bf16[256,512]{1,0:T(8,128)(2,1)} async-done(((bf16[2048,512]{1,0:T(8,128)(2,1)}), bf16[256,512]{1,0:T(8,128)(2,1)}) %reduce-scatter.23.cloned.1.call-update) | async-done | bytes 262160 | tf_op jit(solution)/shard_map/reduce_scatter | solution.py:296
  1004.7 52.3 %reduce-scatter.21.cloned.1.call-done = bf16[256,2048]{1,0:T(8,128)(2,1)} async-done(((bf16[1024,2048]{1,0:T(8,128)(2,1)}), bf16[256,2048]{1,0:T(8,128)(2,1)}) %reduce-scatter.21.cloned.1.call-update) | async-done | bytes 1048592 | tf_op jit(solution)/shard_map/reduce_scatter | solution.py:280
  1060.5 52.3 %reduce-scatter.17.cloned.1.call-done = bf16[256,2048]{1,0:T(8,128)(2,1)} async-done(((bf16[1024,2048]{1,0:T(8,128)(2,1)}), bf16[256,2048]{1,0:T(8,128)(2,1)}) %reduce-scatter.17.cloned.1.call-update) | async-done | bytes 1048592 | tf_op jit(solution)/shard_map/reduce_scatter | solution.py:228
  1118.3 131.4 %reduce-scatter.37.cloned.1.call-done = f32[64,2]{1,0:T(8,128)} async-done(((f32[2048,2]{1,0:T(8,128)}), f32[64,2]{1,0:T(8,128)}) %reduce-scatter.37.cloned.1.call-update) | async-done | bytes 528
  (222 shorter events, 275.5 us)
Async XLA Ops:
  7.2 59.8 %all-gather.5.cloned.1.call-start = ((), (), s32[]{:S(2)}) async-start(), calls=%async_computation.12 | async-start | bytes 5242880 | tf_op jit(solution)/shard_map/all_gather | solution.py:198
  11.5 163.5 %reduce-scatter.15.cloned.1.call-start = ((), (), s32[]{:S(2)}) async-start(), calls=%async_computation.13 | async-start | bytes 5242880 | tf_op jit(solution)/shard_map/reduce_scatter | solution.py:214
  122.1 110.6 %all-gather.7.cloned.1.call-start = ((), (), s32[]{:S(2)}) async-start(), calls=%async_computation.14 | async-start | bytes 5242880 | tf_op jit(solution)/shard_map/all_gather | solution.py:222
  177.0 214.2 %copy-start.27 = (f32[256]{0:T(256)}, f32[256]{0:T(256)S(1)}, u32[]{:S(2)}) copy-start(f32[256]{0:T(256)S(1)} %add_rsqrt_fusion) | copy-start | bytes 3076
  179.9 107.4 %all-gather.9.cloned.1.call-start = ((), (), s32[]{:S(2)}) async-start(), calls=%async_computation.16 | async-start | bytes 5242880 | tf_op jit(solution)/shard_map/all_gather | solution.py:231
  180.5 207.3 %reduce-scatter.19.cloned.1.call-start = ((), (), s32[]{:S(2)}) async-start(), calls=%async_computation.17 | async-start | bytes 5242880 | tf_op jit(solution)/shard_map/reduce_scatter | solution.py:240
  335.0 113.3 %all-gather.11.cloned.1.call-start = ((), (), s32[]{:S(2)}) async-start(), calls=%async_computation.18 | async-start | bytes 5242880 | tf_op jit(solution)/shard_map/all_gather | solution.py:249
  395.5 286.6 %reduce-scatter.27.cloned.1.call-start = ((), (), s32[]{:S(2)}) async-start(), calls=%async_computation.22 | async-start | bytes 589824 | tf_op jit(solution)/shard_map/reduce_scatter | solution.py:302
  595.9 87.7 %reduce-scatter.25.cloned.1.call-start = ((), (), s32[]{:S(2)}) async-start(), calls=%async_computation.21 | async-start | bytes 589824 | tf_op jit(solution)/shard_map/reduce_scatter | solution.py:299
  601.4 147.9 %reduce-scatter.35.cloned.1.call-start = ((), (), s32[]{:S(2)}) async-start(), calls=%async_computation.26 | async-start | bytes 9437184 | tf_op jit(solution)/shard_map/reduce_scatter | solution.py:314
  615.6 223.9 %reduce-scatter.33.cloned.1.call-start = ((), (), s32[]{:S(2)}) async-start(), calls=%async_computation.25 | async-start | bytes 9437184 | tf_op jit(solution)/shard_map/reduce_scatter | solution.py:311
  629.7 300.1 %reduce-scatter.31.cloned.1.call-start = ((), (), s32[]{:S(2)}) async-start(), calls=%async_computation.24 | async-start | bytes 9437184 | tf_op jit(solution)/shard_map/reduce_scatter | solution.py:308
  644.1 322.0 %reduce-scatter.29.cloned.1.call-start = ((), (), s32[]{:S(2)}) async-start(), calls=%async_computation.23 | async-start | bytes 2359296 | tf_op jit(solution)/shard_map/reduce_scatter | solution.py:305
  651.2 351.7 %reduce-scatter.23.cloned.1.call-start = ((), (), s32[]{:S(2)}) async-start(), calls=%async_computation.20 | async-start | bytes 2359296 | tf_op jit(solution)/shard_map/reduce_scatter | solution.py:296
  660.4 396.6 %reduce-scatter.21.cloned.1.call-start = ((), (), s32[]{:S(2)}) async-start(), calls=%async_computation.19 | async-start | bytes 5242880 | tf_op jit(solution)/shard_map/reduce_scatter | solution.py:280
  668.1 444.7 %reduce-scatter.17.cloned.1.call-start = ((), (), s32[]{:S(2)}) async-start(), calls=%async_computation.15 | async-start | bytes 5242880 | tf_op jit(solution)/shard_map/reduce_scatter | solution.py:228
  682.0 567.8 %reduce-scatter.37.cloned.1.call-start = ((), (), s32[]{:S(2)}) async-start(), calls=%async_computation.27 | async-start | bytes 1081344
  752.1 304.9 %copy-start.2 = (bf16[256,2048]{1,0:T(8,128)(2,1)S(1)}, bf16[256,2048]{1,0:T(8,128)(2,1)}, u32[]{:S(2)}) copy-start(bf16[256,2048]{1,0:T(8,128)(2,1)} %param.16) | copy-start | bytes 3145732
  752.1 304.9 %copy-start.25 = (f32[2048]{0:T(1024)S(1)}, f32[2048]{0:T(1024)}, u32[]{:S(2)}) copy-start(f32[2048]{0:T(1024)} %param.18) | copy-start | bytes 24580
  752.1 304.9 %copy-start.30 = (f32[256]{0:T(256)S(1)}, f32[256]{0:T(256)}, u32[]{:S(2)}) copy-start(f32[256]{0:T(256)} %copy-done.29) | copy-start | bytes 3076
  842.3 216.8 %copy-start.26 = (f32[2048]{0:T(1024)S(1)}, f32[2048]{0:T(1024)}, u32[]{:S(2)}) copy-start(f32[2048]{0:T(1024)} %get-tuple-element.274) | copy-start | bytes 24580
  842.3 270.5 %copy-start.24 = (f32[2048]{0:T(1024)S(1)}, f32[2048]{0:T(1024)}, u32[]{:S(2)}) copy-start(f32[2048]{0:T(1024)} %param.23) | copy-start | bytes 24580
  842.3 270.5 %copy-start.28 = (f32[256]{0:T(256)S(1)}, f32[256]{0:T(256)}, u32[]{:S(2)}) copy-start(f32[256]{0:T(256)} %copy-done.27) | copy-start | bytes 3076
  842.3 270.5 %copy-start.32 = (f32[256]{0:T(256)S(1)}, f32[256]{0:T(256)}, u32[]{:S(2)}) copy-start(f32[256]{0:T(256)} %copy-done.31) | copy-start | bytes 3076
  (35 other events, 753.2 us)
Sparse Core Ops, SparseCore 0:
  11.6 55.3 all-gather.4
  122.3 52.6 reduce-scatter.14
  180.0 52.6 all-gather.6
  234.6 52.6 all-gather.8
  335.1 52.6 reduce-scatter.18
  395.6 52.6 all-gather.10
  596.0 30.9 reduce-scatter.26
  629.9 29.1 reduce-scatter.24
  661.4 87.8 reduce-scatter.34
  751.5 87.9 reduce-scatter.32
  841.8 87.9 reduce-scatter.30
  932.0 34.0 reduce-scatter.28
  968.4 34.4 reduce-scatter.22
  1005.7 51.2 reduce-scatter.20
  1060.1 52.6 reduce-scatter.16
  1114.9 134.8 reduce-scatter.36
where the time goes:
time: 1270 us; the launch traced here: 1260 us
  waiting for transfers between devices  835 us (66%)
  matrix products  257 us (20%)
  other arithmetic  80.6 us (6%)
  local copies, waits for them, and re-layouts  69 us (5%)
  between operations  14.9 us (1%)
    unnamed x17, waiting for transfers between devices  132 us
    reduce_scatter x1, waiting for transfers between devices, local(): lax.psum_scatter(grad_w_gate.astype(jnp.bfloat16), 'dp', scatter_dimensio...  87.5 us
    reduce_scatter x1, waiting for transfers between devices, local(): lax.psum_scatter(grad_w_up.astype(jnp.bfloat16), 'dp', scatter_dimension=...  87.4 us
    reduce_scatter x1, waiting for transfers between devices, local(): lax.psum_scatter(grad_w_down.astype(jnp.bfloat16), 'dp', scatter_dimensio...  64.3 us
    dot_general x7, matrix products, contract_rows(): lax.dot_general(operand, weights, (((0,), (0,)), ((), ())), preferred_ele...  60.8 us
    dot_general x7, matrix products, against(): lax.dot_general(operand, weights, (((1,), (1,)), ((), ())), preferred_ele...  60.1 us
    dot_general x7, matrix products, product(): return jnp.dot(operand, weights, preferred_element_type=jnp.float32)  55.2 us
    all_gather x1, waiting for transfers between devices, local(): gathered_one = lax.all_gather(normed_one, 'tensor', axis=0, tiled=True)  54.4 us
  transfers between devices with their start and end apart: 16, of which 14 were waited for; matrix products, arithmetic and copies ran while one was open for 11% of the time, Pallas kernels for 0%

commit v1 on v0

v1 whole, which is shorter than its diff:
```python
import functools
import math

import jax
import jax.numpy as jnp
import numpy as np
from jax import lax
from jax.experimental import pallas as pl
from jax.experimental.pallas import tpu as pltpu
from jax.sharding import PartitionSpec as P

HD = 64
LANES = 128
EPSILON = 1e-05
MASKED = -1e30
LOG2E = math.log2(math.e)
SCALE2 = 0.125 * LOG2E
BF16 = jnp.bfloat16
F32 = jnp.float32
MESH = pl.DeviceIdType.MESH
VMEM_LIMIT = 60 * 2**20


def dot_nn(a, b):
    return jnp.dot(a, b, preferred_element_type=F32)


def dot_nt(a, b):
    return lax.dot_general(a, b, (((1,), (1,)), ((), ())), preferred_element_type=F32)


def dot_tn(a, b):
    return lax.dot_general(a, b, (((0,), (0,)), ((), ())), preferred_element_type=F32)


def layout(length_row, group_rows):
    token_place = jnp.arange(group_rows, dtype=jnp.int32)
    start = jnp.zeros((group_rows,), jnp.int32)
    end = jnp.int32(0)
    for k in range(length_row.shape[0]):
        end = end + length_row[k]
        start = jnp.where(token_place >= end, end, start)
    return (start, token_place - start)


def rope_table(position):
    half_dim = HD // 2
    freq_index = jnp.arange(half_dim, dtype=F32)
    base_freq = jnp.exp(-math.log(500000.0) * 2.0 * freq_index / HD)
    wavelength = 2.0 * math.pi / base_freq
    smooth = (8192.0 / wavelength - 1.0) / 3.0
    blended = (1.0 - smooth) * base_freq / 32.0 + smooth * base_freq
    frequency = jnp.where(
        wavelength < 2048.0, base_freq, jnp.where(wavelength > 8192.0, base_freq / 32.0, blended)
    )
    angles = position.astype(F32)[:, None] * frequency[None, :]
    cos_half, sin_half = (jnp.cos(angles), jnp.sin(angles))
    return (
        jnp.concatenate([cos_half] * 4, axis=1),
        jnp.concatenate([-sin_half, sin_half, -sin_half, sin_half], axis=1),
    )


class Peers:
    def __init__(self):
        self.n = lax.axis_size("tensor")
        self.m = self.n // 2
        index = lax.axis_index("tensor")
        self.y = lax.div(index, np.int32(self.m))
        self.x = lax.rem(index, np.int32(self.m))

    def at(self, flip, step):
        row = 1 - self.y if flip else self.y
        return row * self.m + lax.rem(self.x + np.int32(step + self.m), np.int32(self.m))

    def minor(self, step):
        return {"tensor": self.at(0, step)}

    def major(self):
        return {"tensor": self.at(1, 0)}

    def steps(self):
        return range(1, self.m)


def core_of():
    return lax.rem(lax.axis_index("dp"), np.int32(2))


def other_core():
    return {"dp": lax.axis_index("dp") + 1 - 2 * core_of()}


def greet(peers, core=False):
    barrier = pltpu.get_barrier_semaphore()
    for step in peers.steps():
        pl.semaphore_signal(barrier, inc=1, device_id=peers.minor(step), device_id_type=MESH)
    pl.semaphore_signal(barrier, inc=1, device_id=peers.major(), device_id_type=MESH)
    if core:
        pl.semaphore_signal(barrier, inc=1, device_id=other_core(), device_id_type=MESH)
    pl.semaphore_wait(barrier, peers.m + (1 if core else 0))


class Wire:
    def __init__(self, send_sem, recv_sem):
        self.send_sem, self.recv_sem, self.copies = send_sem, recv_sem, []

    def copy(self, source, target, device):
        k = len(self.copies)
        copy = pltpu.make_async_remote_copy(
            src_ref=source,
            dst_ref=target,
            send_sem=self.send_sem.at[k],
            recv_sem=self.recv_sem.at[k],
            device_id=device,
            device_id_type=MESH,
        )
        copy.start()
        self.copies.append(copy)
        return copy

    def wait_sends(self):
        for copy in self.copies:
            copy.wait_send()


def wire_count(n):
    return 4 * (n // 2 - 1) + 2


def wires(n):
    return [pltpu.SemaphoreType.DMA((wire_count(n),))] * 2


class Local:
    def __init__(self, sem):
        self.sem, self.copies = sem, []

    def copy(self, source, target):
        copy = pltpu.make_async_copy(source, target, self.sem.at[len(self.copies)])
        copy.start()
        self.copies.append(copy)
        return copy


def block(ref, index, rows):
    return ref.at[pl.ds(pl.multiple_of(index * rows, rows), rows)]


def half_block(ref, index, rows, half):
    size = rows // 2
    return ref.at[pl.ds(pl.multiple_of(index * rows + half * size, size), size)]


def gather(peers, wire, buf, rows, use, after_forward=None):
    steps = list(peers.steps())
    part = lambda index, half: half_block(buf, index, rows, half)
    me, major = peers.at(0, 0), peers.at(1, 0)
    send = lambda ref, device: wire.copy(ref, ref, device)
    minor_a = [send(part(me, 0), peers.minor(j)) for j in steps]
    major_b = send(part(me, 1), peers.major())
    minor_b = [send(part(me, 1), peers.minor(j)) for j in steps]
    major_a = send(part(me, 0), peers.major())
    use(me)
    forward_a, forward_b = [], []
    for j, copy in zip(steps, minor_a):
        copy.wait_recv()
        forward_a.append(send(part(peers.at(0, -j), 0), peers.major()))
    major_b.wait_recv()
    for j in steps:
        forward_b.append(send(part(major, 1), peers.minor(j)))
    if after_forward is not None:
        after_forward()
    for j, copy in zip(steps, minor_b):
        copy.wait_recv()
        use(peers.at(0, -j))
    major_a.wait_recv()
    use(major)
    for j, copy_a, copy_b in zip(steps, forward_a, forward_b):
        copy_a.wait_recv()
        copy_b.wait_recv()
        use(peers.at(1, -j))


def add_rows(target, others, size):
    def some(k, carry):
        at = pl.ds(pl.multiple_of(k * 16, 16), 16)
        total = target[at, :].astype(F32)
        for other in others:
            total = total + other[at, :].astype(F32)
        target[at, :] = total.astype(target.dtype)
        return carry

    lax.fori_loop(0, size // 16, some, 0)


def scatter(peers, wire, part_ref, slots, rows, make, meanwhile=None):
    steps = list(peers.steps())
    part = lambda index, half: half_block(part_ref, index, rows, half)
    me, major = peers.at(0, 0), peers.at(1, 0)
    count = len(steps)
    via_a, via_b, direct_b, sum_a = (
        [slots.at[group * count + k] for k in range(count)] for group in range(4)
    )
    direct_a, sum_b = slots.at[4 * count], slots.at[4 * count + 1]
    make((1 - peers.y) * peers.m, peers.m)
    first_a, first_b = [], []
    for k, j in enumerate(steps):
        index = peers.at(1, j)
        first_a.append(wire.copy(part(index, 0), via_a[k], peers.major()))
        first_b.append(wire.copy(part(index, 1), via_b[k], peers.minor(j)))
    plain_a = wire.copy(part(major, 0), direct_a, peers.major())
    make(peers.y * peers.m, peers.m)
    plain_b = [
        wire.copy(part(peers.at(0, j), 1), direct_b[k], peers.minor(j))
        for k, j in enumerate(steps)
    ]
    done_a = []
    for k, j in enumerate(steps):
        first_a[k].wait_recv()
        target = part(peers.at(0, j), 0)
        add_rows(target, [via_a[k]], rows // 2)
        done_a.append(wire.copy(target, sum_a[k], peers.minor(j)))
    for copy in first_b:
        copy.wait_recv()
    target = part(major, 1)
    add_rows(target, via_b, rows // 2)
    done_b = wire.copy(target, sum_b, peers.major())
    if meanwhile is not None:
        meanwhile()
    for copy in (plain_a, *plain_b, *done_a, done_b):
        copy.wait_recv()
    return (
        (part(me, 0), direct_a, *sum_a),
        (part(me, 1), sum_b, *direct_b),
    )


def slots_for(n, rows, width):
    return pltpu.VMEM((wire_count(n), rows // 2, width), BF16)


def lane_of(rows, width=LANES):
    return lax.broadcasted_iota(jnp.int32, (rows, width), 1)


def first_head(rows):
    return lane_of(rows) < HD


def swap_halves(values):
    first = lax.rem(lane_of(values.shape[0]), np.int32(HD)) < HD // 2
    return jnp.where(first, pltpu.roll(values, LANES - HD // 2, 1), pltpu.roll(values, HD // 2, 1))


def doubled(pair, heads):
    if heads == 1:
        return [jnp.concatenate([pair, pair], axis=1)]
    out = []
    for k in range(heads // 2):
        both = pair[:, k * LANES : (k + 1) * LANES]
        swapped = pltpu.roll(both, HD, 1)
        first = first_head(both.shape[0])
        out += [jnp.where(first, both, swapped), jnp.where(first, swapped, both)]
    return out


def project_kernel(
    tokens, gain, cos_table, sin_table, w_query, w_key, w_value,
    gathered_out, query_out, key_out, value_out,
    gathered, weights, raw_key, raw_value, send_sem, recv_sem, local_sem,
):
    peers = Peers()
    rows, depth = tokens.shape
    q_width, kv_heads = w_query.shape[1], w_key.shape[1] // HD
    kv_width = kv_heads * LANES
    local = Local(local_sem)
    loads = [
        local.copy(w_key, raw_key),
        local.copy(w_value, raw_value),
        local.copy(w_query, weights.at[:, pl.ds(0, q_width)]),
    ]
    greet(peers)
    me = peers.at(0, 0)
    gain_row = gain[...]

    def normalize(k, carry):
        values = tokens[pl.ds(pl.multiple_of(k * 16, 16), 16), :].astype(F32)
        scale = lax.rsqrt(jnp.mean(values * values, axis=-1, keepdims=True) + EPSILON)
        gathered[pl.ds(pl.multiple_of(me * rows + k * 16, 16), 16), :] = (
            values * scale * gain_row
        ).astype(BF16)
        return carry

    lax.fori_loop(0, rows // 16, normalize, 0)
    started = [False]
    saves = []

    def prepare():
        for load in loads:
            load.wait()

        def some(k, carry):
            at = pl.ds(pl.multiple_of(k * 128, 128), 128)
            for raw, base in ((raw_key, q_width), (raw_value, q_width + kv_width)):
                for j, twice in enumerate(doubled(raw[at, :].astype(F32), kv_heads)):
                    weights[at, base + j * LANES : base + (j + 1) * LANES] = twice.astype(BF16)
            return carry

        lax.fori_loop(0, depth // 128, some, 0)

    def use(index):
        if not started[0]:
            started[0] = True
            prepare()
        at = pl.ds(pl.multiple_of(index * rows, rows), rows)
        saves.append(local.copy(gathered.at[at], gathered_out.at[at]))
        cos, sin = cos_table[at, :], sin_table[at, :]
        normed = gathered[at, :]
        for base, width, out, turn in (
            (0, q_width, query_out, True),
            (q_width, kv_width, key_out, True),
            (q_width + kv_width, kv_width, value_out, False),
        ):
            raw = dot_nn(normed, weights[:, base : base + width])
            for c in range(0, width, LANES):
                piece = raw[:, c : c + LANES]
                if turn:
                    piece = piece * cos + swap_halves(piece) * sin
                out[at, c : c + LANES] = piece.astype(BF16)

    wire = Wire(send_sem, recv_sem)
    gather(peers, wire, gathered, rows, use)
    wire.wait_sends()
    for save in saves:
        save.wait()


def any_spec():
    return pl.BlockSpec(memory_space=pl.ANY)


def vmem_spec():
    return pl.BlockSpec(memory_space=pltpu.VMEM)


def params(collective_id):
    return pltpu.CompilerParams(
        collective_id=collective_id, has_side_effects=True, vmem_limit_bytes=VMEM_LIMIT
    )


def project(tokens, gain, cos_table, sin_table, w_query, w_key, w_value):
    n = lax.axis_size("tensor")
    rows, depth = tokens.shape
    group = rows * n
    q_width, kv_raw = w_query.shape[1], w_key.shape[1]
    kv_width = kv_raw // HD * LANES
    return pl.pallas_call(
        project_kernel,
        out_shape=(
            jax.ShapeDtypeStruct((group, depth), BF16),
            jax.ShapeDtypeStruct((group, q_width), BF16),
            jax.ShapeDtypeStruct((group, kv_width), BF16),
            jax.ShapeDtypeStruct((group, kv_width), BF16),
        ),
        in_specs=[vmem_spec()] * 4 + [any_spec()] * 3,
        out_specs=(any_spec(), vmem_spec(), vmem_spec(), vmem_spec()),
        scratch_shapes=[
            pltpu.VMEM((group, depth), BF16),
            pltpu.VMEM((depth, q_width + 2 * kv_width), BF16),
            pltpu.VMEM((depth, kv_raw), BF16),
            pltpu.VMEM((depth, kv_raw), BF16),
            *wires(n),
            pltpu.SemaphoreType.DMA((3 + n,)),
        ],
        cost_estimate=pl.CostEstimate(
            flops=2 * group * depth * (q_width + 2 * kv_width),
            bytes_accessed=40 * 2**20,
            transcendentals=0,
        ),
        compiler_params=params(1),
    )(tokens, gain, cos_table, sin_table, w_query, w_key, w_value)


def attend_kernel(
    query, key, value, start, tokens, gain, w_out, cotangent,
    attended, log_total, state_out, normed_out, cot_a, cot_b,
    w_buf, part, slots, send_sem, recv_sem, cot_send, cot_recv, local_sem,
):
    peers = Peers()
    rows, depth = tokens.shape
    group, q_width = query.shape
    pairs_per_kv = q_width // LANES // (key.shape[1] // LANES)
    load = Local(local_sem).copy(w_out, w_buf)
    greet(peers)
    cot_wire = Wire(cot_send, cot_recv)
    for k, j in enumerate(peers.steps()):
        cot_wire.copy(half_block(cotangent, 0, rows, 0), cot_a.at[k], peers.minor(j))
    cot_wire.copy(half_block(cotangent, 0, rows, 1), cot_b, peers.major())

    tile = 256
    for i in range(group // tile):
        keys = (i + 1) * tile

        def one_pair(pair, carry, i=i, keys=keys):
            at = pl.ds(i * tile, tile)
            lanes = pl.ds(pl.multiple_of(pair * LANES, LANES), LANES)
            kv_lanes = pl.ds(
                pl.multiple_of(lax.div(pair, np.int32(pairs_per_kv)) * LANES, LANES), LANES
            )
            both = query[at, lanes]
            key_rows, value_rows = key[0:keys, kv_lanes], value[0:keys, kv_lanes]
            first = first_head(tile)
            column = lax.broadcasted_iota(jnp.int32, (tile, keys), 1)
            row = lax.broadcasted_iota(jnp.int32, (tile, keys), 0) + i * tile
            allowed = (column >= start[at, :]) & (column <= row)
            outs = []
            for h in range(2):
                own = first if h == 0 else jnp.logical_not(first)
                scores = dot_nt(jnp.where(own, both, jnp.zeros_like(both)), key_rows)
                scores = jnp.where(allowed, scores, MASKED)
                row_max = jnp.max(scores, axis=-1, keepdims=True)
                weights = jnp.exp2((scores - row_max) * SCALE2)
                row_sum = jnp.sum(weights, axis=-1, keepdims=True)
                outs.append(dot_nn(weights.astype(BF16), value_rows) / row_sum)
                log_total[pair * 2 + h, at, :] = row_max * SCALE2 + jnp.log2(row_sum)
            attended[at, lanes] = jnp.where(first, outs[0], outs[1]).astype(BF16)
            return carry

        lax.fori_loop(0, q_width // LANES, one_pair, 0)

    load.wait()

    def make(first, count):
        at = pl.ds(pl.multiple_of(first * rows, rows), count * rows)
        heads = attended[at, :]
        for c in range(0, depth, 1024):
            part[at, c : c + 1024] = dot_nn(heads, w_buf[:, c : c + 1024]).astype(BF16)

    wire = Wire(send_sem, recv_sem)
    sums = scatter(peers, wire, part, slots, rows, make)
    gain_row = gain[...]
    half = rows // 2
    for h in range(2):

        def finish(k, carry, h=h):
            inner = pl.ds(pl.multiple_of(k * 16, 16), 16)
            outer = pl.ds(pl.multiple_of(h * half + k * 16, 16), 16)
            mixed = sums[h][0][inner, :].astype(F32)
            for other in sums[h][1:]:
                mixed = mixed + other[inner, :].astype(F32)
            state = tokens[outer, :].astype(F32) + mixed
            scale = lax.rsqrt(jnp.mean(state * state, axis=-1, keepdims=True) + EPSILON)
            state_out[outer, :] = state
            normed_out[outer, :] = (state * scale * gain_row).astype(BF16)
            return carry

        lax.fori_loop(0, half // 16, finish, 0)
    wire.wait_sends()
    for copy in cot_wire.copies:
        copy.wait()


def attend(query, key, value, start, tokens, gain, w_out, cotangent):
    n = lax.axis_size("tensor")
    rows, depth = tokens.shape
    group, q_width = query.shape
    m = n // 2
    return pl.pallas_call(
        attend_kernel,
        out_shape=(
            jax.ShapeDtypeStruct((group, q_width), BF16),
            jax.ShapeDtypeStruct((q_width // HD, group, 1), F32),
            jax.ShapeDtypeStruct((rows, depth), F32),
            jax.ShapeDtypeStruct((rows, depth), BF16),
            jax.ShapeDtypeStruct((m - 1, rows // 2, depth), BF16),
            jax.ShapeDtypeStruct((rows // 2, depth), BF16),
        ),
        in_specs=[vmem_spec()] * 6 + [any_spec()] * 2,
        out_specs=(vmem_spec(), vmem_spec(), vmem_spec(), vmem_spec(), any_spec(), any_spec()),
        scratch_shapes=[
            pltpu.VMEM(w_out.shape, BF16),
            pltpu.VMEM((group, depth), BF16),
            slots_for(n, rows, depth),
            *wires(n),
            pltpu.SemaphoreType.DMA((m,)),
            pltpu.SemaphoreType.DMA((m,)),
            pltpu.SemaphoreType.DMA((1,)),
        ],
        cost_estimate=pl.CostEstimate(
            flops=2 * group * depth * q_width * 4, bytes_accessed=40 * 2**20, transcendentals=0
        ),
        compiler_params=params(2),
    )(query, key, value, start, tokens, gain, w_out, cotangent)


class Exchange:
    def __init__(self, wire, stage, received):
        self.wire, self.stage, self.received, self.sent = wire, stage, received, []

    def run(self, jobs):
        mine = core_of()
        copies = []
        for k in range(len(jobs) + 1):
            if k < len(jobs):
                tile, save, pair = jobs[k]
                slot = self.stage.at[k % 2]
                if k >= 2:
                    copies[k - 2].wait_send()
                tile(2 * pair + 1 - mine, slot, False)
                copies.append(self.wire.copy(slot, self.received.at[k], other_core()))
            if k >= 1:
                tile, save, pair = jobs[k - 1]
                copies[k - 1].wait_recv()
                tile(2 * pair + mine, self.received.at[k - 1], True)
                save(pair, self.received.at[k - 1])
        for copy in copies[-2:]:
            copy.wait_send()


def put(target, at, value, add):
    if add:
        value = value + target[at].astype(F32)
    target[at] = value.astype(BF16)


def hidden_kernel(
    normed, cotangent, cot_a, cot_b, w_gate, w_up,
    gathered_out, hidden_out, slope_gate_out, slope_up_out, cot_out, grad_down_out,
    gathered, gate_buf, up_buf, hidden, slope_gate, slope_up, cot, stage, received,
    send_sem, recv_sem, cot_send, cot_recv, core_send, core_recv, local_sem,
):
    peers = Peers()
    rows, depth = normed.shape
    units = w_gate.shape[1]
    me, major = peers.at(0, 0), peers.at(1, 0)
    local = Local(local_sem)
    first_load = local.copy(normed, block(gathered, me, rows))
    loads = [local.copy(w_gate, gate_buf), local.copy(w_up, up_buf)]
    cot_loads = [local.copy(cotangent, block(cot, me, rows))]
    for k, j in enumerate(peers.steps()):
        cot_loads.append(local.copy(cot_a.at[k], half_block(cot, peers.at(0, -j), rows, 0)))
    cot_loads.append(local.copy(cot_b, half_block(cot, major, rows, 1)))
    greet(peers, core=True)
    first_load.wait()
    saves, waiting = [], list(loads)

    def use(index):
        while waiting:
            waiting.pop().wait()
        at = pl.ds(pl.multiple_of(index * rows, rows), rows)
        saves.append(local.copy(gathered.at[at], gathered_out.at[at]))
        tile = 512

        def some(k, carry):
            lanes = pl.ds(pl.multiple_of(k * tile, tile), tile)
            x = gathered[at, :]
            gate = dot_nn(x, gate_buf[:, lanes])
            up = dot_nn(x, up_buf[:, lanes])
            sigmoid = jax.nn.sigmoid(gate)
            silu = gate * sigmoid
            hidden[at, lanes] = (silu * up).astype(BF16)
            slope_up[at, lanes] = silu.astype(BF16)
            slope_gate[at, lanes] = (up * sigmoid * (1.0 + gate * (1.0 - sigmoid))).astype(BF16)
            return carry

        lax.fori_loop(0, units // tile, some, 0)
        for source, target in (
            (hidden, hidden_out), (slope_gate, slope_gate_out), (slope_up, slope_up_out)
        ):
            saves.append(local.copy(source.at[at], target.at[at]))

    cot_wire = Wire(cot_send, cot_recv)
    cot_copies = []

    def send_rest():
        for load in cot_loads:
            load.wait()
        send = lambda index, half, device: cot_copies.append(
            cot_wire.copy(
                half_block(cot, index, rows, half), half_block(cot, index, rows, half), device
            )
        )
        for j in peers.steps():
            send(me, 1, peers.minor(j))
        send(me, 0, peers.major())
        for j in peers.steps():
            send(peers.at(0, -j), 0, peers.major())
            send(major, 1, peers.minor(j))

    wire = Wire(send_sem, recv_sem)
    gather(peers, wire, gathered, rows, use, send_rest)
    for copy in cot_copies:
        copy.wait_recv()
    saves.append(local.copy(cot, cot_out))
    columns = stage.shape[2]

    def tile(index, target, add):
        lanes = pl.ds(pl.multiple_of(index * columns, columns), columns)
        step = 512

        def some(k, carry):
            at = pl.ds(pl.multiple_of(k * step, step), step)
            put(target, (at, slice(None)), dot_tn(hidden[:, at], cot[:, lanes]), add)
            return carry

        lax.fori_loop(0, units // step, some, 0)

    def save(k, ref):
        saves.append(local.copy(ref, grad_down_out.at[pl.ds(k * units, units)]))

    pairs = received.shape[0]
    Exchange(Wire(core_send, core_recv), stage, received).run(
        [(tile, save, k) for k in range(pairs)]
    )
    wire.wait_sends()
    cot_wire.wait_sends()
    for copy in saves:
        copy.wait()


def hidden_units(normed, cotangent, cot_a, cot_b, w_gate, w_up):
    n = lax.axis_size("tensor")
    pairs = lax.axis_size("dp") // 2
    rows, depth = normed.shape
    group, units, columns = rows * n, w_gate.shape[1], depth // (2 * pairs)
    wide = lambda width: jax.ShapeDtypeStruct((group, width), BF16)
    return pl.pallas_call(
        hidden_kernel,
        out_shape=(
            wide(depth), wide(units), wide(units), wide(units), wide(depth),
            jax.ShapeDtypeStruct((pairs * units, columns), BF16),
        ),
        in_specs=[any_spec()] * 6,
        out_specs=(any_spec(),) * 6,
        scratch_shapes=[
            pltpu.VMEM((group, depth), BF16),
            pltpu.VMEM((depth, units), BF16),
            pltpu.VMEM((depth, units), BF16),
            pltpu.VMEM((group, units), BF16),
            pltpu.VMEM((group, units), BF16),
            pltpu.VMEM((group, units), BF16),
            pltpu.VMEM((group, depth), BF16),
            pltpu.VMEM((2, units, columns), BF16),
            pltpu.VMEM((pairs, units, columns), BF16),
            *wires(n),
            *wires(n),
            pltpu.SemaphoreType.DMA((pairs,)),
            pltpu.SemaphoreType.DMA((pairs,)),
            pltpu.SemaphoreType.DMA((4 * n + pairs + n + 8,)),
        ],
        cost_estimate=pl.CostEstimate(
            flops=6 * group * depth * units, bytes_accessed=60 * 2**20, transcendentals=0
        ),
        compiler_params=params(3),
    )(normed, cotangent, cot_a, cot_b, w_gate, w_up)


def norm_back(values, gain_row, grad_normed):
    scale = lax.rsqrt(jnp.mean(values * values, axis=-1, keepdims=True) + EPSILON)
    unit = values * scale
    scaled = grad_normed * gain_row
    grad = scale * (scaled - unit * jnp.mean(scaled * unit, axis=-1, keepdims=True))
    return grad, grad_normed * unit


def fold_rows(values):
    return values[:8] + values[8:]


def hidden_back_kernel(
    slope_gate, slope_up, cot_all, gathered_in, state, cotangent, gain, w_down, w_gate, w_up,
    grad_state_out, grad_mixed_out, gain_out, grad_gate_up_out,
    gate_buf, up_buf, down_buf, grad_gate, grad_up, cot, part, slots, stage, received,
    send_sem, recv_sem, core_send, core_recv, local_sem,
):
    peers = Peers()
    rows, depth = state.shape
    group, units = slope_gate.shape
    chunk = down_buf.shape[1]
    chunks = units // chunk
    local = Local(local_sem)
    load_cot = local.copy(cot_all, cot)
    down_chunk = lambda c: local.copy(w_down.at[pl.ds(c * chunk, chunk)], down_buf.at[c % 2])
    down_loads = [down_chunk(0), down_chunk(1)]
    load_slopes = [local.copy(slope_gate, grad_gate), local.copy(slope_up, grad_up)]
    loads = [local.copy(w_gate, gate_buf), local.copy(w_up, up_buf)]
    load_state = local.copy(state, grad_state_out)
    greet(peers, core=True)
    load_cot.wait()
    for c in range(chunks):
        down_loads[c].wait()
        if c == 0:
            for load in load_slopes:
                load.wait()
        lanes = slice(c * chunk, (c + 1) * chunk)
        grad_hidden = dot_nt(cot[...], down_buf[c % 2])
        grad_gate[:, lanes] = (grad_hidden * grad_gate[:, lanes].astype(F32)).astype(BF16)
        grad_up[:, lanes] = (grad_hidden * grad_up[:, lanes].astype(F32)).astype(BF16)
        if c + 2 < chunks:
            down_loads.append(down_chunk(c + 2))
    load_gathered = local.copy(gathered_in, cot)
    for load in loads:
        load.wait()

    def make(first, count):
        at = pl.ds(pl.multiple_of(first * rows, rows), count * rows)
        step = 512

        def some(k, carry):
            inner = pl.ds(pl.multiple_of(k * step, step), step)
            total = dot_nt(grad_gate[at, :], gate_buf[inner, :])
            total = total + dot_nt(grad_up[at, :], up_buf[inner, :])
            part[at, inner] = total.astype(BF16)
            return carry

        lax.fori_loop(0, depth // step, some, 0)

    deep = stage.shape[1]
    saves = []

    def tile_of(grad):
        def tile(index, target, add):
            lanes = pl.ds(pl.multiple_of(index * deep, deep), deep)
            step = min(1024, units)

            def some(k, carry):
                inner = pl.ds(pl.multiple_of(k * step, step), step)
                put(target, (slice(None), inner), dot_tn(cot[:, lanes], grad[:, inner]), add)
                return carry

            lax.fori_loop(0, units // step, some, 0)

        return tile

    def save_at(base):
        def save(k, ref):
            target = grad_gate_up_out.at[pl.ds(k * deep, deep), pl.ds(base, units)]
            saves.append(local.copy(ref, target))

        return save

    def weight_grads():
        load_gathered.wait()
        pairs = received.shape[0] // 2
        Exchange(Wire(core_send, core_recv), stage, received).run(
            [(tile_of(grad_gate), save_at(0), k) for k in range(pairs)]
            + [(tile_of(grad_up), save_at(units), k) for k in range(pairs)]
        )

    wire = Wire(send_sem, recv_sem)
    sums = scatter(peers, wire, part, slots, rows, make, weight_grads)
    load_state.wait()
    gain_row = gain[...]
    half = rows // 2
    gain_out[...] = jnp.zeros_like(gain_out)
    for h in range(2):

        def finish(k, carry, h=h):
            inner = pl.ds(pl.multiple_of(k * 16, 16), 16)
            outer = pl.ds(pl.multiple_of(h * half + k * 16, 16), 16)
            grad_normed = sums[h][0][inner, :].astype(F32)
            for other in sums[h][1:]:
                grad_normed = grad_normed + other[inner, :].astype(F32)
            grad, gain_part = norm_back(grad_state_out[outer, :], gain_row, grad_normed)
            grad = grad + cotangent[outer, :].astype(F32)
            gain_out[...] += fold_rows(gain_part)
            grad_state_out[outer, :] = grad
            grad_mixed_out[outer, :] = grad.astype(BF16)
            return carry

        lax.fori_loop(0, half // 16, finish, 0)
    wire.wait_sends()
    for copy in saves:
        copy.wait()


def hidden_back(
    slope_gate, slope_up, cot_all, gathered, state, cotangent, gain, w_down, w_gate, w_up
):
    n = lax.axis_size("tensor")
    pairs = lax.axis_size("dp") // 2
    rows, depth = state.shape
    group, units = slope_gate.shape
    deep = depth // (2 * pairs)
    chunk = 512
    return pl.pallas_call(
        hidden_back_kernel,
        out_shape=(
            jax.ShapeDtypeStruct((rows, depth), F32),
            jax.ShapeDtypeStruct((rows, depth), BF16),
            jax.ShapeDtypeStruct((8, depth), F32),
            jax.ShapeDtypeStruct((pairs * deep, 2 * units), BF16),
        ),
        in_specs=[any_spec()] * 5 + [vmem_spec()] * 2 + [any_spec()] * 3,
        out_specs=(vmem_spec(), vmem_spec(), vmem_spec(), any_spec()),
        scratch_shapes=[
            pltpu.VMEM((depth, units), BF16),
            pltpu.VMEM((depth, units), BF16),
            pltpu.VMEM((2, chunk, depth), BF16),
            pltpu.VMEM((group, units), BF16),
            pltpu.VMEM((group, units), BF16),
            pltpu.VMEM((group, depth), BF16),
            pltpu.VMEM((group, depth), BF16),
            slots_for(n, rows, depth),
            pltpu.VMEM((2, deep, units), BF16),
            pltpu.VMEM((2 * pairs, deep, units), BF16),
            *wires(n),
            pltpu.SemaphoreType.DMA((2 * pairs,)),
            pltpu.SemaphoreType.DMA((2 * pairs,)),
            pltpu.SemaphoreType.DMA((8 + units // chunk + 2 * pairs,)),
        ],
        cost_estimate=pl.CostEstimate(
            flops=10 * group * depth * units, bytes_accessed=80 * 2**20, transcendentals=0
        ),
        compiler_params=params(4),
    )(slope_gate, slope_up, cot_all, gathered, state, cotangent, gain, w_down, w_gate, w_up)


def attend_back_kernel(
    grad_mixed, query, key, value, attended, log_total, start, cos_table, sin_table,
    tokens, gain, grad_state, gathered_in, w_out, w_query, w_key, w_value,
    grad_tokens_out, gain_out, grad_out_out, grad_qkv_out,
    mixed, out_buf, query_buf, key_buf, value_buf, gathered, grad_att, key_acc, value_acc, grads, part, slots,
    stage_out, got_out, stage_qkv, got_qkv,
    send_sem, recv_sem, sums_send, sums_recv, out_send, out_recv, qkv_send, qkv_recv, local_sem,
):
    peers = Peers()
    rows, depth = tokens.shape
    group, q_width = query.shape
    kv_heads = w_key.shape[1] // HD
    kv_raw = kv_heads * HD
    pairs_per_kv = q_width // LANES // kv_heads
    me = peers.at(0, 0)
    local = Local(local_sem)
    first_load = local.copy(grad_mixed, block(mixed, me, rows))
    load_out = local.copy(w_out, out_buf)
    loads = [
        local.copy(w_query, query_buf),
        local.copy(w_key, key_buf),
        local.copy(w_value, value_buf),
        local.copy(gathered_in, gathered),
    ]
    greet(peers, core=True)
    first_load.wait()
    waiting, saves = [load_out], []

    def use(index):
        while waiting:
            waiting.pop().wait()
        at = pl.ds(pl.multiple_of(index * rows, rows), rows)
        grad_att[at, :] = dot_nt(mixed[at, :], out_buf[...]).astype(BF16)

    gather_wire = Wire(send_sem, recv_sem)
    gather(peers, gather_wire, mixed, rows, use)

    columns = stage_out.shape[2]

    def out_tile(index, target, add):
        lanes = pl.ds(pl.multiple_of(index * columns, columns), columns)
        put(target, (slice(None), slice(None)), dot_tn(attended[...], mixed[:, lanes]), add)

    def out_save(k, ref):
        saves.append(local.copy(ref, grad_out_out.at[pl.ds(k * q_width, q_width)]))

    pairs = got_out.shape[0]
    Exchange(Wire(out_send, out_recv), stage_out, got_out).run(
        [(out_tile, out_save, k) for k in range(pairs)]
    )

    key_acc[...] = jnp.zeros_like(key_acc)
    value_acc[...] = jnp.zeros_like(value_acc)
    tile = 256
    for i in range(group // tile):
        keys = (i + 1) * tile

        def one_pair(pair, carry, i=i, keys=keys):
            at = pl.ds(i * tile, tile)
            lanes = pl.ds(pl.multiple_of(pair * LANES, LANES), LANES)
            kv_lanes = pl.ds(
                pl.multiple_of(lax.div(pair, np.int32(pairs_per_kv)) * LANES, LANES), LANES
            )
            both, grad_both = query[at, lanes], grad_att[at, lanes]
            key_rows, value_rows = key[0:keys, kv_lanes], value[0:keys, kv_lanes]
            first = first_head(tile)
            dots = grad_both.astype(F32) * attended[at, lanes].astype(F32)
            column = lax.broadcasted_iota(jnp.int32, (tile, keys), 1)
            row = lax.broadcasted_iota(jnp.int32, (tile, keys), 0) + i * tile
            allowed = (column >= start[at, :]) & (column <= row)
            grad_queries, grad_keys, grad_values = [], 0.0, 0.0
            for h in range(2):
                own = first if h == 0 else jnp.logical_not(first)
                own_query = jnp.where(own, both, jnp.zeros_like(both))
                own_grad = jnp.where(own, grad_both, jnp.zeros_like(grad_both))
                row_dot = jnp.sum(jnp.where(own, dots, 0.0), axis=-1, keepdims=True)
                scores = dot_nt(own_query, key_rows)
                probs = jnp.exp2(scores * SCALE2 - log_total[pair * 2 + h, at, :])
                probs = jnp.where(allowed, probs, 0.0)
                grad_probs = dot_nt(own_grad, value_rows)
                grad_scores = (probs * (grad_probs - row_dot)).astype(BF16)
                grad_queries.append(dot_nn(grad_scores, key_rows))
                grad_keys = grad_keys + dot_tn(grad_scores, own_query)
                grad_values = grad_values + dot_tn(probs.astype(BF16), own_grad)
            key_acc[0:keys, kv_lanes] += grad_keys
            value_acc[0:keys, kv_lanes] += grad_values
            turned = jnp.where(first, grad_queries[0], grad_queries[1]) * 0.125
            turned = turned * cos_table[at, :] - swap_halves(turned) * sin_table[at, :]
            grads[at, lanes] = turned.astype(BF16)
            return carry

        lax.fori_loop(0, q_width // LANES, one_pair, 0)

    def fold(k, carry):
        at = pl.ds(pl.multiple_of(k * 128, 128), 128)
        cos, sin = cos_table[at, :], sin_table[at, :]
        key_heads, value_heads = [], []
        for j in range(kv_heads):
            lanes = slice(j * LANES, (j + 1) * LANES)
            both = key_acc[at, lanes] * 0.125
            both = both + pltpu.roll(both, HD, 1)
            key_heads.append(both * cos - swap_halves(both) * sin)
            both = value_acc[at, lanes]
            value_heads.append(both + pltpu.roll(both, HD, 1))
        for heads, base in ((key_heads, q_width), (value_heads, q_width + kv_raw)):
            if kv_heads == 1:
                grads[at, base : base + HD] = heads[0][:, :HD].astype(BF16)
            for j in range(0, kv_heads - 1, 2):
                pair = jnp.where(first_head(128), heads[j], heads[j + 1])
                grads[at, base + j * HD : base + (j + 2) * HD] = pair.astype(BF16)
        return carry

    lax.fori_loop(0, group // 128, fold, 0)
    for load in loads:
        load.wait()

    def make(first, count):
        at = pl.ds(pl.multiple_of(first * rows, rows), count * rows)
        step = 1024
        for c in range(0, depth, step):
            inner = slice(c, c + step)
            total = dot_nt(grads[at, 0:q_width], query_buf[inner, :])
            total = total + dot_nt(grads[at, q_width : q_width + kv_raw], key_buf[inner, :])
            total = total + dot_nt(grads[at, q_width + kv_raw :], value_buf[inner, :])
            part[at, inner] = total.astype(BF16)

    deep = stage_qkv.shape[1]

    def qkv_tile(index, target, add):
        lanes = pl.ds(pl.multiple_of(index * deep, deep), deep)
        put(target, (slice(None), slice(None)), dot_tn(gathered[:, lanes], grads[...]), add)

    def qkv_save(k, ref):
        saves.append(local.copy(ref, grad_qkv_out.at[pl.ds(k * deep, deep)]))

    def weight_grads():
        Exchange(Wire(qkv_send, qkv_recv), stage_qkv, got_qkv).run(
            [(qkv_tile, qkv_save, k) for k in range(pairs)]
        )

    wire = Wire(sums_send, sums_recv)
    sums = scatter(peers, wire, part, slots, rows, make, weight_grads)
    gain_row = gain[...]
    half = rows // 2
    gain_out[...] = jnp.zeros_like(gain_out)
    for h in range(2):

        def finish(k, carry, h=h):
            inner = pl.ds(pl.multiple_of(k * 16, 16), 16)
            outer = pl.ds(pl.multiple_of(h * half + k * 16, 16), 16)
            grad_normed = sums[h][0][inner, :].astype(F32)
            for other in sums[h][1:]:
                grad_normed = grad_normed + other[inner, :].astype(F32)
            grad, gain_part = norm_back(tokens[outer, :].astype(F32), gain_row, grad_normed)
            gain_out[...] += fold_rows(gain_part)
            grad_tokens_out[outer, :] = (grad + grad_state[outer, :]).astype(BF16)
            return carry

        lax.fori_loop(0, half // 16, finish, 0)
    gather_wire.wait_sends()
    wire.wait_sends()
    for copy in saves:
        copy.wait()


def attend_back(
    grad_mixed, query, key, value, attended, log_total, start, cos_table, sin_table,
    tokens, gain, grad_state, gathered, w_out, w_query, w_key, w_value,
):
    n = lax.axis_size("tensor")
    pairs = lax.axis_size("dp") // 2
    rows, depth = tokens.shape
    group, q_width = query.shape
    kv_width, kv_raw = key.shape[1], w_key.shape[1]
    width = q_width + 2 * kv_raw
    deep = depth // (2 * pairs)
    dma = lambda count: pltpu.SemaphoreType.DMA((count,))
    return pl.pallas_call(
        attend_back_kernel,
        out_shape=(
            jax.ShapeDtypeStruct((rows, depth), BF16),
            jax.ShapeDtypeStruct((8, depth), F32),
            jax.ShapeDtypeStruct((pairs * q_width, deep), BF16),
            jax.ShapeDtypeStruct((pairs * deep, width), BF16),
        ),
        in_specs=[any_spec()] + [vmem_spec()] * 11 + [any_spec()] * 5,
        out_specs=(vmem_spec(), vmem_spec(), any_spec(), any_spec()),
        scratch_shapes=[
            pltpu.VMEM((group, depth), BF16),
            pltpu.VMEM(w_out.shape, BF16),
            pltpu.VMEM(w_query.shape, BF16),
            pltpu.VMEM(w_key.shape, BF16),
            pltpu.VMEM(w_value.shape, BF16),
            pltpu.VMEM((group, depth), BF16),
            pltpu.VMEM((group, q_width), BF16),
            pltpu.VMEM((group, kv_width), F32),
            pltpu.VMEM((group, kv_width), F32),
            pltpu.VMEM((group, width), BF16),
            pltpu.VMEM((group, depth), BF16),
            slots_for(n, rows, depth),
            pltpu.VMEM((2, q_width, deep), BF16),
            pltpu.VMEM((pairs, q_width, deep), BF16),
            pltpu.VMEM((2, deep, width), BF16),
            pltpu.VMEM((pairs, deep, width), BF16),
            *wires(n),
            *wires(n),
            dma(pairs), dma(pairs), dma(pairs), dma(pairs), dma(6 + 2 * pairs),
        ],
        cost_estimate=pl.CostEstimate(
            flops=2 * group * depth * q_width * 12, bytes_accessed=60 * 2**20, transcendentals=0
        ),
        compiler_params=params(5),
    )(grad_mixed, query, key, value, attended, log_total, start, cos_table, sin_table,
      tokens, gain, grad_state, gathered, w_out, w_query, w_key, w_value)


class GainSums:
    def __init__(self, gains, tiles, from_tensor, from_dp, wire, chunk):
        self.gains, self.tiles, self.from_tensor, self.from_dp = gains, tiles, from_tensor, from_dp
        self.wire, self.n, self.dps = wire, lax.axis_size("tensor"), lax.axis_size("dp")
        self.chunk = chunk
        self.me, self.dp = lax.axis_index("tensor"), lax.axis_index("dp")

    def tensor(self, step):
        return lax.rem(self.me + np.int32(step), np.int32(self.n))

    def data(self, step):
        return lax.rem(self.dp + np.int32(step), np.int32(self.dps))

    def greet(self):
        barrier = pltpu.get_barrier_semaphore()
        for step in range(1, self.n):
            device = {"tensor": self.tensor(step)}
            pl.semaphore_signal(barrier, inc=1, device_id=device, device_id_type=MESH)
        for step in range(1, self.dps):
            device = {"dp": self.data(step)}
            pl.semaphore_signal(barrier, inc=1, device_id=device, device_id_type=MESH)
        pl.semaphore_wait(barrier, self.n + self.dps - 2)

    def start(self):
        for t in range(self.n):
            for d in range(self.dps):
                lane = (d * self.n + t) * self.chunk // LANES * LANES
                for k, gain in enumerate(self.gains):
                    self.tiles[t, d, k] = gain[:, lane : lane + LANES]
        self.first = [
            self.wire.copy(
                self.tiles.at[self.tensor(step)],
                self.from_tensor.at[step - 1],
                {"tensor": self.tensor(step)},
            )
            for step in range(1, self.n)
        ]

    def forward(self):
        for copy in self.first:
            copy.wait_recv()
        total = self.tiles[self.me]
        for step in range(1, self.n):
            total = total + self.from_tensor[step - 1]
        self.from_tensor[0] = total
        self.second = [
            self.wire.copy(
                self.from_tensor.at[0, self.data(step)],
                self.from_dp.at[step - 1],
                {"dp": self.data(step)},
            )
            for step in range(1, self.dps)
        ]

    def finish(self, out):
        for copy in self.second:
            copy.wait_recv()
        total = self.from_tensor[0, self.dp]
        for step in range(1, self.dps):
            total = total + self.from_dp[step - 1]
        out[...] = total


def output_kernel(
    hidden_in, w_down, state, gain_one, gain_two,
    output, gains_out,
    hidden, down_buf, part, slots, tiles, from_tensor, from_dp,
    send_sem, recv_sem, gain_send, gain_recv, local_sem,
):
    peers = Peers()
    rows, depth = state.shape
    local = Local(local_sem)
    loads = [local.copy(hidden_in, hidden), local.copy(w_down, down_buf)]
    chunk = depth // (lax.axis_size("tensor") * lax.axis_size("dp"))
    gains = GainSums(
        (gain_one, gain_two), tiles, from_tensor, from_dp, Wire(gain_send, gain_recv), chunk
    )
    gains.greet()
    gains.start()
    for load in loads:
        load.wait()

    def make(first, count):
        at = pl.ds(pl.multiple_of(first * rows, rows), count * rows)
        step = 512

        def some(k, carry):
            lanes = pl.ds(pl.multiple_of(k * step, step), step)
            part[at, lanes] = dot_nn(hidden[at, :], down_buf[:, lanes]).astype(BF16)
            return carry

        lax.fori_loop(0, depth // step, some, 0)

    wire = Wire(send_sem, recv_sem)
    sums = scatter(peers, wire, part, slots, rows, make, gains.forward)
    half = rows // 2
    for h in range(2):

        def finish(k, carry, h=h):
            inner = pl.ds(pl.multiple_of(k * 16, 16), 16)
            outer = pl.ds(pl.multiple_of(h * half + k * 16, 16), 16)
            total = sums[h][0][inner, :].astype(F32)
            for other in sums[h][1:]:
                total = total + other[inner, :].astype(F32)
            output[outer, :] = (state[outer, :] + total).astype(BF16)
            return carry

        lax.fori_loop(0, half // 16, finish, 0)
    gains.finish(gains_out)
    wire.wait_sends()
    gains.wire.wait_sends()


def layer_output(hidden, w_down, state, gain_one, gain_two):
    n, dps = lax.axis_size("tensor"), lax.axis_size("dp")
    rows, depth = state.shape
    dma = lambda count: pltpu.SemaphoreType.DMA((count,))
    return pl.pallas_call(
        output_kernel,
        out_shape=(
            jax.ShapeDtypeStruct((rows, depth), BF16),
            jax.ShapeDtypeStruct((2, 8, LANES), F32),
        ),
        in_specs=[any_spec(), any_spec(), vmem_spec(), vmem_spec(), vmem_spec()],
        out_specs=(vmem_spec(), vmem_spec()),
        scratch_shapes=[
            pltpu.VMEM(hidden.shape, BF16),
            pltpu.VMEM(w_down.shape, BF16),
            pltpu.VMEM((hidden.shape[0], depth), BF16),
            slots_for(n, rows, depth),
            pltpu.VMEM((n, dps, 2, 8, LANES), F32),
            pltpu.VMEM((n - 1, dps, 2, 8, LANES), F32),
            pltpu.VMEM((dps - 1, 2, 8, LANES), F32),
            *wires(n),
            dma(n + dps - 2), dma(n + dps - 2), dma(2),
        ],
        cost_estimate=pl.CostEstimate(
            flops=2 * hidden.shape[0] * depth * hidden.shape[1],
            bytes_accessed=20 * 2**20,
            transcendentals=0,
        ),
        compiler_params=params(6),
    )(hidden, w_down, state, gain_one, gain_two)


def sum_over_chips(grads):
    size = lax.axis_size("dp")
    groups = [list(range(core, size, 2)) for core in range(2)]
    return lax.psum_scatter(
        grads, "dp", scatter_dimension=0, tiled=True, axis_index_groups=groups
    ).astype(F32)


def local(
    tokens, lengths, gain_one, w_query, w_key, w_value, w_out, gain_two, w_gate, w_up, w_down,
    cotangent,
):
    depth, group = tokens.shape[1], tokens.shape[0] * lax.axis_size("tensor")
    q_width, kv_raw, units = w_query.shape[1], w_key.shape[1], w_gate.shape[1]
    start, position = layout(lengths[0], group)
    start = start[:, None]
    cos_table, sin_table = rope_table(position)
    gain_one, gain_two = gain_one[None], gain_two[None]
    gathered_one, query, key, value = project(
        tokens, gain_one, cos_table, sin_table, w_query, w_key, w_value
    )
    attended, log_total, state, normed_two, cot_a, cot_b = attend(
        query, key, value, start, tokens, gain_two, w_out, cotangent
    )
    gathered_two, hidden, slope_gate, slope_up, cot_all, grad_down = hidden_units(
        normed_two, cotangent, cot_a, cot_b, w_gate, w_up
    )
    grad_w_down = sum_over_chips(grad_down)
    grad_state, grad_mixed, gain_two_part, grad_gate_up = hidden_back(
        slope_gate, slope_up, cot_all, gathered_two, state, cotangent, gain_two,
        w_down, w_gate, w_up,
    )
    grad_gate_up, grad_w_down = lax.optimization_barrier((grad_gate_up, grad_w_down))
    grad_w_gate_up = sum_over_chips(grad_gate_up)
    grad_tokens, gain_one_part, grad_out, grad_qkv = attend_back(
        grad_mixed, query, key, value, attended, log_total, start, cos_table, sin_table,
        tokens, gain_one, grad_state, gathered_one, w_out, w_query, w_key, w_value,
    )
    grad_out, grad_w_gate_up = lax.optimization_barrier((grad_out, grad_w_gate_up))
    grad_w_out = sum_over_chips(grad_out)
    grad_qkv, grad_w_out = lax.optimization_barrier((grad_qkv, grad_w_out))
    grad_w_qkv = sum_over_chips(grad_qkv)
    output, gains = layer_output(hidden, w_down, state, gain_one_part, gain_two_part)
    share = depth // (lax.axis_size("tensor") * lax.axis_size("dp"))
    place = lax.rem(
        (lax.axis_index("dp") * lax.axis_size("tensor") + lax.axis_index("tensor")) * share, LANES
    )
    gains = lax.dynamic_slice_in_dim(jnp.sum(gains, axis=1), place, share, axis=1)
    return (
        output,
        grad_tokens,
        gains[0],
        grad_w_qkv[:, :q_width],
        grad_w_qkv[:, q_width : q_width + kv_raw],
        grad_w_qkv[:, q_width + kv_raw :],
        grad_w_out,
        gains[1],
        grad_w_gate_up[:, :units],
        grad_w_gate_up[:, units:],
        grad_w_down,
    )


def solution(mesh):
    return jax.shard_map(
        local,
        mesh=mesh,
        in_specs=(
            P(("dp", "tensor"), None),
            P("dp", None),
            P(),
            P(None, "tensor"),
            P(None, "tensor"),
            P(None, "tensor"),
            P("tensor", None),
            P(),
            P(None, "tensor"),
            P(None, "tensor"),
            P("tensor", None),
            P(("dp", "tensor"), None),
        ),
        out_specs=(
            P(("dp", "tensor"), None),
            P(("dp", "tensor"), None),
            P(("dp", "tensor")),
            P("dp", "tensor"),
            P("dp", "tensor"),
            P("dp", "tensor"),
            P("tensor", "dp"),
            P(("dp", "tensor")),
            P("dp", "tensor"),
            P("dp", "tensor"),
            P("tensor", "dp"),
        ),
        check_vma=False,
    )
```

time: 1270 us -> 530 us (0.42)
  waiting for transfers between devices: 835 us -> 59.4 us
  Pallas kernels: 0 us -> 424 us
  matrix products: 257 us -> 0 us
  other arithmetic: 80.6 us -> 15.2 us
  local copies, waits for them, and re-layouts: 69 us -> 12.2 us
    reduce_scatter x11 -> x4, waiting for transfers between devices: 518 us -> 59.3 us  [sum_over_chips(): lax.psum_scatter(grads, 'dp', scatter_dimension=0, tiled=True, axis_index...]
    pallas_call x0 -> x6, Pallas kernels: none -> 424 us  [the longest x1 116 us: attend_back(): pl.pallas_call(attend_back_kernel, out_shape=(jax.ShapeDtypeStruct((rows,...]
    dot_general x35 -> x0, matrix products: 257 us -> none  [the longest x7 60.8 us: contract_rows(): lax.dot_general(operand, weights, (((0,), (0,)), ((), ())), preferred_ele...]
    all_gather x4 -> x0, waiting for transfers between devices: 185 us -> none  [the longest x1 54.4 us: local(): gathered_one = lax.all_gather(normed_one, 'tensor', axis=0, tiled=True)]
    unnamed x17 -> x4, waiting for transfers between devices: 132 us -> 0.07 us
    convert_element_type x15 -> x4, other arithmetic: 53.3 us -> 9.17 us  [the longest x3 8.52 us: sum_over_chips(): return lax.psum_scatter(grads, 'dp', scatter_dimension=0, tiled=True, axi...]
    dynamic_update_slice x4 -> x0, local copies, waits for them, and re-layouts: 41.4 us -> none  [attend_back(): (key_grad, value_grad), query_grad = lax.scan(one_block, initial, stacked)]
    reduce_sum x8 -> x1, other arithmetic: 18 us -> 0.71 us  [local(): jnp.sum(gains, axis=1)]
  transfers between devices with their start and end apart: 16 -> 4, of which waited for: 14 -> 3; matrix products, arithmetic and copies ran while one was open for 11% -> 1% of each run, Pallas kernels for 0% -> 46%
where the time goes in v1:
time: 530 us; the launch traced here: 527 us
  Pallas kernels  424 us (80%)
  waiting for transfers between devices  59.4 us (11%)
  between operations  16.2 us (3%)
  other arithmetic  15.2 us (3%)
  local copies, waits for them, and re-layouts  12.2 us (2%)
    pallas_call x1, Pallas kernels, attend_back(): pl.pallas_call(attend_back_kernel, out_shape=(jax.ShapeDtypeStruct((rows,...  116 us
    pallas_call x1, Pallas kernels, hidden_units(): pl.pallas_call(hidden_kernel, out_shape=(wide(depth), wide(units), wide(u...  77.1 us
    pallas_call x1, Pallas kernels, hidden_back(): pl.pallas_call(hidden_back_kernel, out_shape=(jax.ShapeDtypeStruct((rows,...  75.3 us
    pallas_call x1, Pallas kernels, attend(): pl.pallas_call(attend_kernel, out_shape=(jax.ShapeDtypeStruct((group, q_w...  60.7 us
    reduce_scatter x4, waiting for transfers between devices, sum_over_chips(): lax.psum_scatter(grads, 'dp', scatter_dimension=0, tiled=True, axis_index...  59.3 us
    pallas_call x1, Pallas kernels, layer_output(): pl.pallas_call(output_kernel, out_shape=(jax.ShapeDtypeStruct((rows, dept...  49.2 us
    pallas_call x1, Pallas kernels, project(): pl.pallas_call(project_kernel, out_shape=(jax.ShapeDtypeStruct((group, de...  45.9 us
  transfers between devices with their start and end apart: 4, of which 3 were waited for; matrix products, arithmetic and copies ran while one was open for 1% of the time, Pallas kernels for 46%

profile of v1, /device:TPU:0, one launch (start us, length us, event | category | flops | bytes accessed | tf_op | source)
XLA Modules:
  0.0 527.1 jit_solution(17875520629172798020)
XLA Ops:
  7.2 1.4 fusion.3
  10.5 0.7 subtract_convert_fusion
  11.2 1.6 select_select_fusion.start
  12.8 1.9 fusion
  14.7 1.8 pad_maximum_fusion
  16.5 45.9 %shard_map.203 = (bf16[1024,2048]{1,0:T(8,128)(2,1)}, bf16[1024,512]{1,0:T(8,128)(2,1)}, bf16[1024,256]{1,0:T(8,128)(2,1)}, bf16[1024,256]{1,0:T(8,128)(2,1)}) custom-call(bf16[256,2048]{1,0:T(8,128)(2,1)} %tokens.5, f32[1,2048]{1,0:T(1,128)} %bitcast.11, f32[1024,128]{1,0:T(8,128)} %get-tuple-element.87.cos_table, f32[1024,128]{1,0:T(8,128)} %get-tuple-element.88.sin_table, ...), custom_call_target="tpu_custom_call" | custom-call | flops 4294967296 | bytes 41943040 | tf_op jit(solution)/shard_map/pallas_call | solution.py:359
  62.5 60.7 %shard_map.204 = (bf16[1024,512]{1,0:T(8,128)(2,1)}, f32[8,1024,1]{2,1,0:T(8,128)}, f32[256,2048]{1,0:T(8,128)}, bf16[256,2048]{1,0:T(8,128)(2,1)}, bf16[1,128,2...) custom-call(bf16[1024,512]{1,0:T(8,128)(2,1)} %get-tuple-element.43.query, bf16[1024,256]{1,0:T(8,128)(2,1)} %get-tuple-element.44.key, ...), custom_call_target="tpu_custom_call" | custom-call | flops 8589934592 | bytes 41943040 | tf_op jit(solution)/shard_map/pallas_call | solution.py:470
  123.2 77.1 %shard_map.205 = (bf16[1024,2048]{1,0:T(8,128)(2,1)}, bf16[1024,2048]{1,0:T(8,128)(2,1)}, bf16[1024,2048]{1,0:T(8,128)(2,1)}, bf16[1024,2048]{1,0:T(8,128)(2,1)}...) custom-call(bf16[256,2048]{1,0:T(8,128)(2,1)} %get-tuple-element.46.normed, bf16[256,2048]{1,0:T(8,128)(2,1)} %cotangent.5, ...), custom_call_target="tpu_custom_call" | custom-call | flops 25769803776 | bytes 62914560 | tf_op jit(solution)/shard_map/pallas_call | solution.py:629
  200.3 75.3 %shard_map.206 = (f32[256,2048]{1,0:T(8,128)}, bf16[256,2048]{1,0:T(8,128)(2,1)}, f32[8,2048]{1,0:T(8,128)}, bf16[1024,4096]{1,0:T(8,128)(2,1)}) custom-call(bf16[1024,2048]{1,0:T(8,128)(2,1)} %get-tuple-element.51.slope_gate, bf16[1024,2048]{1,0:T(8,128)(2,1)} %get-tuple-element.52.slope_up, bf16[1024,2048]{1,0:T(8,128)(2,1)} %get-tuple-element.53.cot_all, ...), custom_call_target="tpu_custom_call" | custom-call | flops 42949672960 | bytes 83886080 | tf_op jit(solution)/shard_map/pallas_call | solution.py:788
  275.7 1.9 reduce-scatter.5.cloned.1.call-done
  277.6 2.7 convert_element_type.20
  280.4 115.6 %shard_map.207 = (bf16[256,2048]{1,0:T(8,128)(2,1)}, f32[8,2048]{1,0:T(8,128)}, bf16[2048,256]{1,0:T(8,128)(2,1)}, bf16[1024,768]{1,0:T(8,128)(2,1)}) custom-call(bf16[256,2048]{1,0:T(8,128)(2,1)} %get-tuple-element.55.grad_mixed, bf16[1024,512]{1,0:T(8,128)(2,1)} %get-tuple-element.43.query, bf16[1024,256]{1,0:T(8,128)(2,1)} %get-tuple-element.44.key, ...), custom_call_target="tpu_custom_call" | custom-call | flops 25769803776 | bytes 62914560 | tf_op jit(solution)/shard_map/pallas_call | solution.py:998
  396.0 29.4 %reduce-scatter.7.cloned.1.call-done = bf16[256,4096]{1,0:T(8,128)(2,1)} async-done(((bf16[1024,4096]{1,0:T(8,128)(2,1)}), bf16[256,4096]{1,0:T(8,128)(2,1)}) %reduce-scatter.7.cloned.1.call-update) | async-done | bytes 2097168 | tf_op jit(solution)/shard_map/reduce_scatter | solution.py:1185
  425.5 4.0 convert_element_type.21
  429.6 28.0 %reduce-scatter.9.cloned.1.call-done = bf16[512,256]{1,0:T(8,128)(2,1)} async-done(((bf16[2048,256]{1,0:T(8,128)(2,1)}), bf16[512,256]{1,0:T(8,128)(2,1)}) %reduce-scatter.9.cloned.1.call-update) | async-done | bytes 262160 | tf_op jit(solution)/shard_map/reduce_scatter | solution.py:1185
  457.6 1.8 convert_element_type.22
  459.4 49.2 %shard_map.208 = (bf16[256,2048]{1,0:T(8,128)(2,1)}, f32[2,8,128]{2,1,0:T(8,128)}) custom-call(bf16[1024,2048]{1,0:T(8,128)(2,1)} %get-tuple-element.49.hidden_in, bf16[2048,2048]{1,0:T(8,128)(2,1)} %w_down.3, f32[256,2048]{1,0:T(8,128)} %get-tuple-element.50.state, f32[8,2048]{1,0:T(8,128)} %get-tuple-element.60.gain_one, f32[8,2048]{1,0:T(8,128)} %get-tuple-element.61.gain_two), custom_call_target="tpu_custom_call" | custom-call | flops 8589934592 | bytes 20971520 | tf_op jit(solution)/shard_map/pallas_call | solution.py:1154
  508.6 0.7 reduce_sum.9
  509.4 0.5 slice_bitcast_fusion
  509.9 4.9 fusion.1
  514.8 1.6 fusion.2
  516.4 1.8 slice.43
  518.2 1.0 copy.26
  519.1 1.0 copy.27
  (15 shorter events, 0.3 us)
Async XLA Ops:
  7.2 270.4 %reduce-scatter.5.cloned.1.call-start = ((), (), s32[]{:S(2)}) async-start(), calls=%async_computation.4 | async-start | bytes 5242880 | tf_op jit(solution)/shard_map/reduce_scatter | solution.py:1185
  200.3 225.2 %reduce-scatter.7.cloned.1.call-start = ((), (), s32[]{:S(2)}) async-start(), calls=%async_computation.5 | async-start | bytes 10485760 | tf_op jit(solution)/shard_map/reduce_scatter | solution.py:1185
  280.3 177.2 %reduce-scatter.9.cloned.1.call-start = ((), (), s32[]{:S(2)}) async-start(), calls=%async_computation.6 | async-start | bytes 1310720 | tf_op jit(solution)/shard_map/reduce_scatter | solution.py:1185
  429.5 85.2 %reduce-scatter.11.cloned.1.call-start = ((), (), s32[]{:S(2)}) async-start(), calls=%async_computation.7 | async-start | bytes 1966080 | tf_op jit(solution)/shard_map/reduce_scatter | solution.py:1185
  509.9 8.3 %copy-start.1 = (bf16[256,2048]{1,0:T(8,128)(2,1)S(1)}, bf16[256,2048]{1,0:T(8,128)(2,1)}, u32[]{:S(2)}) copy-start(bf16[256,2048]{1,0:T(8,128)(2,1)} %get-tuple-element.100) | copy-start | bytes 3145732
  509.9 9.3 %copy-start = (bf16[256,2048]{1,0:T(8,128)(2,1)S(1)}, bf16[256,2048]{1,0:T(8,128)(2,1)}, u32[]{:S(2)}) copy-start(bf16[256,2048]{1,0:T(8,128)(2,1)} %get-tuple-element.101) | copy-start | bytes 3145732
Sparse Core Ops, SparseCore 0:
  200.4 77.1 reduce-scatter.4
  280.5 144.9 reduce-scatter.6
  429.7 27.8 reduce-scatter.8
  459.7 34.9 reduce-scatter.10

commit v2 on v1

--- a/solution.py
+++ b/solution.py
@@ -33,32 +33,48 @@
     return lax.dot_general(a, b, (((0,), (0,)), ((), ())), preferred_element_type=F32)
 
 
-def layout(length_row, group_rows):
-    token_place = jnp.arange(group_rows, dtype=jnp.int32)
-    start = jnp.zeros((group_rows,), jnp.int32)
-    end = jnp.int32(0)
-    for k in range(length_row.shape[0]):
-        end = end + length_row[k]
-        start = jnp.where(token_place >= end, end, start)
-    return (start, token_place - start)
-
-
-def rope_table(position):
-    half_dim = HD // 2
-    freq_index = jnp.arange(half_dim, dtype=F32)
-    base_freq = jnp.exp(-math.log(500000.0) * 2.0 * freq_index / HD)
-    wavelength = 2.0 * math.pi / base_freq
+def place_tables(group):
+    index = np.arange(HD // 2, dtype=np.float64)
+    base = np.exp(-math.log(500000.0) * 2.0 * index / HD)
+    wavelength = 2.0 * math.pi / base
     smooth = (8192.0 / wavelength - 1.0) / 3.0
-    blended = (1.0 - smooth) * base_freq / 32.0 + smooth * base_freq
-    frequency = jnp.where(
-        wavelength < 2048.0, base_freq, jnp.where(wavelength > 8192.0, base_freq / 32.0, blended)
-    )
-    angles = position.astype(F32)[:, None] * frequency[None, :]
-    cos_half, sin_half = (jnp.cos(angles), jnp.sin(angles))
+    blended = (1.0 - smooth) * base / 32.0 + smooth * base
+    frequency = np.where(
+        wavelength < 2048.0, base, np.where(wavelength > 8192.0, base / 32.0, blended)
+    )
+    angles = np.arange(group, dtype=np.float64)[:, None] * frequency[None, :]
+    cos_half, sin_half = np.cos(angles), np.sin(angles)
     return (
-        jnp.concatenate([cos_half] * 4, axis=1),
-        jnp.concatenate([-sin_half, sin_half, -sin_half, sin_half], axis=1),
-    )
+        np.concatenate([cos_half] * 4, axis=1).astype(np.float32),
+        np.concatenate([-sin_half, sin_half, -sin_half, sin_half], axis=1).astype(np.float32),
+    )
+
+
+def ends_of(lengths):
+    ends, end = [], 0
+    for k in range(lengths.shape[1]):
+        end = end + lengths[0, k]
+        ends.append(end)
+    return ends
+
+
+def starts_of(places, ends):
+    start = jnp.zeros_like(places)
+    for end in ends:
+        start = jnp.where(places >= end, end, start)
+    return start
+
+
+def turn_tables(ends, first, count, cos_place, sin_place):
+    places = lax.broadcasted_iota(jnp.int32, (count, LANES), 0) + first
+    cos_start, sin_start = jnp.ones((count, LANES), F32), jnp.zeros((count, LANES), F32)
+    for end in ends:
+        at = pl.ds(jnp.minimum(end, cos_place.shape[0] - 1), 1)
+        cos_start = jnp.where(places >= end, cos_place[at, :], cos_start)
+        sin_start = jnp.where(places >= end, sin_place[at, :], sin_start)
+    rows = pl.ds(first, count)
+    cos, sin = cos_place[rows, :], sin_place[rows, :]
+    return cos * cos_start + sin * sin_start, sin * cos_start - cos * sin_start
 
 
 class Peers:
@@ -152,34 +168,41 @@
     return ref.at[pl.ds(pl.multiple_of(index * rows + half * size, size), size)]
 
 
-def gather(peers, wire, buf, rows, use, after_forward=None):
-    steps = list(peers.steps())
-    part = lambda index, half: half_block(buf, index, rows, half)
+def gather(peers, wire, buf, rows):
+    steps, half = list(peers.steps()), rows // 2
+    part = lambda index, side: half_block(buf, index, rows, side)
+    span = lambda index, side: (pl.multiple_of(index * rows + side * half, half), half)
     me, major = peers.at(0, 0), peers.at(1, 0)
     send = lambda ref, device: wire.copy(ref, ref, device)
     minor_a = [send(part(me, 0), peers.minor(j)) for j in steps]
     major_b = send(part(me, 1), peers.major())
     minor_b = [send(part(me, 1), peers.minor(j)) for j in steps]
     major_a = send(part(me, 0), peers.major())
-    use(me)
-    forward_a, forward_b = [], []
+    yield [(pl.multiple_of(me * rows, rows), rows)]
+    forward = []
     for j, copy in zip(steps, minor_a):
         copy.wait_recv()
-        forward_a.append(send(part(peers.at(0, -j), 0), peers.major()))
+        forward.append(send(part(peers.at(0, -j), 0), peers.major()))
     major_b.wait_recv()
-    for j in steps:
-        forward_b.append(send(part(major, 1), peers.minor(j)))
-    if after_forward is not None:
-        after_forward()
-    for j, copy in zip(steps, minor_b):
+    forward += [send(part(major, 1), peers.minor(j)) for j in steps]
+    yield [span(peers.at(0, -j), 0) for j in steps] + [span(major, 1)]
+    for copy in (*minor_b, major_a):
         copy.wait_recv()
-        use(peers.at(0, -j))
-    major_a.wait_recv()
-    use(major)
-    for j, copy_a, copy_b in zip(steps, forward_a, forward_b):
-        copy_a.wait_recv()
-        copy_b.wait_recv()
-        use(peers.at(1, -j))
+    yield [span(peers.at(0, -j), 1) for j in steps] + [span(major, 0)]
+    for copy in forward:
+        copy.wait_recv()
+    yield [(pl.multiple_of(peers.at(1, -j) * rows, rows), rows) for j in steps]
+
+
+def load_rows(ref, spans):
+    return jnp.concatenate([ref[pl.ds(first, count), :] for first, count in spans], axis=0)
+
+
+def store_rows(ref, spans, lanes, value):
+    at = 0
+    for first, count in spans:
+        ref[pl.ds(first, count), lanes] = value[at : at + count]
+        at += count
 
 
 def add_rows(target, others, size):
@@ -266,12 +289,13 @@
 
 
 def project_kernel(
-    tokens, gain, cos_table, sin_table, w_query, w_key, w_value,
-    gathered_out, query_out, key_out, value_out,
+    lengths, tokens, gain, cos_place, sin_place, w_query, w_key, w_value,
+    gathered_out, query_out, key_out, value_out, cos_out, sin_out,
     gathered, weights, raw_key, raw_value, send_sem, recv_sem, local_sem,
 ):
     peers = Peers()
     rows, depth = tokens.shape
+    group = gathered.shape[0]
     q_width, kv_heads = w_query.shape[1], w_key.shape[1] // HD
     kv_width = kv_heads * LANES
     local = Local(local_sem)
@@ -280,7 +304,6 @@
         local.copy(w_value, raw_value),
         local.copy(w_query, weights.at[:, pl.ds(0, q_width)]),
     ]
-    greet(peers)
     me = peers.at(0, 0)
     gain_row = gain[...]
 
@@ -293,10 +316,19 @@
         return carry
 
     lax.fori_loop(0, rows // 16, normalize, 0)
-    started = [False]
-    saves = []
+    greet(peers)
 
     def prepare():
+        ends = ends_of(lengths)
+
+        def turn(k, carry):
+            first = pl.multiple_of(k * 128, 128)
+            cos, sin = turn_tables(ends, first, 128, cos_place, sin_place)
+            cos_out[pl.ds(first, 128), :] = cos
+            sin_out[pl.ds(first, 128), :] = sin
+            return carry
+
+        lax.fori_loop(0, group // 128, turn, 0)
         for load in loads:
             load.wait()
 
@@ -309,15 +341,15 @@
 
         lax.fori_loop(0, depth // 128, some, 0)
 
-    def use(index):
-        if not started[0]:
-            started[0] = True
+    wire = Wire(send_sem, recv_sem)
+    for step, spans in enumerate(gather(peers, wire, gathered, rows)):
+        if step == 0:
             prepare()
-        at = pl.ds(pl.multiple_of(index * rows, rows), rows)
-        saves.append(local.copy(gathered.at[at], gathered_out.at[at]))
-        cos, sin = cos_table[at, :], sin_table[at, :]
-        normed = gathered[at, :]
-        for base, width, out, turn in (
+        if step == 3:
+            save = local.copy(gathered, gathered_out)
+        cos, sin = load_rows(cos_out, spans), load_rows(sin_out, spans)
+        normed = load_rows(gathered, spans)
+        for base, width, out, turned in (
             (0, q_width, query_out, True),
             (q_width, kv_width, key_out, True),
             (q_width + kv_width, kv_width, value_out, False),
@@ -325,15 +357,11 @@
             raw = dot_nn(normed, weights[:, base : base + width])
             for c in range(0, width, LANES):
                 piece = raw[:, c : c + LANES]
-                if turn:
+                if turned:
                     piece = piece * cos + swap_halves(piece) * sin
-                out[at, c : c + LANES] = piece.astype(BF16)
-
-    wire = Wire(send_sem, recv_sem)
-    gather(peers, wire, gathered, rows, use)
+                store_rows(out, spans, slice(c, c + LANES), piece.astype(BF16))
     wire.wait_sends()
-    for save in saves:
-        save.wait()
+    save.wait()
 
 
 def any_spec():
@@ -350,7 +378,11 @@
     )
 
 
-def project(tokens, gain, cos_table, sin_table, w_query, w_key, w_value):
+def smem_spec():
+    return pl.BlockSpec(memory_space=pltpu.SMEM)
+
+
+def project(lengths, tokens, gain, w_query, w_key, w_value):
     n = lax.axis_size("tensor")
     rows, depth = tokens.shape
     group = rows * n
@@ -363,16 +395,18 @@
             jax.ShapeDtypeStruct((group, q_width), BF16),
             jax.ShapeDtypeStruct((group, kv_width), BF16),
             jax.ShapeDtypeStruct((group, kv_width), BF16),
-        ),
-        in_specs=[vmem_spec()] * 4 + [any_spec()] * 3,
-        out_specs=(any_spec(), vmem_spec(), vmem_spec(), vmem_spec()),
+            jax.ShapeDtypeStruct((group, LANES), F32),
+            jax.ShapeDtypeStruct((group, LANES), F32),
+        ),
+        in_specs=[smem_spec()] + [vmem_spec()] * 4 + [any_spec()] * 3,
+        out_specs=(any_spec(),) + (vmem_spec(),) * 5,
         scratch_shapes=[
             pltpu.VMEM((group, depth), BF16),
             pltpu.VMEM((depth, q_width + 2 * kv_width), BF16),
             pltpu.VMEM((depth, kv_raw), BF16),
             pltpu.VMEM((depth, kv_raw), BF16),
             *wires(n),
-            pltpu.SemaphoreType.DMA((3 + n,)),
+            pltpu.SemaphoreType.DMA((4,)),
         ],
         cost_estimate=pl.CostEstimate(
             flops=2 * group * depth * (q_width + 2 * kv_width),
@@ -380,20 +414,24 @@
             transcendentals=0,
         ),
         compiler_params=params(1),
-    )(tokens, gain, cos_table, sin_table, w_query, w_key, w_value)
+    )(lengths, tokens, gain, *place_tables(group), w_query, w_key, w_value)
 
 
 def attend_kernel(
-    query, key, value, start, tokens, gain, w_out, cotangent,
-    attended, log_total, state_out, normed_out, cot_a, cot_b,
-    w_buf, part, slots, send_sem, recv_sem, cot_send, cot_recv, local_sem,
+    lengths, query, key, value, gain, tokens_in, w_out, cotangent,
+    attended_out, log_out, state_out, normed_out, cot_a, cot_b,
+    tokens, w_buf, attended, log_total, part, slots,
+    send_sem, recv_sem, cot_send, cot_recv, local_sem,
 ):
     peers = Peers()
     rows, depth = tokens.shape
     group, q_width = query.shape
     pairs_per_kv = q_width // LANES // (key.shape[1] // LANES)
-    load = Local(local_sem).copy(w_out, w_buf)
+    ends = ends_of(lengths)
+    local = Local(local_sem)
+    loads = [local.copy(w_out, w_buf), local.copy(tokens_in, tokens)]
     greet(peers)
+    log_total[...] = jnp.zeros_like(log_total)
     cot_wire = Wire(cot_send, cot_recv)
     for k, j in enumerate(peers.steps()):
         cot_wire.copy(half_block(cotangent, 0, rows, 0), cot_a.at[k], peers.minor(j))
@@ -414,7 +452,9 @@
             first = first_head(tile)
             column = lax.broadcasted_iota(jnp.int32, (tile, keys), 1)
             row = lax.broadcasted_iota(jnp.int32, (tile, keys), 0) + i * tile
-            allowed = (column >= start[at, :]) & (column <= row)
+            start = starts_of(lax.broadcasted_iota(jnp.int32, (tile, 1), 0) + i * tile, ends)
+            allowed = (column >= start) & (column <= row)
+            logs = log_total[at, :]
             outs = []
             for h in range(2):
                 own = first if h == 0 else jnp.logical_not(first)
@@ -424,13 +464,18 @@
                 weights = jnp.exp2((scores - row_max) * SCALE2)
                 row_sum = jnp.sum(weights, axis=-1, keepdims=True)
                 outs.append(dot_nn(weights.astype(BF16), value_rows) / row_sum)
-                log_total[pair * 2 + h, at, :] = row_max * SCALE2 + jnp.log2(row_sum)
+                logs = jnp.where(
+                    lane_of(tile) == pair * 2 + h, row_max * SCALE2 + jnp.log2(row_sum), logs
+                )
+            log_total[at, :] = logs
             attended[at, lanes] = jnp.where(first, outs[0], outs[1]).astype(BF16)
             return carry
 
         lax.fori_loop(0, q_width // LANES, one_pair, 0)
 
-    load.wait()
+    saves = [local.copy(attended, attended_out), local.copy(log_total, log_out)]
+    for load in loads:
+        load.wait()
 
     def make(first, count):
         at = pl.ds(pl.multiple_of(first * rows, rows), count * rows)
@@ -458,11 +503,11 @@
 
         lax.fori_loop(0, half // 16, finish, 0)
     wire.wait_sends()
-    for copy in cot_wire.copies:
+    for copy in (*cot_wire.copies, *saves):
         copy.wait()
 
 
-def attend(query, key, value, start, tokens, gain, w_out, cotangent):
+def attend(lengths, query, key, value, tokens, gain, w_out, cotangent):
     n = lax.axis_size("tensor")
     rows, depth = tokens.shape
     group, q_width = query.shape
@@ -471,28 +516,31 @@
         attend_kernel,
         out_shape=(
             jax.ShapeDtypeStruct((group, q_width), BF16),
-            jax.ShapeDtypeStruct((q_width // HD, group, 1), F32),
+            jax.ShapeDtypeStruct((group, LANES), F32),
             jax.ShapeDtypeStruct((rows, depth), F32),
             jax.ShapeDtypeStruct((rows, depth), BF16),
             jax.ShapeDtypeStruct((m - 1, rows // 2, depth), BF16),
             jax.ShapeDtypeStruct((rows // 2, depth), BF16),
         ),
-        in_specs=[vmem_spec()] * 6 + [any_spec()] * 2,
-        out_specs=(vmem_spec(), vmem_spec(), vmem_spec(), vmem_spec(), any_spec(), any_spec()),
+        in_specs=[smem_spec()] + [vmem_spec()] * 4 + [any_spec()] * 3,
+        out_specs=(any_spec(), any_spec(), vmem_spec(), vmem_spec(), any_spec(), any_spec()),
         scratch_shapes=[
+            pltpu.VMEM((rows, depth), BF16),
             pltpu.VMEM(w_out.shape, BF16),
+            pltpu.VMEM((group, q_width), BF16),
+            pltpu.VMEM((group, LANES), F32),
             pltpu.VMEM((group, depth), BF16),
             slots_for(n, rows, depth),
             *wires(n),
             pltpu.SemaphoreType.DMA((m,)),
             pltpu.SemaphoreType.DMA((m,)),
-            pltpu.SemaphoreType.DMA((1,)),
+            pltpu.SemaphoreType.DMA((4,)),
         ],
         cost_estimate=pl.CostEstimate(
             flops=2 * group * depth * q_width * 4, bytes_accessed=40 * 2**20, transcendentals=0
         ),
         compiler_params=params(2),
-    )(query, key, value, start, tokens, gain, w_out, cotangent)
+    )(lengths, query, key, value, gain, tokens, w_out, cotangent)
 
 
 class Exchange:
@@ -544,76 +592,89 @@
     cot_loads.append(local.copy(cot_b, half_block(cot, major, rows, 1)))
     greet(peers, core=True)
     first_load.wait()
-    saves, waiting = [], list(loads)
-
-    def use(index):
-        while waiting:
-            waiting.pop().wait()
-        at = pl.ds(pl.multiple_of(index * rows, rows), rows)
-        saves.append(local.copy(gathered.at[at], gathered_out.at[at]))
+
+    def use(spans):
         tile = 512
 
         def some(k, carry):
             lanes = pl.ds(pl.multiple_of(k * tile, tile), tile)
-            x = gathered[at, :]
+            x = load_rows(gathered, spans)
             gate = dot_nn(x, gate_buf[:, lanes])
             up = dot_nn(x, up_buf[:, lanes])
             sigmoid = jax.nn.sigmoid(gate)
             silu = gate * sigmoid
-            hidden[at, lanes] = (silu * up).astype(BF16)
-            slope_up[at, lanes] = silu.astype(BF16)
-            slope_gate[at, lanes] = (up * sigmoid * (1.0 + gate * (1.0 - sigmoid))).astype(BF16)
+            slope = up * sigmoid * (1.0 + gate * (1.0 - sigmoid))
+            store_rows(hidden, spans, lanes, (silu * up).astype(BF16))
+            store_rows(slope_up, spans, lanes, silu.astype(BF16))
+            store_rows(slope_gate, spans, lanes, slope.astype(BF16))
             return carry
 
         lax.fori_loop(0, units // tile, some, 0)
-        for source, target in (
-            (hidden, hidden_out), (slope_gate, slope_gate_out), (slope_up, slope_up_out)
-        ):
-            saves.append(local.copy(source.at[at], target.at[at]))
 
     cot_wire = Wire(cot_send, cot_recv)
-    cot_copies = []
+    rest = ([], [])
+    width = depth // 2
 
     def send_rest():
         for load in cot_loads:
             load.wait()
-        send = lambda index, half, device: cot_copies.append(
-            cot_wire.copy(
-                half_block(cot, index, rows, half), half_block(cot, index, rows, half), device
-            )
-        )
-        for j in peers.steps():
-            send(me, 1, peers.minor(j))
-        send(me, 0, peers.major())
-        for j in peers.steps():
-            send(peers.at(0, -j), 0, peers.major())
-            send(major, 1, peers.minor(j))
+        for side in range(2):
+            lanes = pl.ds(side * width, width)
+
+            def send(index, half, device):
+                ref = half_block(cot, index, rows, half).at[:, lanes]
+                rest[side].append(cot_wire.copy(ref, ref, device))
+
+            for j in peers.steps():
+                send(me, 1, peers.minor(j))
+                send(major, 1, peers.minor(j))
+            send(me, 0, peers.major())
+            for j in peers.steps():
+                send(peers.at(0, -j), 0, peers.major())
 
     wire = Wire(send_sem, recv_sem)
-    gather(peers, wire, gathered, rows, use, send_rest)
-    for copy in cot_copies:
-        copy.wait_recv()
-    saves.append(local.copy(cot, cot_out))
+    for step, spans in enumerate(gather(peers, wire, gathered, rows)):
+        if step == 0:
+            for load in loads:
+                load.wait()
+        if step == 3:
+            send_rest()
+        use(spans)
+    saves = [
+        local.copy(gathered, gathered_out),
+        local.copy(hidden, hidden_out),
+        local.copy(slope_gate, slope_gate_out),
+        local.copy(slope_up, slope_up_out),
+    ]
     columns = stage.shape[2]
-
-    def tile(index, target, add):
-        lanes = pl.ds(pl.multiple_of(index * columns, columns), columns)
-        step = 512
-
-        def some(k, carry):
-            at = pl.ds(pl.multiple_of(k * step, step), step)
-            put(target, (at, slice(None)), dot_tn(hidden[:, at], cot[:, lanes]), add)
-            return carry
-
-        lax.fori_loop(0, units // step, some, 0)
+    pairs = received.shape[0]
+    arrived = set()
+
+    def tile_of(side):
+        def tile(index, target, add):
+            if side not in arrived:
+                arrived.add(side)
+                for copy in rest[side]:
+                    copy.wait_recv()
+            lanes = pl.ds(pl.multiple_of(index * columns, columns), columns)
+            step = 512
+
+            def some(k, carry):
+                at = pl.ds(pl.multiple_of(k * step, step), step)
+                put(target, (at, slice(None)), dot_tn(hidden[:, at], cot[:, lanes]), add)
+                return carry
+
+            lax.fori_loop(0, units // step, some, 0)
+
+        return tile
 
     def save(k, ref):
         saves.append(local.copy(ref, grad_down_out.at[pl.ds(k * units, units)]))
 
-    pairs = received.shape[0]
     Exchange(Wire(core_send, core_recv), stage, received).run(
-        [(tile, save, k) for k in range(pairs)]
-    )
+        [(tile_of(2 * k // pairs), save, k) for k in range(pairs)]
+    )
+    saves.append(local.copy(cot, cot_out))
     wire.wait_sends()
     cot_wire.wait_sends()
     for copy in saves:
@@ -645,10 +706,11 @@
             pltpu.VMEM((2, units, columns), BF16),
             pltpu.VMEM((pairs, units, columns), BF16),
             *wires(n),
-            *wires(n),
+            pltpu.SemaphoreType.DMA((2 * wire_count(n),)),
+            pltpu.SemaphoreType.DMA((2 * wire_count(n),)),
             pltpu.SemaphoreType.DMA((pairs,)),
             pltpu.SemaphoreType.DMA((pairs,)),
-            pltpu.SemaphoreType.DMA((4 * n + pairs + n + 8,)),
+            pltpu.SemaphoreType.DMA((3 + n // 2 + 1 + 5 + pairs,)),
         ],
         cost_estimate=pl.CostEstimate(
             flops=6 * group * depth * units, bytes_accessed=60 * 2**20, transcendentals=0
@@ -682,30 +744,44 @@
     chunks = units // chunk
     local = Local(local_sem)
     load_cot = local.copy(cot_all, cot)
-    down_chunk = lambda c: local.copy(w_down.at[pl.ds(c * chunk, chunk)], down_buf.at[c % 2])
-    down_loads = [down_chunk(0), down_chunk(1)]
-    load_slopes = [local.copy(slope_gate, grad_gate), local.copy(slope_up, grad_up)]
-    loads = [local.copy(w_gate, gate_buf), local.copy(w_up, up_buf)]
-    load_state = local.copy(state, grad_state_out)
+
+    def load_down(k):
+        source = w_down.at[pl.ds(k % chunks * chunk, chunk)]
+        return local.copy(source, down_buf.at[k % 2])
+
+    downs = [load_down(0)]
+    slopes = [local.copy(slope_gate, grad_gate), local.copy(slope_up, grad_up)]
+    downs.append(load_down(1))
     greet(peers, core=True)
-    load_cot.wait()
-    for c in range(chunks):
-        down_loads[c].wait()
-        if c == 0:
-            for load in load_slopes:
-                load.wait()
-        lanes = slice(c * chunk, (c + 1) * chunk)
-        grad_hidden = dot_nt(cot[...], down_buf[c % 2])
-        grad_gate[:, lanes] = (grad_hidden * grad_gate[:, lanes].astype(F32)).astype(BF16)
-        grad_up[:, lanes] = (grad_hidden * grad_up[:, lanes].astype(F32)).astype(BF16)
-        if c + 2 < chunks:
-            down_loads.append(down_chunk(c + 2))
-    load_gathered = local.copy(gathered_in, cot)
-    for load in loads:
-        load.wait()
+    later = []
 
     def make(first, count):
         at = pl.ds(pl.multiple_of(first * rows, rows), count * rows)
+        base = chunks if later else 0
+        for c in range(chunks):
+            downs[base + c].wait()
+            if not later:
+                load_cot.wait()
+                for load in slopes:
+                    load.wait()
+                later.extend(
+                    [
+                        local.copy(w_gate, gate_buf),
+                        local.copy(w_up, up_buf),
+                        local.copy(state, grad_state_out),
+                    ]
+                )
+            lanes = slice(c * chunk, (c + 1) * chunk)
+            grad_hidden = dot_nt(cot[at, :], down_buf[c % 2])
+            grad_gate[at, lanes] = (grad_hidden * grad_gate[at, lanes].astype(F32)).astype(BF16)
+            grad_up[at, lanes] = (grad_hidden * grad_up[at, lanes].astype(F32)).astype(BF16)
+            if base + c + 2 < 2 * chunks:
+                downs.append(load_down(base + c + 2))
+        if base == 0:
+            for load in later[:2]:
+                load.wait()
+        else:
+            later.append(local.copy(gathered_in, cot))
         step = 512
 
         def some(k, carry):
@@ -742,7 +818,7 @@
         return save
 
     def weight_grads():
-        load_gathered.wait()
+        later[3].wait()
         pairs = received.shape[0] // 2
         Exchange(Wire(core_send, core_recv), stage, received).run(
             [(tile_of(grad_gate), save_at(0), k) for k in range(pairs)]
@@ -751,7 +827,7 @@
 
     wire = Wire(send_sem, recv_sem)
     sums = scatter(peers, wire, part, slots, rows, make, weight_grads)
-    load_state.wait()
+    later[2].wait()
     gain_row = gain[...]
     half = rows // 2
     gain_out[...] = jnp.zeros_like(gain_out)
@@ -809,7 +885,7 @@
             *wires(n),
             pltpu.SemaphoreType.DMA((2 * pairs,)),
             pltpu.SemaphoreType.DMA((2 * pairs,)),
-            pltpu.SemaphoreType.DMA((8 + units // chunk + 2 * pairs,)),
+            pltpu.SemaphoreType.DMA((7 + 2 * (units // chunk) + 2 * pairs,)),
         ],
         cost_estimate=pl.CostEstimate(
             flops=10 * group * depth * units, bytes_accessed=80 * 2**20, transcendentals=0
@@ -819,9 +895,10 @@
 
 
 def attend_back_kernel(
-    grad_mixed, query, key, value, attended, log_total, start, cos_table, sin_table,
-    tokens, gain, grad_state, gathered_in, w_out, w_query, w_key, w_value,
-    grad_tokens_out, gain_out, grad_out_out, grad_qkv_out,
+    lengths, gain, grad_mixed, query_in, key_in, value_in, attended_in, log_in, cos_in, sin_in,
+    tokens_in, state_in, gathered_in, w_out, w_query, w_key, w_value,
+    grad_tokens_out, gain_out, grads_out,
+    query, key, value, attended, log_total, cos_table, sin_table, tokens, grad_state,
     mixed, out_buf, query_buf, key_buf, value_buf, gathered, grad_att, key_acc, value_acc, grads, part, slots,
     stage_out, got_out, stage_qkv, got_qkv,
     send_sem, recv_sem, sums_send, sums_recv, out_send, out_recv, qkv_send, qkv_recv, local_sem,
@@ -836,7 +913,12 @@
     local = Local(local_sem)
     first_load = local.copy(grad_mixed, block(mixed, me, rows))
     load_out = local.copy(w_out, out_buf)
-    loads = [
+    sources = (
+        query_in, key_in, value_in, attended_in, log_in, cos_in, sin_in, tokens_in, state_in
+    )
+    buffers = (query, key, value, attended, log_total, cos_table, sin_table, tokens, grad_state)
+    loads = [local.copy(source, buffer) for source, buffer in zip(sources, buffers)]
+    loads += [
         local.copy(w_query, query_buf),
         local.copy(w_key, key_buf),
         local.copy(w_value, value_buf),
@@ -844,27 +926,32 @@
     ]
     greet(peers, core=True)
     first_load.wait()
-    waiting, saves = [load_out], []
-
-    def use(index):
-        while waiting:
-            waiting.pop().wait()
-        at = pl.ds(pl.multiple_of(index * rows, rows), rows)
-        grad_att[at, :] = dot_nt(mixed[at, :], out_buf[...]).astype(BF16)
-
+    ends, saves = ends_of(lengths), []
     gather_wire = Wire(send_sem, recv_sem)
-    gather(peers, gather_wire, mixed, rows, use)
-
+    for step, spans in enumerate(gather(peers, gather_wire, mixed, rows)):
+        if step == 0:
+            load_out.wait()
+        grad_rows = dot_nt(load_rows(mixed, spans), out_buf[...]).astype(BF16)
+        store_rows(grad_att, spans, slice(None), grad_rows)
+
+    for load in loads:
+        load.wait()
     columns = stage_out.shape[2]
 
     def out_tile(index, target, add):
         lanes = pl.ds(pl.multiple_of(index * columns, columns), columns)
         put(target, (slice(None), slice(None)), dot_tn(attended[...], mixed[:, lanes]), add)
 
+    pairs = got_out.shape[0]
+    width = grads.shape[1]
+
     def out_save(k, ref):
-        saves.append(local.copy(ref, grad_out_out.at[pl.ds(k * q_width, q_width)]))
-
-    pairs = got_out.shape[0]
+        for c in range(q_width // columns):
+            target = grads_out.at[
+                pl.ds(k * columns, columns), pl.ds(width + c * columns, columns)
+            ]
+            saves.append(local.copy(ref.at[pl.ds(c * columns, columns)], target))
+
     Exchange(Wire(out_send, out_recv), stage_out, got_out).run(
         [(out_tile, out_save, k) for k in range(pairs)]
     )
@@ -887,7 +974,9 @@
             dots = grad_both.astype(F32) * attended[at, lanes].astype(F32)
             column = lax.broadcasted_iota(jnp.int32, (tile, keys), 1)
             row = lax.broadcasted_iota(jnp.int32, (tile, keys), 0) + i * tile
-            allowed = (column >= start[at, :]) & (column <= row)
+            start = starts_of(lax.broadcasted_iota(jnp.int32, (tile, 1), 0) + i * tile, ends)
+            allowed = (column >= start) & (column <= row)
+            logs = log_total[at, :]
             grad_queries, grad_keys, grad_values = [], 0.0, 0.0
             for h in range(2):
                 own = first if h == 0 else jnp.logical_not(first)
@@ -895,7 +984,10 @@
                 own_grad = jnp.where(own, grad_both, jnp.zeros_like(grad_both))
                 row_dot = jnp.sum(jnp.where(own, dots, 0.0), axis=-1, keepdims=True)
                 scores = dot_nt(own_query, key_rows)
-                probs = jnp.exp2(scores * SCALE2 - log_total[pair * 2 + h, at, :])
+                log_row = jnp.sum(
+                    jnp.where(lane_of(tile) == pair * 2 + h, logs, 0.0), axis=-1, keepdims=True
+                )
+                probs = jnp.exp2(scores * SCALE2 - log_row)
                 probs = jnp.where(allowed, probs, 0.0)
                 grad_probs = dot_nt(own_grad, value_rows)
                 grad_scores = (probs * (grad_probs - row_dot)).astype(BF16)
@@ -931,8 +1023,6 @@
         return carry
 
     lax.fori_loop(0, group // 128, fold, 0)
-    for load in loads:
-        load.wait()
 
     def make(first, count):
         at = pl.ds(pl.multiple_of(first * rows, rows), count * rows)
@@ -951,7 +1041,8 @@
         put(target, (slice(None), slice(None)), dot_tn(gathered[:, lanes], grads[...]), add)
 
     def qkv_save(k, ref):
-        saves.append(local.copy(ref, grad_qkv_out.at[pl.ds(k * deep, deep)]))
+        target = grads_out.at[pl.ds(k * deep, deep), pl.ds(0, width)]
+        saves.append(local.copy(ref, target))
 
     def weight_grads():
         Exchange(Wire(qkv_send, qkv_recv), stage_qkv, got_qkv).run(
@@ -984,7 +1075,7 @@
 
 
 def attend_back(
-    grad_mixed, query, key, value, attended, log_total, start, cos_table, sin_table,
+    lengths, grad_mixed, query, key, value, attended, log_total, cos_table, sin_table,
     tokens, gain, grad_state, gathered, w_out, w_query, w_key, w_value,
 ):
     n = lax.axis_size("tensor")
@@ -1000,12 +1091,17 @@
         out_shape=(
             jax.ShapeDtypeStruct((rows, depth), BF16),
             jax.ShapeDtypeStruct((8, depth), F32),
-            jax.ShapeDtypeStruct((pairs * q_width, deep), BF16),
-            jax.ShapeDtypeStruct((pairs * deep, width), BF16),
-        ),
-        in_specs=[any_spec()] + [vmem_spec()] * 11 + [any_spec()] * 5,
-        out_specs=(vmem_spec(), vmem_spec(), any_spec(), any_spec()),
+            jax.ShapeDtypeStruct((pairs * deep, width + q_width), BF16),
+        ),
+        in_specs=[smem_spec(), vmem_spec()] + [any_spec()] * 15,
+        out_specs=(vmem_spec(), vmem_spec(), any_spec()),
         scratch_shapes=[
+            *[
+                pltpu.VMEM(source.shape, source.dtype)
+                for source in (
+                    query, key, value, attended, log_total, cos_table, sin_table, tokens, grad_state
+                )
+            ],
             pltpu.VMEM((group, depth), BF16),
             pltpu.VMEM(w_out.shape, BF16),
             pltpu.VMEM(w_query.shape, BF16),
@@ -1024,14 +1120,14 @@
             pltpu.VMEM((pairs, deep, width), BF16),
             *wires(n),
             *wires(n),
-            dma(pairs), dma(pairs), dma(pairs), dma(pairs), dma(6 + 2 * pairs),
+            dma(pairs), dma(pairs), dma(pairs), dma(pairs), dma(15 + pairs * (1 + q_width // deep)),
         ],
         cost_estimate=pl.CostEstimate(
             flops=2 * group * depth * q_width * 12, bytes_accessed=60 * 2**20, transcendentals=0
         ),
         compiler_params=params(5),
-    )(grad_mixed, query, key, value, attended, log_total, start, cos_table, sin_table,
-      tokens, gain, grad_state, gathered, w_out, w_query, w_key, w_value)
+    )(lengths, gain, grad_mixed, query, key, value, attended, log_total, cos_table, sin_table,
+      tokens, grad_state, gathered, w_out, w_query, w_key, w_value)
 
 
 class GainSums:
@@ -1179,29 +1275,51 @@
     )(hidden, w_down, state, gain_one, gain_two)
 
 
+def unpack_kernel(packed, grad_query, grad_key, grad_value, grad_out):
+    first = 0
+    for target in (grad_query, grad_key, grad_value):
+        width = target.shape[1]
+        target[...] = packed[:, first : first + width].astype(F32)
+        first += width
+    deep = packed.shape[0]
+    for c in range(grad_out.shape[0] // deep):
+        at = slice(c * deep, (c + 1) * deep)
+        grad_out[at, :] = packed[:, first + c * deep : first + (c + 1) * deep].astype(F32)
+
+
+def unpack(packed, q_width, kv_raw):
+    deep = packed.shape[0]
+    return pl.pallas_call(
+        unpack_kernel,
+        out_shape=(
+            jax.ShapeDtypeStruct((deep, q_width), F32),
+            jax.ShapeDtypeStruct((deep, kv_raw), F32),
+            jax.ShapeDtypeStruct((deep, kv_raw), F32),
+            jax.ShapeDtypeStruct((q_width, deep), F32),
+        ),
+    )(packed)
+
+
 def sum_over_chips(grads):
     size = lax.axis_size("dp")
     groups = [list(range(core, size, 2)) for core in range(2)]
     return lax.psum_scatter(
         grads, "dp", scatter_dimension=0, tiled=True, axis_index_groups=groups
-    ).astype(F32)
+    )
 
 
 def local(
     tokens, lengths, gain_one, w_query, w_key, w_value, w_out, gain_two, w_gate, w_up, w_down,
     cotangent,
 ):
-    depth, group = tokens.shape[1], tokens.shape[0] * lax.axis_size("tensor")
+    depth = tokens.shape[1]
     q_width, kv_raw, units = w_query.shape[1], w_key.shape[1], w_gate.shape[1]
-    start, position = layout(lengths[0], group)
-    start = start[:, None]
-    cos_table, sin_table = rope_table(position)
     gain_one, gain_two = gain_one[None], gain_two[None]
-    gathered_one, query, key, value = project(
-        tokens, gain_one, cos_table, sin_table, w_query, w_key, w_value
+    gathered_one, query, key, value, cos_table, sin_table = project(
+        lengths, tokens, gain_one, w_query, w_key, w_value
     )
     attended, log_total, state, normed_two, cot_a, cot_b = attend(
-        query, key, value, start, tokens, gain_two, w_out, cotangent
+        lengths, query, key, value, tokens, gain_two, w_out, cotangent
     )
     gathered_two, hidden, slope_gate, slope_up, cot_all, grad_down = hidden_units(
         normed_two, cotangent, cot_a, cot_b, w_gate, w_up
@@ -1213,14 +1331,13 @@
     )
     grad_gate_up, grad_w_down = lax.optimization_barrier((grad_gate_up, grad_w_down))
     grad_w_gate_up = sum_over_chips(grad_gate_up)
-    grad_tokens, gain_one_part, grad_out, grad_qkv = attend_back(
-        grad_mixed, query, key, value, attended, log_total, start, cos_table, sin_table,
+    grad_tokens, gain_one_part, grads = attend_back(
+        lengths, grad_mixed, query, key, value, attended, log_total, cos_table, sin_table,
         tokens, gain_one, grad_state, gathered_one, w_out, w_query, w_key, w_value,
     )
-    grad_out, grad_w_gate_up = lax.optimization_barrier((grad_out, grad_w_gate_up))
-    grad_w_out = sum_over_chips(grad_out)
-    grad_qkv, grad_w_out = lax.optimization_barrier((grad_qkv, grad_w_out))
-    grad_w_qkv = sum_over_chips(grad_qkv)
+    grads, grad_w_gate_up = lax.optimization_barrier((grads, grad_w_gate_up))
+    grads = sum_over_chips(grads)
+    grad_w_query, grad_w_key, grad_w_value, grad_w_out = unpack(grads, q_width, kv_raw)
     output, gains = layer_output(hidden, w_down, state, gain_one_part, gain_two_part)
     share = depth // (lax.axis_size("tensor") * lax.axis_size("dp"))
     place = lax.rem(
@@ -1231,14 +1348,14 @@
         output,
         grad_tokens,
         gains[0],
-        grad_w_qkv[:, :q_width],
-        grad_w_qkv[:, q_width : q_width + kv_raw],
-        grad_w_qkv[:, q_width + kv_raw :],
+        grad_w_query,
+        grad_w_key,
+        grad_w_value,
         grad_w_out,
         gains[1],
-        grad_w_gate_up[:, :units],
-        grad_w_gate_up[:, units:],
-        grad_w_down,
+        grad_w_gate_up[:, :units].astype(F32),
+        grad_w_gate_up[:, units:].astype(F32),
+        grad_w_down.astype(F32),
     )
 
 

time: 530 us -> 485 us (0.915)
  waiting for transfers between devices: 59.4 us -> 40.5 us
  other arithmetic: 15.2 us -> 4.88 us
  local copies, waits for them, and re-layouts: 12.2 us -> 2.55 us
  Pallas kernels: 424 us -> 415 us
    reduce_scatter x4 -> x3, waiting for transfers between devices: 59.3 us -> 40.5 us  [sum_over_chips(): lax.psum_scatter(grads, 'dp', scatter_dimension=0, tiled=True, axis_index...]
    slice x4 -> x0, local copies, waits for them, and re-layouts: 9.63 us -> none  [the longest x1 4.88 us: local(): grad_w_gate_up[:, units:]]
  transfers between devices with their start and end apart: 4 -> 3, of which waited for: 3 -> 3; matrix products, arithmetic and copies ran while one was open for 1% -> 1% of each run, Pallas kernels for 46% -> 49%
where the time goes in v2:
time: 485 us; the launch traced here: 477 us
  Pallas kernels  415 us (86%)
  waiting for transfers between devices  40.5 us (8%)
  between operations  14.3 us (3%)
  other arithmetic  4.88 us (1%)
    pallas_call x1, Pallas kernels, attend_back(): pl.pallas_call(attend_back_kernel, out_shape=(jax.ShapeDtypeStruct((rows,...  112 us
    pallas_call x1, Pallas kernels, hidden_back(): pl.pallas_call(hidden_back_kernel, out_shape=(jax.ShapeDtypeStruct((rows,...  73.6 us
    pallas_call x1, Pallas kernels, hidden_units(): pl.pallas_call(hidden_kernel, out_shape=(wide(depth), wide(units), wide(u...  72.4 us
    pallas_call x1, Pallas kernels, attend(): pl.pallas_call(attend_kernel, out_shape=(jax.ShapeDtypeStruct((group, q_w...  57.8 us
    pallas_call x1, Pallas kernels, layer_output(): pl.pallas_call(output_kernel, out_shape=(jax.ShapeDtypeStruct((rows, dept...  49 us
    pallas_call x1, Pallas kernels, project(): pl.pallas_call(project_kernel, out_shape=(jax.ShapeDtypeStruct((group, de...  47.1 us
    reduce_scatter x3, waiting for transfers between devices, sum_over_chips(): lax.psum_scatter(grads, 'dp', scatter_dimension=0, tiled=True, axis_index...  40.5 us
  transfers between devices with their start and end apart: 3, of which 3 were waited for; matrix products, arithmetic and copies ran while one was open for 1% of the time, Pallas kernels for 49%

profile of v2, /device:TPU:0, one launch (start us, length us, event | category | flops | bytes accessed | tf_op | source)
XLA Modules:
  0.0 476.9 jit_solution(15472388912308174536)
XLA Ops:
  7.2 0.0 reduce-scatter.4.cloned.1.call-start
  7.2 47.1 %shard_map.221 = (bf16[1024,2048]{1,0:T(8,128)(2,1)}, bf16[1024,512]{1,0:T(8,128)(2,1)}, bf16[1024,256]{1,0:T(8,128)(2,1)}, bf16[1024,256]{1,0:T(8,128)(2,1)}, f32[1024,128]{1,0:T(8,128)}, /*index=5*/f32[1024,128]{1,0:T(8,128)}) custom-call(s32[1,3]{1,0:T(1,128)} %lengths.5, bf16[256,2048]{1,0:T(8,128)(2,1)} %tokens_in.3, f32[1,2048]{1,0:T(1,128)} %bitcast.8, ...), custom_call_target="tpu_custom_call" | custom-call | flops 4294967296 | bytes 41943040 | tf_op jit(solution)/shard_map/pallas_call | solution.py:391
  54.3 57.8 %shard_map.222 = (bf16[1024,512]{1,0:T(8,128)(2,1)}, f32[1024,128]{1,0:T(8,128)}, f32[256,2048]{1,0:T(8,128)}, bf16[256,2048]{1,0:T(8,128)(2,1)}, bf16[1,128,204...) custom-call(s32[1,3]{1,0:T(1,128)} %lengths.5, bf16[1024,512]{1,0:T(8,128)(2,1)} %get-tuple-element.46.query.query_in, ...), custom_call_target="tpu_custom_call" | custom-call | flops 8589934592 | bytes 41943040 | tf_op jit(solution)/shard_map/pallas_call | solution.py:515
  112.1 72.4 %shard_map.223 = (bf16[1024,2048]{1,0:T(8,128)(2,1)}, bf16[1024,2048]{1,0:T(8,128)(2,1)}, bf16[1024,2048]{1,0:T(8,128)(2,1)}, bf16[1024,2048]{1,0:T(8,128)(2,1)}...) custom-call(bf16[256,2048]{1,0:T(8,128)(2,1)} %get-tuple-element.49.normed, bf16[256,2048]{1,0:T(8,128)(2,1)} %cotangent.5, ...), custom_call_target="tpu_custom_call" | custom-call | flops 25769803776 | bytes 62914560 | tf_op jit(solution)/shard_map/pallas_call | solution.py:690
  184.5 0.0 reduce-scatter.4.cloned.1.call-update
  184.5 0.0 reduce-scatter.6.cloned.1.call-start
  184.6 73.6 %shard_map.224 = (f32[256,2048]{1,0:T(8,128)}, bf16[256,2048]{1,0:T(8,128)(2,1)}, f32[8,2048]{1,0:T(8,128)}, bf16[1024,4096]{1,0:T(8,128)(2,1)}) custom-call(bf16[1024,2048]{1,0:T(8,128)(2,1)} %get-tuple-element.54.slope_gate, bf16[1024,2048]{1,0:T(8,128)(2,1)} %get-tuple-element.55.slope_up, bf16[1024,2048]{1,0:T(8,128)(2,1)} %get-tuple-element.56.cot_all, ...), custom_call_target="tpu_custom_call" | custom-call | flops 42949672960 | bytes 83886080 | tf_op jit(solution)/shard_map/pallas_call | solution.py:864
  258.2 3.8 reduce-scatter.4.cloned.1.call-done
  262.0 0.0 reduce-scatter.6.cloned.1.call-update
  262.1 0.0 reduce-scatter.8.cloned.1.call-start
  262.1 112.4 %shard_map.225 = (bf16[256,2048]{1,0:T(8,128)(2,1)}, f32[8,2048]{1,0:T(8,128)}, bf16[1024,1280]{1,0:T(8,128)(2,1)}) custom-call(s32[1,3]{1,0:T(1,128)} %lengths.5, f32[1,2048]{1,0:T(1,128)} %bitcast.9, bf16[256,2048]{1,0:T(8,128)(2,1)} %get-tuple-element.58.grad_mixed, bf16[1024,512]{1,0:T(8,128)(2,1)} %get-tuple-element.46.query.query_in, ...), custom_call_target="tpu_custom_call" | custom-call | flops 25769803776 | bytes 62914560 | tf_op jit(solution)/shard_map/pallas_call | solution.py:1089
  374.5 35.0 %reduce-scatter.6.cloned.1.call-done = bf16[256,4096]{1,0:T(8,128)(2,1)} async-done(((bf16[1024,4096]{1,0:T(8,128)(2,1)}), bf16[256,4096]{1,0:T(8,128)(2,1)}) %reduce-scatter.6.cloned.1.call-update) | async-done | bytes 2097168 | tf_op jit(solution)/shard_map/reduce_scatter | solution.py:1306
  409.5 0.0 reduce-scatter.8.cloned.1.call-update
  409.6 0.0 copy-start.1
  409.6 49.0 %shard_map.226 = (bf16[256,2048]{1,0:T(8,128)(2,1)}, f32[2,8,128]{2,1,0:T(8,128)}) custom-call(bf16[1024,2048]{1,0:T(8,128)(2,1)} %get-tuple-element.52.hidden_in, bf16[2048,2048]{1,0:T(8,128)(2,1)} %w_down.3, f32[256,2048]{1,0:T(8,128)} %get-tuple-element.53.state, f32[8,2048]{1,0:T(8,128)} %get-tuple-element.65.gain_one, f32[8,2048]{1,0:T(8,128)} %get-tuple-element.66.gain_two), custom_call_target="tpu_custom_call" | custom-call | flops 8589934592 | bytes 20971520 | tf_op jit(solution)/shard_map/pallas_call | solution.py:1250
  458.7 0.9 reduce_sum.9
  459.5 0.1 constant_dynamic-slice_fusion
  459.6 0.5 slice_bitcast_fusion
  460.1 1.5 convert_element_type.11
  461.6 2.5 slice_convert_fusion
  464.1 1.7 reduce-scatter.8.cloned.1.call-done.packed
  465.8 2.1 shard_map.227
  468.0 1.0 copy.27
  469.0 1.0 copy.28
  (7 shorter events, 0.0 us)
Async XLA Ops:
  7.2 254.9 %reduce-scatter.4.cloned.1.call-start = ((), (), s32[]{:S(2)}) async-start(), calls=%async_computation.3 | async-start | bytes 5242880 | tf_op jit(solution)/shard_map/reduce_scatter | solution.py:1306
  184.5 225.0 %reduce-scatter.6.cloned.1.call-start = ((), (), s32[]{:S(2)}) async-start(), calls=%async_computation.4 | async-start | bytes 10485760 | tf_op jit(solution)/shard_map/reduce_scatter | solution.py:1306
  262.1 203.8 %reduce-scatter.8.cloned.1.call-start = ((), (), s32[]{:S(2)}) async-start(), calls=%async_computation.5 | async-start | bytes 3276800 | tf_op jit(solution)/shard_map/reduce_scatter | solution.py:1306
  409.6 50.5 %copy-start.1 = (bf16[2048,256]{1,0:T(8,128)(2,1)S(1)}, bf16[2048,256]{1,0:T(8,128)(2,1)}, u32[]{:S(2)}) copy-start(bf16[2048,256]{1,0:T(8,128)(2,1)} %reduce-scatter.4.cloned.1.call-done) | copy-start | bytes 3145732
  458.6 3.0 copy-start
  461.6 6.4 %copy-start.3 = (bf16[256,2048]{1,0:T(8,128)(2,1)S(1)}, bf16[256,2048]{1,0:T(8,128)(2,1)}, u32[]{:S(2)}) copy-start(bf16[256,2048]{1,0:T(8,128)(2,1)} %get-tuple-element.96) | copy-start | bytes 3145732
  464.1 4.8 %copy-start.2 = (bf16[256,2048]{1,0:T(8,128)(2,1)S(1)}, bf16[256,2048]{1,0:T(8,128)(2,1)}, u32[]{:S(2)}) copy-start(bf16[256,2048]{1,0:T(8,128)(2,1)} %get-tuple-element.97) | copy-start | bytes 3145732
Sparse Core Ops, SparseCore 0:
  184.6 77.3 reduce-scatter.3
  264.5 144.9 reduce-scatter.5
  412.0 53.8 reduce-scatter.7

commit v3 on v2

--- a/solution.py
+++ b/solution.py
@@ -107,14 +107,15 @@
     return {"dp": lax.axis_index("dp") + 1 - 2 * core_of()}
 
 
-def greet(peers, core=False):
+def greet(peers, core=False, chips=False):
     barrier = pltpu.get_barrier_semaphore()
     for step in peers.steps():
         pl.semaphore_signal(barrier, inc=1, device_id=peers.minor(step), device_id_type=MESH)
     pl.semaphore_signal(barrier, inc=1, device_id=peers.major(), device_id_type=MESH)
     if core:
         pl.semaphore_signal(barrier, inc=1, device_id=other_core(), device_id_type=MESH)
-    pl.semaphore_wait(barrier, peers.m + (1 if core else 0))
+    more = greet_chips() if chips else 0
+    pl.semaphore_wait(barrier, peers.m + (1 if core else 0) + more)
 
 
 class Wire:
@@ -217,7 +218,7 @@
     lax.fori_loop(0, size // 16, some, 0)
 
 
-def scatter(peers, wire, part_ref, slots, rows, make, meanwhile=None):
+def scatter(peers, wire, part_ref, slots, rows, make, meanwhile=None, tick=lambda: None, early=None):
     steps = list(peers.steps())
     part = lambda index, half: half_block(part_ref, index, rows, half)
     me, major = peers.at(0, 0), peers.at(1, 0)
@@ -238,6 +239,9 @@
         wire.copy(part(peers.at(0, j), 1), direct_b[k], peers.minor(j))
         for k, j in enumerate(steps)
     ]
+    tick()
+    if early is not None:
+        early()
     done_a = []
     for k, j in enumerate(steps):
         first_a[k].wait_recv()
@@ -249,10 +253,15 @@
     target = part(major, 1)
     add_rows(target, via_b, rows // 2)
     done_b = wire.copy(target, sum_b, peers.major())
+    tick()
     if meanwhile is not None:
         meanwhile()
-    for copy in (plain_a, *plain_b, *done_a, done_b):
+    for copy in (plain_a, *plain_b):
         copy.wait_recv()
+    tick()
+    for copy in (*done_a, done_b):
+        copy.wait_recv()
+    tick()
     return (
         (part(me, 0), direct_a, *sum_a),
         (part(me, 1), sum_b, *direct_b),
@@ -286,6 +295,392 @@
         first = first_head(both.shape[0])
         out += [jnp.where(first, both, swapped), jnp.where(first, swapped, both)]
     return out
+
+
+class ChipSum:
+    def __init__(self, source, base, scratch, landing, total, first, span):
+        self.source, self.base, self.landing, self.total = source, base, landing, total
+        self.stage, self.last, *sems = scratch
+        self.send_sem, self.recv_sem, self.load_sem = sems
+        self.size = lax.axis_size("dp") // 2
+        self.pitch = source.shape[0] // self.size
+        self.dp = lax.axis_index("dp")
+        place = lax.div(self.dp, np.int32(2))
+        self.place, self.along = place, (place, self.size - 1 - place)
+        self.chunks = self.send_sem.shape[2]
+        self.deep = landing.shape[2]
+        self.rows = self.deep // self.chunks
+        self.pending = None
+        events = []
+        step = span / ((self.size - 1) * self.chunks)
+        for hop in range(self.size - 1):
+            for rank in range(self.size - 1 - hop):
+                for c in range(self.chunks):
+                    order = rank * self.chunks + c
+                    due = first if hop == 0 else first + step * (order + hop) + 3.0 * hop
+                    events.append((due, hop, rank, c))
+        for c in range(self.chunks):
+            due = first + span - step * (self.chunks - 1 - c) + 3.0
+            events.append((max(due, max(events)[0]), self.size, 0, c))
+        self.events = sorted(events)
+
+    def dest(self, flow, rank):
+        return self.size - 1 - rank if flow == 0 else rank
+
+    def chunk(self, d, c):
+        return self.source.at[pl.ds(pl.multiple_of(d * self.pitch + self.base + c * self.rows, 16), self.rows)]
+
+    def landed(self, flow, rank, c):
+        return self.landing.at[flow, rank, pl.ds(c * self.rows, self.rows)]
+
+    def remote(self, flow, rank, c, source):
+        return pltpu.make_async_remote_copy(
+            src_ref=source,
+            dst_ref=self.landed(flow, rank, c),
+            send_sem=self.send_sem.at[flow, rank, c],
+            recv_sem=self.recv_sem.at[flow, rank, c],
+            device_id={"dp": self.dp + (2 if flow == 0 else -2)},
+            device_id_type=MESH,
+        )
+
+    def loads(self, flow, slot, sources):
+        return [
+            pltpu.make_async_copy(ref, self.stage.at[flow, slot, k], self.load_sem.at[flow, slot, k])
+            for k, ref in enumerate(sources)
+        ]
+
+    def sources(self, flow, rank, c):
+        return (self.landed(flow, rank, c), self.chunk(self.dest(flow, rank), c))
+
+    def begin(self, hop, rank, c):
+        order = rank * self.chunks + c
+        for flow in range(2):
+            if hop == 0:
+
+                @pl.when(self.along[flow] == 0)
+                def _():
+                    if order >= AHEAD:
+                        before = divmod(order - AHEAD, self.chunks)
+                        self.remote(flow, *before, self.chunk(self.dest(flow, before[0]), before[1])).wait_send()
+                    self.remote(flow, rank, c, self.chunk(self.dest(flow, rank), c)).start()
+
+            else:
+
+                @pl.when(self.along[flow] == hop)
+                def _():
+                    slot = order % 2
+                    if order >= 2:
+                        before = divmod(order - 2, self.chunks)
+                        self.remote(flow, *before, self.stage.at[flow, slot, 0]).wait_send()
+                    self.remote(flow, rank, c, self.stage.at[flow, slot, 0]).wait_recv()
+                    for load in self.loads(flow, slot, self.sources(flow, rank, c)):
+                        load.start()
+
+    def end(self, hop, rank, c):
+        order = rank * self.chunks + c
+        if hop == 0:
+            return
+        for flow in range(2):
+
+            @pl.when(self.along[flow] == hop)
+            def _():
+                slot = order % 2
+                for load in self.loads(flow, slot, self.sources(flow, rank, c)):
+                    load.wait()
+                target = self.stage.at[flow, slot, 0]
+                add_rows(target, [self.stage.at[flow, slot, 1]], self.rows)
+                self.remote(flow, rank, c, target).start()
+
+    def last_loads(self, c):
+        slot = c % 2
+        copies = [
+            pltpu.make_async_copy(
+                self.landing.at[flow, self.size - 1 - self.along[flow], pl.ds(c * self.rows, self.rows)],
+                self.last.at[slot, flow],
+                self.load_sem.at[flow, slot, 2],
+            )
+            for flow in range(2)
+        ]
+        own = pltpu.make_async_copy(
+            self.chunk(self.place, c), self.last.at[slot, 2], self.load_sem.at[slot, 0, 3]
+        )
+        return copies, own
+
+    def last_begin(self, c):
+        copies, own = self.last_loads(c)
+        own.start()
+        for flow in range(2):
+
+            @pl.when(self.along[flow] > 0)
+            def _():
+                rank = self.size - 1 - self.along[flow]
+                landed = self.landing.at[flow, rank, pl.ds(c * self.rows, self.rows)]
+                pltpu.make_async_remote_copy(
+                    src_ref=landed,
+                    dst_ref=landed,
+                    send_sem=self.send_sem.at[flow, rank, c],
+                    recv_sem=self.recv_sem.at[flow, rank, c],
+                    device_id={"dp": self.dp},
+                    device_id_type=MESH,
+                ).wait_recv()
+                copies[flow].start()
+
+    def last_end(self, c):
+        copies, own = self.last_loads(c)
+        own.wait()
+        slot = c % 2
+        for flow in range(2):
+
+            @pl.when(self.along[flow] > 0)
+            def _():
+                copies[flow].wait()
+                add_rows(self.last.at[slot, 2], [self.last.at[slot, flow]], self.rows)
+
+        self.save(c).start()
+
+    def save(self, c):
+        return pltpu.make_async_copy(
+            self.last.at[c % 2, 2],
+            self.total.at[pl.ds(c * self.rows, self.rows)],
+            self.load_sem.at[c % 2, 1, 3],
+        )
+
+    def advance(self, time):
+        while self.events and self.events[0][0] <= time:
+            _, hop, rank, c = self.events.pop(0)
+            self.settle()
+            if hop == self.size:
+                if c >= 2:
+                    self.save(c - 2).wait()
+                self.last_begin(c)
+            else:
+                self.begin(hop, rank, c)
+            self.pending = (hop, rank, c)
+
+    def settle(self):
+        if self.pending is not None:
+            hop, rank, c = self.pending
+            self.pending = None
+            if hop == self.size:
+                self.last_end(c)
+            else:
+                self.end(hop, rank, c)
+
+    def finish(self):
+        self.advance(1e9)
+        self.settle()
+        for c in range(max(self.chunks - 2, 0), self.chunks):
+            self.save(c).wait()
+        for flow in range(2):
+            for hop in range(self.size - 1):
+                depth = AHEAD if hop == 0 else 2
+                count = (self.size - 1 - hop) * self.chunks
+
+                @pl.when(self.along[flow] == hop)
+                def _():
+                    for order in range(max(count - depth, 0), count):
+                        rank, c = divmod(order, self.chunks)
+                        if hop == 0:
+                            source = self.chunk(self.dest(flow, rank), c)
+                        else:
+                            source = self.stage.at[flow, order % 2, 0]
+                        self.remote(flow, rank, c, source).wait_send()
+
+
+AHEAD = 100
+
+
+class Clock:
+    def __init__(self, sums):
+        self.sums, self.time = sums, 0.0
+
+    def start(self):
+        for one in self.sums:
+            one.start()
+
+    def to(self, time):
+        self.time = time
+        for one in self.sums:
+            one.advance(time)
+
+    def by(self, step):
+        self.to(self.time + step)
+
+    def at(self, *times):
+        left = list(times)
+        return lambda: self.to(left.pop(0))
+
+    def finish(self):
+        for one in self.sums:
+            one.finish()
+
+
+MARGIN = 12.0
+
+
+class NearChipSum:
+    def __init__(self, source, base, scratch, total, first, span):
+        self.source, self.base, self.total = source, base, total
+        self.blocks, self.landing, self.send_sem, self.recv_sem, load_sem, self.save_sem = scratch
+        self.size = lax.axis_size("dp") // 2
+        self.pitch = source.shape[0] // self.size
+        self.dp = lax.axis_index("dp")
+        self.place = lax.div(self.dp, np.int32(2))
+        self.along = (self.place, self.size - 1 - self.place)
+        self.chunks = self.send_sem.shape[2]
+        self.deep = self.landing.shape[2]
+        self.rows = self.deep // self.chunks
+        self.loads = [
+            pltpu.make_async_copy(
+                source.at[pl.ds(d * self.pitch + base, self.deep)], self.blocks.at[d], load_sem.at[d]
+            )
+            for d in range(self.size)
+        ]
+        self.step = span / ((self.size - 1) * self.chunks)
+        events = []
+        for rank in range(self.size - 1):
+            due = first + self.step * self.chunks * rank - MARGIN
+            events += [(due, 0, rank, c) for c in range(self.chunks)]
+        for hop in range(1, self.size - 1):
+            for rank in range(self.size - 1 - hop):
+                for c in range(self.chunks):
+                    due = first + self.step * (rank * self.chunks + c + hop) + hop
+                    events.append((due, hop, rank, c))
+        latest = max(events)[0]
+        for c in range(self.chunks):
+            due = max(first + span - self.step * (self.chunks - 1 - c) + 1.0, latest)
+            events.append((due, self.size, 0, c))
+        self.events = sorted(events)
+
+    def dest(self, flow, rank):
+        return self.size - 1 - rank if flow == 0 else rank
+
+    def landed(self, flow, rank, c):
+        return self.landing.at[flow, rank, pl.ds(c * self.rows, self.rows)]
+
+    def remote(self, flow, rank, c, source=None):
+        landed = self.landed(flow, rank, c)
+        return pltpu.make_async_remote_copy(
+            src_ref=landed if source is None else source,
+            dst_ref=landed,
+            send_sem=self.send_sem.at[flow, rank, c],
+            recv_sem=self.recv_sem.at[flow, rank, c],
+            device_id={"dp": self.dp + (2 if flow == 0 else -2)},
+            device_id_type=MESH,
+        )
+
+    def outer(self, flow, rank, c):
+        first = self.dest(flow, rank) * self.pitch + self.base + c * self.rows
+        return self.remote(flow, rank, c, self.source.at[pl.ds(first, self.rows)])
+
+    def start(self):
+        for load in self.loads:
+            load.start()
+
+    def send(self, rank, c):
+        for flow in range(2):
+
+            @pl.when(self.along[flow] == 0)
+            def _():
+                self.outer(flow, rank, c).start()
+
+    def pass_on(self, hop, rank, c):
+        for flow in range(2):
+
+            @pl.when(self.along[flow] == hop)
+            def _():
+                copy = self.remote(flow, rank, c)
+                copy.wait_recv()
+                own = self.blocks.at[self.dest(flow, rank), pl.ds(c * self.rows, self.rows)]
+                add_rows(self.landed(flow, rank, c), [own], self.rows)
+                copy.start()
+
+    def own(self, c):
+        return self.blocks.at[self.place, pl.ds(c * self.rows, self.rows)]
+
+    def save(self, c):
+        target = self.total.at[pl.ds(c * self.rows, self.rows)]
+        return pltpu.make_async_copy(self.own(c), target, self.save_sem.at[c])
+
+    def take(self, c):
+        for flow in range(2):
+
+            @pl.when(self.along[flow] > 0)
+            def _():
+                rank = self.size - 1 - self.along[flow]
+                self.remote(flow, rank, c).wait_recv()
+                add_rows(self.own(c), [self.landed(flow, rank, c)], self.rows)
+
+        self.save(c).start()
+
+    def advance(self, time):
+        while self.events and self.events[0][0] <= time:
+            _, hop, rank, c = self.events.pop(0)
+            if hop == 0:
+                self.send(rank, c)
+                continue
+            while self.loads:
+                self.loads.pop().wait()
+            if hop == self.size:
+                self.take(c)
+            else:
+                self.pass_on(hop, rank, c)
+
+    def finish(self):
+        self.advance(1e9)
+        for c in range(self.chunks):
+            self.save(c).wait()
+        for flow in range(2):
+            for hop in range(self.size - 1):
+
+                @pl.when(self.along[flow] == hop)
+                def _():
+                    for rank in range(self.size - 1 - hop):
+                        for c in range(self.chunks):
+                            copy = self.outer if hop == 0 else self.remote
+                            copy(flow, rank, c).wait_send()
+
+
+def near_chip_sum_scratch(size, deep, width):
+    chunks = chip_chunks(size)
+    dma = lambda *shape: pltpu.SemaphoreType.DMA(shape)
+    return [
+        pltpu.VMEM((size, deep, width), BF16),
+        pltpu.VMEM((2, size - 1, deep, width), BF16),
+        dma(2, size - 1, chunks),
+        dma(2, size - 1, chunks),
+        dma(size),
+        dma(chunks),
+    ]
+
+
+def greet_chips():
+    barrier = pltpu.get_barrier_semaphore()
+    dp, dps = lax.axis_index("dp"), lax.axis_size("dp")
+    for step in (2, dps - 2):
+        device = {"dp": lax.rem(dp + np.int32(step), np.int32(dps))}
+        pl.semaphore_signal(barrier, inc=1, device_id=device, device_id_type=MESH)
+    return 2
+
+
+def chip_chunks(size):
+    return 4 if size == 4 else 1
+
+
+def chip_sum_shapes(size, deep, width):
+    chunks = chip_chunks(size)
+    rows = deep // chunks
+    dma = lambda *shape: pltpu.SemaphoreType.DMA(shape)
+    return (
+        jax.ShapeDtypeStruct((2, size - 1, deep, width), BF16),
+        [
+            pltpu.VMEM((2, 2, 2, rows, width), BF16),
+            pltpu.VMEM((2, 3, rows, width), BF16),
+            dma(2, size - 1, chunks),
+            dma(2, size - 1, chunks),
+            dma(2, 2, 4),
+        ],
+    )
 
 
 def project_kernel(
@@ -547,7 +942,7 @@
     def __init__(self, wire, stage, received):
         self.wire, self.stage, self.received, self.sent = wire, stage, received, []
 
-    def run(self, jobs):
+    def run(self, jobs, tick=lambda: None):
         mine = core_of()
         copies = []
         for k in range(len(jobs) + 1):
@@ -558,11 +953,13 @@
                     copies[k - 2].wait_send()
                 tile(2 * pair + 1 - mine, slot, False)
                 copies.append(self.wire.copy(slot, self.received.at[k], other_core()))
+                tick()
             if k >= 1:
                 tile, save, pair = jobs[k - 1]
                 copies[k - 1].wait_recv()
                 tile(2 * pair + mine, self.received.at[k - 1], True)
                 save(pair, self.received.at[k - 1])
+                tick()
         for copy in copies[-2:]:
             copy.wait_send()
 
@@ -732,10 +1129,10 @@
 
 
 def hidden_back_kernel(
-    slope_gate, slope_up, cot_all, gathered_in, state, cotangent, gain, w_down, w_gate, w_up,
-    grad_state_out, grad_mixed_out, gain_out, grad_gate_up_out,
+    slope_gate, slope_up, cot_all, gathered_in, state, cotangent, gain, w_down, w_gate, w_up, grad_down,
+    grad_state_out, grad_mixed_out, gain_out, grad_gate_up_out, landing, total_down,
     gate_buf, up_buf, down_buf, grad_gate, grad_up, cot, part, slots, stage, received,
-    send_sem, recv_sem, core_send, core_recv, local_sem,
+    send_sem, recv_sem, core_send, core_recv, local_sem, *chip_scratch,
 ):
     peers = Peers()
     rows, depth = state.shape
@@ -752,7 +1149,9 @@
     downs = [load_down(0)]
     slopes = [local.copy(slope_gate, grad_gate), local.copy(slope_up, grad_up)]
     downs.append(load_down(1))
-    greet(peers, core=True)
+    greet(peers, core=True, chips=True)
+    clock = Clock([ChipSum(grad_down, 0, chip_scratch, landing, total_down, 0.0, 72.0)])
+    clock.to(1.0)
     later = []
 
     def make(first, count):
@@ -777,6 +1176,7 @@
             grad_up[at, lanes] = (grad_hidden * grad_up[at, lanes].astype(F32)).astype(BF16)
             if base + c + 2 < 2 * chunks:
                 downs.append(load_down(base + c + 2))
+            clock.by(7.0 if base + c == 0 else 1.5)
         if base == 0:
             for load in later[:2]:
                 load.wait()
@@ -784,14 +1184,12 @@
             later.append(local.copy(gathered_in, cot))
         step = 512
 
-        def some(k, carry):
-            inner = pl.ds(pl.multiple_of(k * step, step), step)
+        for k in range(depth // step):
+            inner = slice(k * step, (k + 1) * step)
             total = dot_nt(grad_gate[at, :], gate_buf[inner, :])
             total = total + dot_nt(grad_up[at, :], up_buf[inner, :])
             part[at, inner] = total.astype(BF16)
-            return carry
-
-        lax.fori_loop(0, depth // step, some, 0)
+            clock.by(2.7)
 
     deep = stage.shape[1]
     saves = []
@@ -822,11 +1220,12 @@
         pairs = received.shape[0] // 2
         Exchange(Wire(core_send, core_recv), stage, received).run(
             [(tile_of(grad_gate), save_at(0), k) for k in range(pairs)]
-            + [(tile_of(grad_up), save_at(units), k) for k in range(pairs)]
+            + [(tile_of(grad_up), save_at(units), k) for k in range(pairs)],
+            lambda: clock.by(1.6),
         )
 
     wire = Wire(send_sem, recv_sem)
-    sums = scatter(peers, wire, part, slots, rows, make, weight_grads)
+    sums = scatter(peers, wire, part, slots, rows, make, weight_grads, lambda: clock.by(0.5))
     later[2].wait()
     gain_row = gain[...]
     half = rows // 2
@@ -847,13 +1246,14 @@
             return carry
 
         lax.fori_loop(0, half // 16, finish, 0)
+    clock.finish()
     wire.wait_sends()
     for copy in saves:
         copy.wait()
 
 
 def hidden_back(
-    slope_gate, slope_up, cot_all, gathered, state, cotangent, gain, w_down, w_gate, w_up
+    slope_gate, slope_up, cot_all, gathered, state, cotangent, gain, w_down, w_gate, w_up, grad_down
 ):
     n = lax.axis_size("tensor")
     pairs = lax.axis_size("dp") // 2
@@ -861,6 +1261,7 @@
     group, units = slope_gate.shape
     deep = depth // (2 * pairs)
     chunk = 512
+    landing, chip_scratch = chip_sum_shapes(pairs, units, grad_down.shape[1])
     return pl.pallas_call(
         hidden_back_kernel,
         out_shape=(
@@ -868,9 +1269,11 @@
             jax.ShapeDtypeStruct((rows, depth), BF16),
             jax.ShapeDtypeStruct((8, depth), F32),
             jax.ShapeDtypeStruct((pairs * deep, 2 * units), BF16),
+            landing,
+            jax.ShapeDtypeStruct((units, grad_down.shape[1]), BF16),
         ),
-        in_specs=[any_spec()] * 5 + [vmem_spec()] * 2 + [any_spec()] * 3,
-        out_specs=(vmem_spec(), vmem_spec(), vmem_spec(), any_spec()),
+        in_specs=[any_spec()] * 5 + [vmem_spec()] * 2 + [any_spec()] * 4,
+        out_specs=(vmem_spec(), vmem_spec(), vmem_spec(), any_spec(), any_spec(), any_spec()),
         scratch_shapes=[
             pltpu.VMEM((depth, units), BF16),
             pltpu.VMEM((depth, units), BF16),
@@ -886,22 +1289,26 @@
             pltpu.SemaphoreType.DMA((2 * pairs,)),
             pltpu.SemaphoreType.DMA((2 * pairs,)),
             pltpu.SemaphoreType.DMA((7 + 2 * (units // chunk) + 2 * pairs,)),
+            *chip_scratch,
         ],
         cost_estimate=pl.CostEstimate(
             flops=10 * group * depth * units, bytes_accessed=80 * 2**20, transcendentals=0
         ),
         compiler_params=params(4),
-    )(slope_gate, slope_up, cot_all, gathered, state, cotangent, gain, w_down, w_gate, w_up)
+    )(
+        slope_gate, slope_up, cot_all, gathered, state, cotangent, gain, w_down, w_gate, w_up,
+        grad_down,
+    )
 
 
 def attend_back_kernel(
     lengths, gain, grad_mixed, query_in, key_in, value_in, attended_in, log_in, cos_in, sin_in,
-    tokens_in, state_in, gathered_in, w_out, w_query, w_key, w_value,
-    grad_tokens_out, gain_out, grads_out,
+    tokens_in, state_in, gathered_in, w_out, w_query, w_key, w_value, grad_gate_up,
+    grad_tokens_out, gain_out, grads_out, total_gate_up,
     query, key, value, attended, log_total, cos_table, sin_table, tokens, grad_state,
     mixed, out_buf, query_buf, key_buf, value_buf, gathered, grad_att, key_acc, value_acc, grads, part, slots,
     stage_out, got_out, stage_qkv, got_qkv,
-    send_sem, recv_sem, sums_send, sums_recv, out_send, out_recv, qkv_send, qkv_recv, local_sem,
+    send_sem, recv_sem, sums_send, sums_recv, out_send, out_recv, qkv_send, qkv_recv, local_sem, *chip_scratch,
 ):
     peers = Peers()
     rows, depth = tokens.shape
@@ -924,7 +1331,10 @@
         local.copy(w_value, value_buf),
         local.copy(gathered_in, gathered),
     ]
-    greet(peers, core=True)
+    greet(peers, core=True, chips=True)
+    clock = Clock([NearChipSum(grad_gate_up, 0, chip_scratch, total_gate_up, 0.0, 108.0)])
+    clock.start()
+    clock.to(0.5)
     first_load.wait()
     ends, saves = ends_of(lengths), []
     gather_wire = Wire(send_sem, recv_sem)
@@ -933,6 +1343,7 @@
             load_out.wait()
         grad_rows = dot_nt(load_rows(mixed, spans), out_buf[...]).astype(BF16)
         store_rows(grad_att, spans, slice(None), grad_rows)
+        clock.to(1.0 + 12.0 * step)
 
     for load in loads:
         load.wait()
@@ -951,10 +1362,6 @@
                 pl.ds(k * columns, columns), pl.ds(width + c * columns, columns)
             ]
             saves.append(local.copy(ref.at[pl.ds(c * columns, columns)], target))
-
-    Exchange(Wire(out_send, out_recv), stage_out, got_out).run(
-        [(out_tile, out_save, k) for k in range(pairs)]
-    )
 
     key_acc[...] = jnp.zeros_like(key_acc)
     value_acc[...] = jnp.zeros_like(value_acc)
@@ -1002,6 +1409,7 @@
             return carry
 
         lax.fori_loop(0, q_width // LANES, one_pair, 0)
+        clock.by(2.1 * (i + 1))
 
     def fold(k, carry):
         at = pl.ds(pl.multiple_of(k * 128, 128), 128)
@@ -1033,6 +1441,7 @@
             total = total + dot_nt(grads[at, q_width : q_width + kv_raw], key_buf[inner, :])
             total = total + dot_nt(grads[at, q_width + kv_raw :], value_buf[inner, :])
             part[at, inner] = total.astype(BF16)
+            clock.by(1.2)
 
     deep = stage_qkv.shape[1]
 
@@ -1045,12 +1454,17 @@
         saves.append(local.copy(ref, target))
 
     def weight_grads():
+        Exchange(Wire(out_send, out_recv), stage_out, got_out).run(
+            [(out_tile, out_save, k) for k in range(pairs)], lambda: clock.by(0.5)
+        )
         Exchange(Wire(qkv_send, qkv_recv), stage_qkv, got_qkv).run(
-            [(qkv_tile, qkv_save, k) for k in range(pairs)]
+            [(qkv_tile, qkv_save, k) for k in range(pairs)], lambda: clock.by(0.9)
         )
 
     wire = Wire(sums_send, sums_recv)
-    sums = scatter(peers, wire, part, slots, rows, make, weight_grads)
+    sums = scatter(
+        peers, wire, part, slots, rows, make, tick=clock.at(66.0, 80.0, 90.0, 101.0), early=weight_grads
+    )
     gain_row = gain[...]
     half = rows // 2
     gain_out[...] = jnp.zeros_like(gain_out)
@@ -1068,6 +1482,7 @@
             return carry
 
         lax.fori_loop(0, half // 16, finish, 0)
+    clock.finish()
     gather_wire.wait_sends()
     wire.wait_sends()
     for copy in saves:
@@ -1076,7 +1491,7 @@
 
 def attend_back(
     lengths, grad_mixed, query, key, value, attended, log_total, cos_table, sin_table,
-    tokens, gain, grad_state, gathered, w_out, w_query, w_key, w_value,
+    tokens, gain, grad_state, gathered, w_out, w_query, w_key, w_value, grad_gate_up,
 ):
     n = lax.axis_size("tensor")
     pairs = lax.axis_size("dp") // 2
@@ -1086,15 +1501,18 @@
     width = q_width + 2 * kv_raw
     deep = depth // (2 * pairs)
     dma = lambda count: pltpu.SemaphoreType.DMA((count,))
+    early = deep - deep // 4
+    chip_scratch = near_chip_sum_scratch(pairs, early, grad_gate_up.shape[1])
     return pl.pallas_call(
         attend_back_kernel,
         out_shape=(
             jax.ShapeDtypeStruct((rows, depth), BF16),
             jax.ShapeDtypeStruct((8, depth), F32),
             jax.ShapeDtypeStruct((pairs * deep, width + q_width), BF16),
+            jax.ShapeDtypeStruct((early, grad_gate_up.shape[1]), BF16),
         ),
-        in_specs=[smem_spec(), vmem_spec()] + [any_spec()] * 15,
-        out_specs=(vmem_spec(), vmem_spec(), any_spec()),
+        in_specs=[smem_spec(), vmem_spec()] + [any_spec()] * 16,
+        out_specs=(vmem_spec(), vmem_spec(), any_spec(), any_spec()),
         scratch_shapes=[
             *[
                 pltpu.VMEM(source.shape, source.dtype)
@@ -1121,13 +1539,14 @@
             *wires(n),
             *wires(n),
             dma(pairs), dma(pairs), dma(pairs), dma(pairs), dma(15 + pairs * (1 + q_width // deep)),
+            *chip_scratch,
         ],
         cost_estimate=pl.CostEstimate(
             flops=2 * group * depth * q_width * 12, bytes_accessed=60 * 2**20, transcendentals=0
         ),
         compiler_params=params(5),
     )(lengths, gain, grad_mixed, query, key, value, attended, log_total, cos_table, sin_table,
-      tokens, grad_state, gathered, w_out, w_query, w_key, w_value)
+      tokens, grad_state, gathered, w_out, w_query, w_key, w_value, grad_gate_up)
 
 
 class GainSums:
@@ -1194,10 +1613,10 @@
 
 
 def output_kernel(
-    hidden_in, w_down, state, gain_one, gain_two,
-    output, gains_out,
+    hidden_in, w_down, state, gain_one, gain_two, grad_gate_up, grads,
+    output, gains_out, total_gate_up, total_grads,
     hidden, down_buf, part, slots, tiles, from_tensor, from_dp,
-    send_sem, recv_sem, gain_send, gain_recv, local_sem,
+    send_sem, recv_sem, gain_send, gain_recv, local_sem, *chip_scratch,
 ):
     peers = Peers()
     rows, depth = state.shape
@@ -1208,6 +1627,16 @@
         (gain_one, gain_two), tiles, from_tensor, from_dp, Wire(gain_send, gain_recv), chunk
     )
     gains.greet()
+    base = grad_gate_up.shape[0] // (lax.axis_size("dp") // 2) - total_gate_up.shape[0]
+    half = len(chip_scratch) // 2
+    clock = Clock(
+        [
+            NearChipSum(grad_gate_up, base, chip_scratch[:half], total_gate_up, 0.0, 36.0),
+            NearChipSum(grads, 0, chip_scratch[half:], total_grads, 36.0, 45.0),
+        ]
+    )
+    clock.start()
+    clock.to(0.5)
     gains.start()
     for load in loads:
         load.wait()
@@ -1216,15 +1645,14 @@
         at = pl.ds(pl.multiple_of(first * rows, rows), count * rows)
         step = 512
 
-        def some(k, carry):
-            lanes = pl.ds(pl.multiple_of(k * step, step), step)
+        for k in range(depth // step):
+            lanes = slice(k * step, (k + 1) * step)
             part[at, lanes] = dot_nn(hidden[at, :], down_buf[:, lanes]).astype(BF16)
-            return carry
-
-        lax.fori_loop(0, depth // step, some, 0)
+            clock.by(1.6)
 
     wire = Wire(send_sem, recv_sem)
-    sums = scatter(peers, wire, part, slots, rows, make, gains.forward)
+    ticks = clock.at(17.0, 29.0, 35.0, 47.0)
+    sums = scatter(peers, wire, part, slots, rows, make, gains.forward, ticks)
     half = rows // 2
     for h in range(2):
 
@@ -1239,22 +1667,29 @@
 
         lax.fori_loop(0, half // 16, finish, 0)
     gains.finish(gains_out)
+    clock.finish()
     wire.wait_sends()
     gains.wire.wait_sends()
 
 
-def layer_output(hidden, w_down, state, gain_one, gain_two):
+def layer_output(hidden, w_down, state, gain_one, gain_two, grad_gate_up, grads):
     n, dps = lax.axis_size("tensor"), lax.axis_size("dp")
     rows, depth = state.shape
     dma = lambda count: pltpu.SemaphoreType.DMA((count,))
+    pairs = dps // 2
+    deep = grads.shape[0] // pairs
+    scratch_a = near_chip_sum_scratch(pairs, deep // 4, grad_gate_up.shape[1])
+    scratch_b = near_chip_sum_scratch(pairs, deep, grads.shape[1])
     return pl.pallas_call(
         output_kernel,
         out_shape=(
             jax.ShapeDtypeStruct((rows, depth), BF16),
             jax.ShapeDtypeStruct((2, 8, LANES), F32),
+            jax.ShapeDtypeStruct((deep // 4, grad_gate_up.shape[1]), BF16),
+            jax.ShapeDtypeStruct((deep, grads.shape[1]), BF16),
         ),
-        in_specs=[any_spec(), any_spec(), vmem_spec(), vmem_spec(), vmem_spec()],
-        out_specs=(vmem_spec(), vmem_spec()),
+        in_specs=[any_spec()] * 2 + [vmem_spec()] * 3 + [any_spec()] * 2,
+        out_specs=(vmem_spec(), vmem_spec()) + (any_spec(),) * 2,
         scratch_shapes=[
             pltpu.VMEM(hidden.shape, BF16),
             pltpu.VMEM(w_down.shape, BF16),
@@ -1265,6 +1700,8 @@
             pltpu.VMEM((dps - 1, 2, 8, LANES), F32),
             *wires(n),
             dma(n + dps - 2), dma(n + dps - 2), dma(2),
+            *scratch_a,
+            *scratch_b,
         ],
         cost_estimate=pl.CostEstimate(
             flops=2 * hidden.shape[0] * depth * hidden.shape[1],
@@ -1272,40 +1709,72 @@
             transcendentals=0,
         ),
         compiler_params=params(6),
-    )(hidden, w_down, state, gain_one, gain_two)
-
-
-def unpack_kernel(packed, grad_query, grad_key, grad_value, grad_out):
+    )(hidden, w_down, state, gain_one, gain_two, grad_gate_up, grads)
+
+
+def unpack_kernel(
+    down, gate_up_a, gate_up_b, packed, output_in, tokens_in,
+    grad_down, grad_gate, grad_up, grad_query, grad_key, grad_value, grad_out, output, grad_tokens,
+):
+    output[...] = output_in[...]
+    grad_tokens[...] = tokens_in[...]
+    grad_down[...] = down[...].astype(F32)
+    units = grad_gate.shape[1]
+    last = pl.num_programs(0) - 1
+
+    @pl.when(pl.program_id(0) < last)
+    def _():
+        grad_gate[...] = gate_up_a[:, :units].astype(F32)
+        grad_up[...] = gate_up_a[:, units:].astype(F32)
+
+    @pl.when(pl.program_id(0) == last)
+    def _():
+        grad_gate[...] = gate_up_b[:, :units].astype(F32)
+        grad_up[...] = gate_up_b[:, units:].astype(F32)
+
     first = 0
     for target in (grad_query, grad_key, grad_value):
         width = target.shape[1]
         target[...] = packed[:, first : first + width].astype(F32)
         first += width
-    deep = packed.shape[0]
-    for c in range(grad_out.shape[0] // deep):
-        at = slice(c * deep, (c + 1) * deep)
-        grad_out[at, :] = packed[:, first + c * deep : first + (c + 1) * deep].astype(F32)
-
-
-def unpack(packed, q_width, kv_raw):
-    deep = packed.shape[0]
-    return pl.pallas_call(
+    deep = grad_out.shape[2]
+    for c in range(grad_out.shape[0]):
+        grad_out[c] = packed[:, first + c * deep : first + (c + 1) * deep].astype(F32)
+
+
+def unpack(down, gate_up_a, gate_up_b, packed, output, tokens, q_width, kv_raw):
+    deep, units = packed.shape[0], gate_up_a.shape[1] // 2
+    steps = 4
+    rows = lambda array: (array[0] // steps, array[1])
+    spec = lambda array: pl.BlockSpec(rows(array), lambda i: (i, 0))
+    early = pl.BlockSpec((deep // steps, 2 * units), lambda i: (jnp.minimum(i, steps - 2), 0))
+    late = pl.BlockSpec((deep // steps, 2 * units), lambda i: (0, 0))
+    flat = (
+        (down.shape, F32), ((deep, units), F32), ((deep, units), F32),
+        ((deep, q_width), F32), ((deep, kv_raw), F32), ((deep, kv_raw), F32),
+    )
+    pieces = q_width // deep
+    *grads, grad_out, output, tokens = pl.pallas_call(
         unpack_kernel,
+        grid=(steps,),
         out_shape=(
-            jax.ShapeDtypeStruct((deep, q_width), F32),
-            jax.ShapeDtypeStruct((deep, kv_raw), F32),
-            jax.ShapeDtypeStruct((deep, kv_raw), F32),
-            jax.ShapeDtypeStruct((q_width, deep), F32),
+            *[jax.ShapeDtypeStruct(shape, kind) for shape, kind in flat],
+            jax.ShapeDtypeStruct((pieces, deep, deep), F32),
+            jax.ShapeDtypeStruct(output.shape, BF16),
+            jax.ShapeDtypeStruct(tokens.shape, BF16),
         ),
-    )(packed)
-
-
-def sum_over_chips(grads):
-    size = lax.axis_size("dp")
-    groups = [list(range(core, size, 2)) for core in range(2)]
-    return lax.psum_scatter(
-        grads, "dp", scatter_dimension=0, tiled=True, axis_index_groups=groups
-    )
+        in_specs=[
+            spec(down.shape), early, late, spec(packed.shape), spec(output.shape),
+            spec(tokens.shape),
+        ],
+        out_specs=(
+            *[spec(shape) for shape, _ in flat],
+            pl.BlockSpec((pieces, deep // steps, deep), lambda i: (0, i, 0)),
+            spec(output.shape),
+            spec(tokens.shape),
+        ),
+    )(down, gate_up_a, gate_up_b, packed, output, tokens)
+    return *grads, grad_out.reshape(q_width, deep), output, tokens
 
 
 def local(
@@ -1313,7 +1782,6 @@
     cotangent,
 ):
     depth = tokens.shape[1]
-    q_width, kv_raw, units = w_query.shape[1], w_key.shape[1], w_gate.shape[1]
     gain_one, gain_two = gain_one[None], gain_two[None]
     gathered_one, query, key, value, cos_table, sin_table = project(
         lengths, tokens, gain_one, w_query, w_key, w_value
@@ -1324,38 +1792,32 @@
     gathered_two, hidden, slope_gate, slope_up, cot_all, grad_down = hidden_units(
         normed_two, cotangent, cot_a, cot_b, w_gate, w_up
     )
-    grad_w_down = sum_over_chips(grad_down)
-    grad_state, grad_mixed, gain_two_part, grad_gate_up = hidden_back(
+    grad_state, grad_mixed, gain_two_part, grad_gate_up, _, total_down = hidden_back(
         slope_gate, slope_up, cot_all, gathered_two, state, cotangent, gain_two,
-        w_down, w_gate, w_up,
-    )
-    grad_gate_up, grad_w_down = lax.optimization_barrier((grad_gate_up, grad_w_down))
-    grad_w_gate_up = sum_over_chips(grad_gate_up)
-    grad_tokens, gain_one_part, grads = attend_back(
+        w_down, w_gate, w_up, grad_down,
+    )
+    grad_tokens, gain_one_part, grads, gate_up_a = attend_back(
         lengths, grad_mixed, query, key, value, attended, log_total, cos_table, sin_table,
-        tokens, gain_one, grad_state, gathered_one, w_out, w_query, w_key, w_value,
-    )
-    grads, grad_w_gate_up = lax.optimization_barrier((grads, grad_w_gate_up))
-    grads = sum_over_chips(grads)
-    grad_w_query, grad_w_key, grad_w_value, grad_w_out = unpack(grads, q_width, kv_raw)
-    output, gains = layer_output(hidden, w_down, state, gain_one_part, gain_two_part)
+        tokens, gain_one, grad_state, gathered_one, w_out, w_query, w_key, w_value, grad_gate_up,
+    )
+    output, gains, gate_up_b, packed = layer_output(
+        hidden, w_down, state, gain_one_part, gain_two_part, grad_gate_up, grads
+    )
     share = depth // (lax.axis_size("tensor") * lax.axis_size("dp"))
     place = lax.rem(
         (lax.axis_index("dp") * lax.axis_size("tensor") + lax.axis_index("tensor")) * share, LANES
     )
     gains = lax.dynamic_slice_in_dim(jnp.sum(gains, axis=1), place, share, axis=1)
+    (
+        grad_w_down, grad_w_gate, grad_w_up, grad_w_query, grad_w_key, grad_w_value, grad_w_out,
+        output, grad_tokens,
+    ) = unpack(
+        total_down, gate_up_a, gate_up_b, packed, output, grad_tokens,
+        w_query.shape[1], w_key.shape[1],
+    )
     return (
-        output,
-        grad_tokens,
-        gains[0],
-        grad_w_query,
-        grad_w_key,
-        grad_w_value,
-        grad_w_out,
-        gains[1],
-        grad_w_gate_up[:, :units].astype(F32),
-        grad_w_gate_up[:, units:].astype(F32),
-        grad_w_down.astype(F32),
+        output, grad_tokens, gains[0], grad_w_query, grad_w_key, grad_w_value, grad_w_out,
+        gains[1], grad_w_gate, grad_w_up, grad_w_down,
     )
 
 

time: 485 us -> 478 us (0.986)
  Pallas kernels: 415 us -> 468 us
  waiting for transfers between devices: 40.5 us -> 0 us
  between operations: 14.3 us -> 0.95 us
  other arithmetic: 4.88 us -> 0.02 us
    pallas_call x1, Pallas kernels: 49 us -> 89.6 us  [layer_output(): pl.pallas_call(output_kernel, out_shape=(jax.ShapeDtypeStruct((rows, dept...]
    reduce_scatter x3 -> x0, waiting for transfers between devices: 40.5 us -> none  [sum_over_chips(): lax.psum_scatter(grads, 'dp', scatter_dimension=0, tiled=True, axis_index...]
  transfers between devices with their start and end apart: 3 -> 0, of which waited for: 3 -> 0; matrix products, arithmetic and copies ran while one was open for 1% -> 0% of each run, Pallas kernels for 49% -> 0%
where the time goes in v3:
time: 478 us; the launch traced here: 470 us
  Pallas kernels  468 us (98%)
    pallas_call x1, Pallas kernels, attend_back(): pl.pallas_call(attend_back_kernel, out_shape=(jax.ShapeDtypeStruct((rows,...  117 us
    pallas_call x1, Pallas kernels, layer_output(): pl.pallas_call(output_kernel, out_shape=(jax.ShapeDtypeStruct((rows, dept...  89.6 us
    pallas_call x1, Pallas kernels, hidden_back(): pl.pallas_call(hidden_back_kernel, out_shape=(jax.ShapeDtypeStruct((rows,...  77.1 us
    pallas_call x1, Pallas kernels, hidden_units(): pl.pallas_call(hidden_kernel, out_shape=(wide(depth), wide(units), wide(u...  72.8 us
    pallas_call x1, Pallas kernels, attend(): pl.pallas_call(attend_kernel, out_shape=(jax.ShapeDtypeStruct((group, q_w...  57.8 us
    pallas_call x1, Pallas kernels, project(): pl.pallas_call(project_kernel, out_shape=(jax.ShapeDtypeStruct((group, de...  47.1 us

profile of v3, /device:TPU:0, one launch (start us, length us, event | category | flops | bytes accessed | tf_op | source)
XLA Modules:
  0.0 469.7 jit_solution(12218884828680863484)
XLA Ops:
  0.6 47.1 %shard_map.221 = (bf16[1024,2048]{1,0:T(8,128)(2,1)}, bf16[1024,512]{1,0:T(8,128)(2,1)}, bf16[1024,256]{1,0:T(8,128)(2,1)}, bf16[1024,256]{1,0:T(8,128)(2,1)}, f32[1024,128]{1,0:T(8,128)}, /*index=5*/f32[1024,128]{1,0:T(8,128)}) custom-call(s32[1,3]{1,0:T(1,128)} %lengths.5, bf16[256,2048]{1,0:T(8,128)(2,1)} %tokens_in.3, f32[1,2048]{1,0:T(1,128)} %bitcast.10, ...), custom_call_target="tpu_custom_call" | custom-call | flops 4294967296 | bytes 41943040 | tf_op jit(solution)/shard_map/pallas_call | solution.py:786
  47.7 57.8 %shard_map.222 = (bf16[1024,512]{1,0:T(8,128)(2,1)}, f32[1024,128]{1,0:T(8,128)}, f32[256,2048]{1,0:T(8,128)}, bf16[256,2048]{1,0:T(8,128)(2,1)}, bf16[1,128,204...) custom-call(s32[1,3]{1,0:T(1,128)} %lengths.5, bf16[1024,512]{1,0:T(8,128)(2,1)} %get-tuple-element.51.query.query_in, ...), custom_call_target="tpu_custom_call" | custom-call | flops 8589934592 | bytes 41943040 | tf_op jit(solution)/shard_map/pallas_call | solution.py:910
  105.5 72.8 %shard_map.223 = (bf16[1024,2048]{1,0:T(8,128)(2,1)}, bf16[1024,2048]{1,0:T(8,128)(2,1)}, bf16[1024,2048]{1,0:T(8,128)(2,1)}, bf16[1024,2048]{1,0:T(8,128)(2,1)}...) custom-call(bf16[256,2048]{1,0:T(8,128)(2,1)} %get-tuple-element.54.normed, bf16[256,2048]{1,0:T(8,128)(2,1)} %cotangent.5, ...), custom_call_target="tpu_custom_call" | custom-call | flops 25769803776 | bytes 62914560 | tf_op jit(solution)/shard_map/pallas_call | solution.py:1087
  178.3 77.1 %shard_map.224 = (f32[256,2048]{1,0:T(8,128)}, bf16[256,2048]{1,0:T(8,128)(2,1)}, f32[8,2048]{1,0:T(8,128)}, bf16[1024,4096]{1,0:T(8,128)(2,1)}, bf16[2,3,2048,2...) custom-call(bf16[1024,2048]{1,0:T(8,128)(2,1)} %get-tuple-element.57.slope_gate, ...), custom_call_target="tpu_custom_call" | custom-call | flops 42949672960 | bytes 83886080 | tf_op jit(solution)/shard_map/pallas_call | solution.py:1265
  255.5 116.7 %shard_map.225 = (bf16[256,2048]{1,0:T(8,128)(2,1)}, f32[8,2048]{1,0:T(8,128)}, bf16[1024,1280]{1,0:T(8,128)(2,1)}, bf16[192,4096]{1,0:T(8,128)(2,1)}) custom-call(s32[1,3]{1,0:T(1,128)} %lengths.5, f32[1,2048]{1,0:T(1,128)} %bitcast.11, bf16[256,2048]{1,0:T(8,128)(2,1)} %get-tuple-element.64.grad_mixed, bf16[1024,512]{1,0:T(8,128)(2,1)} %get-tuple-element.51.query.query_in, ...), custom_call_target="tpu_custom_call" | custom-call | flops 25769803776 | bytes 62914560 | tf_op jit(solution)/shard_map/pallas_call | solution.py:1506
  372.3 89.6 %shard_map.226 = (bf16[256,2048]{1,0:T(8,128)(2,1)}, f32[2,8,128]{2,1,0:T(8,128)}, bf16[64,4096]{1,0:T(8,128)(2,1)}, bf16[256,1280]{1,0:T(8,128)(2,1)}) custom-call(bf16[1024,2048]{1,0:T(8,128)(2,1)} %get-tuple-element.73.hidden_in, bf16[2048,2048]{1,0:T(8,128)(2,1)} %w_down.3, f32[256,2048]{1,0:T(8,128)} %get-tuple-element.61.state, ...), custom_call_target="tpu_custom_call" | custom-call | flops 8589934592 | bytes 20971520 | tf_op jit(solution)/shard_map/pallas_call | solution.py:1683
  461.8 0.0 copy-start
  461.8 7.0 %shard_map.227 = (f32[2048,256]{1,0:T(8,128)}, f32[256,2048]{1,0:T(8,128)}, f32[256,2048]{1,0:T(8,128)}, f32[256,512]{1,0:T(8,128)}, f32[256,128]{1,0:T(8,128)},...) custom-call(bf16[2048,256]{1,0:T(8,128)(2,1)} %get-tuple-element.63.down, ...), custom_call_target="tpu_custom_call" | custom-call | tf_op jit(solution)/shard_map/pallas_call | solution.py:1757
  468.8 0.0 copy-done
  468.8 0.1 constant_dynamic-slice_fusion
  468.9 0.5 slice_bitcast_fusion
  (1 shorter events, 0.0 us)
Async XLA Ops:
  461.8 7.0 %copy-start = (f32[2,8,128]{2,1,0:T(8,128)S(1)}, f32[2,8,128]{2,1,0:T(8,128)}, u32[]{:S(2)}) copy-start(f32[2,8,128]{2,1,0:T(8,128)} %get-tuple-element.83) | copy-start | bytes 24580

commit v4 on v3

--- a/solution.py
+++ b/solution.py
@@ -207,15 +207,19 @@
 
 
 def add_rows(target, others, size):
+    step = 16
+    while step * target.shape[1] < 32768 and size % (2 * step) == 0:
+        step *= 2
+
     def some(k, carry):
-        at = pl.ds(pl.multiple_of(k * 16, 16), 16)
+        at = pl.ds(pl.multiple_of(k * step, step), step)
         total = target[at, :].astype(F32)
         for other in others:
             total = total + other[at, :].astype(F32)
         target[at, :] = total.astype(target.dtype)
         return carry
 
-    lax.fori_loop(0, size // 16, some, 0)
+    lax.fori_loop(0, size // step, some, 0)
 
 
 def scatter(peers, wire, part_ref, slots, rows, make, meanwhile=None, tick=lambda: None, early=None):
@@ -317,7 +321,9 @@
             for rank in range(self.size - 1 - hop):
                 for c in range(self.chunks):
                     order = rank * self.chunks + c
-                    due = first if hop == 0 else first + step * (order + hop) + 3.0 * hop
+                    due = first + step * (order + hop) + 3.0 * hop
+                    if hop == 0:
+                        due = first + step * self.chunks * rank - MARGIN
                     events.append((due, hop, rank, c))
         for c in range(self.chunks):
             due = first + span - step * (self.chunks - 1 - c) + 3.0
@@ -683,10 +689,12 @@
     )
 
 
-def project_kernel(
-    lengths, tokens, gain, cos_place, sin_place, w_query, w_key, w_value,
+def front_kernel(
+    lengths, tokens, gain, gain_two, cos_place, sin_place, w_query, w_key, w_value, w_out, cotangent,
     gathered_out, query_out, key_out, value_out, cos_out, sin_out,
-    gathered, weights, raw_key, raw_value, send_sem, recv_sem, local_sem,
+    attended_out, log_out, state_out, normed_out, cot_minor, cot_major,
+    gathered, weights, raw_key, raw_value, query, key, value, w_buf, attended, log_total, part, slots,
+    send_sem, recv_sem, sums_send, sums_recv, cot_send, cot_recv, local_sem,
 ):
     peers = Peers()
     rows, depth = tokens.shape
@@ -694,6 +702,7 @@
     q_width, kv_heads = w_query.shape[1], w_key.shape[1] // HD
     kv_width = kv_heads * LANES
     local = Local(local_sem)
+    load_out = local.copy(w_out, w_buf)
     loads = [
         local.copy(w_key, raw_key),
         local.copy(w_value, raw_value),
@@ -736,18 +745,31 @@
 
         lax.fori_loop(0, depth // 128, some, 0)
 
-    wire = Wire(send_sem, recv_sem)
-    for step, spans in enumerate(gather(peers, wire, gathered, rows)):
+    cot_wire = Wire(cot_send, cot_recv)
+
+    def send_cotangent():
+        part = lambda half: half_block(cotangent, 0, rows, half)
+        landed = lambda ref, half: half_block(ref, 0, rows, half)
+        for k, j in enumerate(peers.steps()):
+            cot_wire.copy(part(0), landed(cot_minor.at[k], 0), peers.minor(j))
+        cot_wire.copy(part(1), landed(cot_major, 1), peers.major())
+        for k, j in enumerate(peers.steps()):
+            cot_wire.copy(part(1), landed(cot_minor.at[k], 1), peers.minor(j))
+        cot_wire.copy(part(0), landed(cot_major, 0), peers.major())
+
+    gather_wire = Wire(send_sem, recv_sem)
+    for step, spans in enumerate(gather(peers, gather_wire, gathered, rows)):
         if step == 0:
             prepare()
         if step == 3:
-            save = local.copy(gathered, gathered_out)
+            saves = [local.copy(gathered, gathered_out)]
+            send_cotangent()
         cos, sin = load_rows(cos_out, spans), load_rows(sin_out, spans)
         normed = load_rows(gathered, spans)
         for base, width, out, turned in (
-            (0, q_width, query_out, True),
-            (q_width, kv_width, key_out, True),
-            (q_width + kv_width, kv_width, value_out, False),
+            (0, q_width, query, True),
+            (q_width, kv_width, key, True),
+            (q_width + kv_width, kv_width, value, False),
         ):
             raw = dot_nn(normed, weights[:, base : base + width])
             for c in range(0, width, LANES):
@@ -755,83 +777,10 @@
                 if turned:
                     piece = piece * cos + swap_halves(piece) * sin
                 store_rows(out, spans, slice(c, c + LANES), piece.astype(BF16))
-    wire.wait_sends()
-    save.wait()
-
-
-def any_spec():
-    return pl.BlockSpec(memory_space=pl.ANY)
-
-
-def vmem_spec():
-    return pl.BlockSpec(memory_space=pltpu.VMEM)
-
-
-def params(collective_id):
-    return pltpu.CompilerParams(
-        collective_id=collective_id, has_side_effects=True, vmem_limit_bytes=VMEM_LIMIT
-    )
-
-
-def smem_spec():
-    return pl.BlockSpec(memory_space=pltpu.SMEM)
-
-
-def project(lengths, tokens, gain, w_query, w_key, w_value):
-    n = lax.axis_size("tensor")
-    rows, depth = tokens.shape
-    group = rows * n
-    q_width, kv_raw = w_query.shape[1], w_key.shape[1]
-    kv_width = kv_raw // HD * LANES
-    return pl.pallas_call(
-        project_kernel,
-        out_shape=(
-            jax.ShapeDtypeStruct((group, depth), BF16),
-            jax.ShapeDtypeStruct((group, q_width), BF16),
-            jax.ShapeDtypeStruct((group, kv_width), BF16),
-            jax.ShapeDtypeStruct((group, kv_width), BF16),
-            jax.ShapeDtypeStruct((group, LANES), F32),
-            jax.ShapeDtypeStruct((group, LANES), F32),
-        ),
-        in_specs=[smem_spec()] + [vmem_spec()] * 4 + [any_spec()] * 3,
-        out_specs=(any_spec(),) + (vmem_spec(),) * 5,
-        scratch_shapes=[
-            pltpu.VMEM((group, depth), BF16),
-            pltpu.VMEM((depth, q_width + 2 * kv_width), BF16),
-            pltpu.VMEM((depth, kv_raw), BF16),
-            pltpu.VMEM((depth, kv_raw), BF16),
-            *wires(n),
-            pltpu.SemaphoreType.DMA((4,)),
-        ],
-        cost_estimate=pl.CostEstimate(
-            flops=2 * group * depth * (q_width + 2 * kv_width),
-            bytes_accessed=40 * 2**20,
-            transcendentals=0,
-        ),
-        compiler_params=params(1),
-    )(lengths, tokens, gain, *place_tables(group), w_query, w_key, w_value)
-
-
-def attend_kernel(
-    lengths, query, key, value, gain, tokens_in, w_out, cotangent,
-    attended_out, log_out, state_out, normed_out, cot_a, cot_b,
-    tokens, w_buf, attended, log_total, part, slots,
-    send_sem, recv_sem, cot_send, cot_recv, local_sem,
-):
-    peers = Peers()
-    rows, depth = tokens.shape
-    group, q_width = query.shape
-    pairs_per_kv = q_width // LANES // (key.shape[1] // LANES)
+    saves += [local.copy(query, query_out), local.copy(key, key_out), local.copy(value, value_out)]
     ends = ends_of(lengths)
-    local = Local(local_sem)
-    loads = [local.copy(w_out, w_buf), local.copy(tokens_in, tokens)]
-    greet(peers)
+    pairs_per_kv = q_width // LANES // kv_heads
     log_total[...] = jnp.zeros_like(log_total)
-    cot_wire = Wire(cot_send, cot_recv)
-    for k, j in enumerate(peers.steps()):
-        cot_wire.copy(half_block(cotangent, 0, rows, 0), cot_a.at[k], peers.minor(j))
-    cot_wire.copy(half_block(cotangent, 0, rows, 1), cot_b, peers.major())
-
     tile = 256
     for i in range(group // tile):
         keys = (i + 1) * tile
@@ -868,9 +817,8 @@
 
         lax.fori_loop(0, q_width // LANES, one_pair, 0)
 
-    saves = [local.copy(attended, attended_out), local.copy(log_total, log_out)]
-    for load in loads:
-        load.wait()
+    saves += [local.copy(attended, attended_out), local.copy(log_total, log_out)]
+    load_out.wait()
 
     def make(first, count):
         at = pl.ds(pl.multiple_of(first * rows, rows), count * rows)
@@ -878,9 +826,9 @@
         for c in range(0, depth, 1024):
             part[at, c : c + 1024] = dot_nn(heads, w_buf[:, c : c + 1024]).astype(BF16)
 
-    wire = Wire(send_sem, recv_sem)
+    wire = Wire(sums_send, sums_recv)
     sums = scatter(peers, wire, part, slots, rows, make)
-    gain_row = gain[...]
+    gain_row = gain_two[...]
     half = rows // 2
     for h in range(2):
 
@@ -897,45 +845,85 @@
             return carry
 
         lax.fori_loop(0, half // 16, finish, 0)
+    gather_wire.wait_sends()
     wire.wait_sends()
     for copy in (*cot_wire.copies, *saves):
         copy.wait()
 
 
-def attend(lengths, query, key, value, tokens, gain, w_out, cotangent):
+def any_spec():
+    return pl.BlockSpec(memory_space=pl.ANY)
+
+
+def vmem_spec():
+    return pl.BlockSpec(memory_space=pltpu.VMEM)
+
+
+def params(collective_id):
+    return pltpu.CompilerParams(
+        collective_id=collective_id, has_side_effects=True, vmem_limit_bytes=VMEM_LIMIT
+    )
+
+
+def smem_spec():
+    return pl.BlockSpec(memory_space=pltpu.SMEM)
+
+
+def front(lengths, tokens, gain, gain_two, w_query, w_key, w_value, w_out, cotangent):
     n = lax.axis_size("tensor")
+    m = n // 2
     rows, depth = tokens.shape
-    group, q_width = query.shape
-    m = n // 2
+    group = rows * n
+    q_width, kv_raw = w_query.shape[1], w_key.shape[1]
+    kv_width = kv_raw // HD * LANES
+    heads = [(group, q_width), (group, kv_width), (group, kv_width)]
+    low = lambda *shape: jax.ShapeDtypeStruct(shape, BF16)
     return pl.pallas_call(
-        attend_kernel,
+        front_kernel,
         out_shape=(
-            jax.ShapeDtypeStruct((group, q_width), BF16),
+            low(group, depth),
+            *[low(*shape) for shape in heads],
+            jax.ShapeDtypeStruct((group, LANES), F32),
+            jax.ShapeDtypeStruct((group, LANES), F32),
+            low(group, q_width),
             jax.ShapeDtypeStruct((group, LANES), F32),
             jax.ShapeDtypeStruct((rows, depth), F32),
-            jax.ShapeDtypeStruct((rows, depth), BF16),
-            jax.ShapeDtypeStruct((m - 1, rows // 2, depth), BF16),
-            jax.ShapeDtypeStruct((rows // 2, depth), BF16),
+            low(rows, depth),
+            low(m - 1, rows, depth),
+            low(rows, depth),
         ),
-        in_specs=[smem_spec()] + [vmem_spec()] * 4 + [any_spec()] * 3,
-        out_specs=(any_spec(), any_spec(), vmem_spec(), vmem_spec(), any_spec(), any_spec()),
+        in_specs=[smem_spec()] + [vmem_spec()] * 5 + [any_spec()] * 5,
+        out_specs=(
+            *[any_spec()] * 4, vmem_spec(), vmem_spec(), any_spec(), any_spec(),
+            vmem_spec(), vmem_spec(), any_spec(), any_spec(),
+        ),
         scratch_shapes=[
-            pltpu.VMEM((rows, depth), BF16),
+            pltpu.VMEM((group, depth), BF16),
+            pltpu.VMEM((depth, q_width + 2 * kv_width), BF16),
+            pltpu.VMEM((depth, kv_raw), BF16),
+            pltpu.VMEM((depth, kv_raw), BF16),
+            *[pltpu.VMEM(shape, BF16) for shape in heads],
             pltpu.VMEM(w_out.shape, BF16),
             pltpu.VMEM((group, q_width), BF16),
             pltpu.VMEM((group, LANES), F32),
             pltpu.VMEM((group, depth), BF16),
             slots_for(n, rows, depth),
             *wires(n),
-            pltpu.SemaphoreType.DMA((m,)),
-            pltpu.SemaphoreType.DMA((m,)),
-            pltpu.SemaphoreType.DMA((4,)),
+            *wires(n),
+            pltpu.SemaphoreType.DMA((2 * m,)),
+            pltpu.SemaphoreType.DMA((2 * m,)),
+            pltpu.SemaphoreType.DMA((10,)),
         ],
         cost_estimate=pl.CostEstimate(
-            flops=2 * group * depth * q_width * 4, bytes_accessed=40 * 2**20, transcendentals=0
+            flops=2 * group * depth * (2 * q_width + 2 * kv_width),
+            bytes_accessed=60 * 2**20,
+            transcendentals=0,
         ),
-        compiler_params=params(2),
-    )(lengths, query, key, value, gain, tokens, w_out, cotangent)
+        compiler_params=params(1),
+    )(
+        lengths, tokens, gain, gain_two, *place_tables(group), w_query, w_key, w_value, w_out,
+        cotangent,
+    )
 
 
 class Exchange:
@@ -971,7 +959,7 @@
 
 
 def hidden_kernel(
-    normed, cotangent, cot_a, cot_b, w_gate, w_up,
+    normed, cotangent, cot_minor, cot_major, w_gate, w_up,
     gathered_out, hidden_out, slope_gate_out, slope_up_out, cot_out, grad_down_out,
     gathered, gate_buf, up_buf, hidden, slope_gate, slope_up, cot, stage, received,
     send_sem, recv_sem, cot_send, cot_recv, core_send, core_recv, local_sem,
@@ -985,8 +973,8 @@
     loads = [local.copy(w_gate, gate_buf), local.copy(w_up, up_buf)]
     cot_loads = [local.copy(cotangent, block(cot, me, rows))]
     for k, j in enumerate(peers.steps()):
-        cot_loads.append(local.copy(cot_a.at[k], half_block(cot, peers.at(0, -j), rows, 0)))
-    cot_loads.append(local.copy(cot_b, half_block(cot, major, rows, 1)))
+        cot_loads.append(local.copy(cot_minor.at[k], block(cot, peers.at(0, -j), rows)))
+    cot_loads.append(local.copy(cot_major, block(cot, major, rows)))
     greet(peers, core=True)
     first_load.wait()
 
@@ -1023,9 +1011,7 @@
                 rest[side].append(cot_wire.copy(ref, ref, device))
 
             for j in peers.steps():
-                send(me, 1, peers.minor(j))
                 send(major, 1, peers.minor(j))
-            send(me, 0, peers.major())
             for j in peers.steps():
                 send(peers.at(0, -j), 0, peers.major())
 
@@ -1078,7 +1064,7 @@
         copy.wait()
 
 
-def hidden_units(normed, cotangent, cot_a, cot_b, w_gate, w_up):
+def hidden_units(normed, cotangent, cot_minor, cot_major, w_gate, w_up):
     n = lax.axis_size("tensor")
     pairs = lax.axis_size("dp") // 2
     rows, depth = normed.shape
@@ -1113,7 +1099,7 @@
             flops=6 * group * depth * units, bytes_accessed=60 * 2**20, transcendentals=0
         ),
         compiler_params=params(3),
-    )(normed, cotangent, cot_a, cot_b, w_gate, w_up)
+    )(normed, cotangent, cot_minor, cot_major, w_gate, w_up)
 
 
 def norm_back(values, gain_row, grad_normed):
@@ -1150,7 +1136,7 @@
     slopes = [local.copy(slope_gate, grad_gate), local.copy(slope_up, grad_up)]
     downs.append(load_down(1))
     greet(peers, core=True, chips=True)
-    clock = Clock([ChipSum(grad_down, 0, chip_scratch, landing, total_down, 0.0, 72.0)])
+    clock = Clock([ChipSum(grad_down, 0, chip_scratch, landing, total_down, 4.0, 72.0)])
     clock.to(1.0)
     later = []
 
@@ -1783,14 +1769,14 @@
 ):
     depth = tokens.shape[1]
     gain_one, gain_two = gain_one[None], gain_two[None]
-    gathered_one, query, key, value, cos_table, sin_table = project(
-        lengths, tokens, gain_one, w_query, w_key, w_value
-    )
-    attended, log_total, state, normed_two, cot_a, cot_b = attend(
-        lengths, query, key, value, tokens, gain_two, w_out, cotangent
+    (
+        gathered_one, query, key, value, cos_table, sin_table, attended, log_total, state, normed_two,
+        cot_minor, cot_major,
+    ) = front(
+        lengths, tokens, gain_one, gain_two, w_query, w_key, w_value, w_out, cotangent
     )
     gathered_two, hidden, slope_gate, slope_up, cot_all, grad_down = hidden_units(
-        normed_two, cotangent, cot_a, cot_b, w_gate, w_up
+        normed_two, cotangent, cot_minor, cot_major, w_gate, w_up
     )
     grad_state, grad_mixed, gain_two_part, grad_gate_up, _, total_down = hidden_back(
         slope_gate, slope_up, cot_all, gathered_two, state, cotangent, gain_two,

time: 478 us -> 465 us (0.973)
  Pallas kernels: 468 us -> 454 us
    pallas_call x1, Pallas kernels: 72.8 us -> 65.2 us  [hidden_units(): pl.pallas_call(hidden_kernel, out_shape=(wide(depth), wide(units), wide(u...]
    pallas_call x2 -> x1, Pallas kernels: 105 us -> 103 us  [front(): pl.pallas_call(front_kernel, out_shape=(low(group, depth), *[low(*shape)...]
where the time goes in v4:
time: 465 us; the launch traced here: 456 us
  Pallas kernels  454 us (98%)
    pallas_call x1, Pallas kernels, attend_back(): pl.pallas_call(attend_back_kernel, out_shape=(jax.ShapeDtypeStruct((rows,...  112 us
    pallas_call x1, Pallas kernels, front(): pl.pallas_call(front_kernel, out_shape=(low(group, depth), *[low(*shape)...  103 us
    pallas_call x1, Pallas kernels, layer_output(): pl.pallas_call(output_kernel, out_shape=(jax.ShapeDtypeStruct((rows, dept...  89.2 us
    pallas_call x1, Pallas kernels, hidden_back(): pl.pallas_call(hidden_back_kernel, out_shape=(jax.ShapeDtypeStruct((rows,...  77.4 us
    pallas_call x1, Pallas kernels, hidden_units(): pl.pallas_call(hidden_kernel, out_shape=(wide(depth), wide(units), wide(u...  65.2 us

profile of v4, /device:TPU:0, one launch (start us, length us, event | category | flops | bytes accessed | tf_op | source)
XLA Modules:
  0.0 455.9 jit_solution(12264047877606400617)
XLA Ops:
  0.6 103.4 %shard_map.221 = (bf16[1024,2048]{1,0:T(8,128)(2,1)}, bf16[1024,512]{1,0:T(8,128)(2,1)}, bf16[1024,256]{1,0:T(8,128)(2,1)}, bf16[1024,256]{1,0:T(8,128)(2,1)}, f...) custom-call(s32[1,3]{1,0:T(1,128)} %lengths.3, ...), custom_call_target="tpu_custom_call" | custom-call | flops 6442450944 | bytes 62914560 | tf_op jit(solution)/shard_map/pallas_call | solution.py:881
  104.0 65.2 %shard_map.222 = (bf16[1024,2048]{1,0:T(8,128)(2,1)}, bf16[1024,2048]{1,0:T(8,128)(2,1)}, bf16[1024,2048]{1,0:T(8,128)(2,1)}, bf16[1024,2048]{1,0:T(8,128)(2,1)}...) custom-call(bf16[256,2048]{1,0:T(8,128)(2,1)} %get-tuple-element.51.normed, bf16[256,2048]{1,0:T(8,128)(2,1)} %cotangent.5, ...), custom_call_target="tpu_custom_call" | custom-call | flops 25769803776 | bytes 62914560 | tf_op jit(solution)/shard_map/pallas_call | solution.py:1073
  169.2 77.4 %shard_map.223 = (f32[256,2048]{1,0:T(8,128)}, bf16[256,2048]{1,0:T(8,128)(2,1)}, f32[8,2048]{1,0:T(8,128)}, bf16[1024,4096]{1,0:T(8,128)(2,1)}, bf16[2,3,2048,2...) custom-call(bf16[1024,2048]{1,0:T(8,128)(2,1)} %get-tuple-element.54.slope_gate, ...), custom_call_target="tpu_custom_call" | custom-call | flops 42949672960 | bytes 83886080 | tf_op jit(solution)/shard_map/pallas_call | solution.py:1251
  246.6 112.2 %shard_map.224 = (bf16[256,2048]{1,0:T(8,128)(2,1)}, f32[8,2048]{1,0:T(8,128)}, bf16[1024,1280]{1,0:T(8,128)(2,1)}, bf16[192,4096]{1,0:T(8,128)(2,1)}) custom-call(s32[1,3]{1,0:T(1,128)} %lengths.3, f32[1,2048]{1,0:T(1,128)} %bitcast.11, bf16[256,2048]{1,0:T(8,128)(2,1)} %get-tuple-element.61.grad_mixed, bf16[1024,512]{1,0:T(8,128)(2,1)} %get-tuple-element.62.query_in, ...), custom_call_target="tpu_custom_call" | custom-call | flops 25769803776 | bytes 62914560 | tf_op jit(solution)/shard_map/pallas_call | solution.py:1492
  358.8 89.2 %shard_map.225 = (bf16[256,2048]{1,0:T(8,128)(2,1)}, f32[2,8,128]{2,1,0:T(8,128)}, bf16[64,4096]{1,0:T(8,128)(2,1)}, bf16[256,1280]{1,0:T(8,128)(2,1)}) custom-call(bf16[1024,2048]{1,0:T(8,128)(2,1)} %get-tuple-element.73.hidden_in, bf16[2048,2048]{1,0:T(8,128)(2,1)} %w_down.3, f32[256,2048]{1,0:T(8,128)} %get-tuple-element.58.state, ...), custom_call_target="tpu_custom_call" | custom-call | flops 8589934592 | bytes 20971520 | tf_op jit(solution)/shard_map/pallas_call | solution.py:1669
  448.1 0.0 copy-start
  448.1 7.0 %shard_map.226 = (f32[2048,256]{1,0:T(8,128)}, f32[256,2048]{1,0:T(8,128)}, f32[256,2048]{1,0:T(8,128)}, f32[256,512]{1,0:T(8,128)}, f32[256,128]{1,0:T(8,128)},...) custom-call(bf16[2048,256]{1,0:T(8,128)(2,1)} %get-tuple-element.60.down, ...), custom_call_target="tpu_custom_call" | custom-call | tf_op jit(solution)/shard_map/pallas_call | solution.py:1743
  455.1 0.0 copy-done
  455.1 0.1 constant_dynamic-slice_fusion
  455.2 0.5 slice_bitcast_fusion
  (1 shorter events, 0.0 us)
Async XLA Ops:
  448.1 7.0 %copy-start = (f32[2,8,128]{2,1,0:T(8,128)S(1)}, f32[2,8,128]{2,1,0:T(8,128)}, u32[]{:S(2)}) copy-start(f32[2,8,128]{2,1,0:T(8,128)} %get-tuple-element.83) | copy-start | bytes 24580

commit v5 on v4

--- a/solution.py
+++ b/solution.py
@@ -1126,14 +1126,19 @@
     chunk = down_buf.shape[1]
     chunks = units // chunk
     local = Local(local_sem)
-    load_cot = local.copy(cot_all, cot)
+
+    def load_rows_of(flip):
+        row = 1 - peers.y if flip else peers.y
+        at = pl.ds(pl.multiple_of(row * (peers.m * rows), peers.m * rows), peers.m * rows)
+        pairs = ((cot_all, cot), (slope_gate, grad_gate), (slope_up, grad_up))
+        return [local.copy(source.at[at], target.at[at]) for source, target in pairs]
 
     def load_down(k):
         source = w_down.at[pl.ds(k % chunks * chunk, chunk)]
         return local.copy(source, down_buf.at[k % 2])
 
     downs = [load_down(0)]
-    slopes = [local.copy(slope_gate, grad_gate), local.copy(slope_up, grad_up)]
+    inputs = load_rows_of(True)
     downs.append(load_down(1))
     greet(peers, core=True, chips=True)
     clock = Clock([ChipSum(grad_down, 0, chip_scratch, landing, total_down, 4.0, 72.0)])
@@ -1145,10 +1150,9 @@
         base = chunks if later else 0
         for c in range(chunks):
             downs[base + c].wait()
+            while inputs:
+                inputs.pop().wait()
             if not later:
-                load_cot.wait()
-                for load in slopes:
-                    load.wait()
                 later.extend(
                     [
                         local.copy(w_gate, gate_buf),
@@ -1162,10 +1166,11 @@
             grad_up[at, lanes] = (grad_hidden * grad_up[at, lanes].astype(F32)).astype(BF16)
             if base + c + 2 < 2 * chunks:
                 downs.append(load_down(base + c + 2))
-            clock.by(7.0 if base + c == 0 else 1.5)
+            clock.by(5.0 if base + c == 0 else 1.5)
         if base == 0:
             for load in later[:2]:
                 load.wait()
+            inputs.extend(load_rows_of(False))
         else:
             later.append(local.copy(gathered_in, cot))
         step = 512
@@ -1274,7 +1279,7 @@
             *wires(n),
             pltpu.SemaphoreType.DMA((2 * pairs,)),
             pltpu.SemaphoreType.DMA((2 * pairs,)),
-            pltpu.SemaphoreType.DMA((7 + 2 * (units // chunk) + 2 * pairs,)),
+            pltpu.SemaphoreType.DMA((10 + 2 * (units // chunk) + 2 * pairs,)),
             *chip_scratch,
         ],
         cost_estimate=pl.CostEstimate(
@@ -1706,14 +1711,14 @@
     grad_tokens[...] = tokens_in[...]
     grad_down[...] = down[...].astype(F32)
     units = grad_gate.shape[1]
-    last = pl.num_programs(0) - 1
+    last = pl.num_programs(0) * 3 // 4
 
     @pl.when(pl.program_id(0) < last)
     def _():
         grad_gate[...] = gate_up_a[:, :units].astype(F32)
         grad_up[...] = gate_up_a[:, units:].astype(F32)
 
-    @pl.when(pl.program_id(0) == last)
+    @pl.when(pl.program_id(0) >= last)
     def _():
         grad_gate[...] = gate_up_b[:, :units].astype(F32)
         grad_up[...] = gate_up_b[:, units:].astype(F32)
@@ -1730,11 +1735,11 @@
 
 def unpack(down, gate_up_a, gate_up_b, packed, output, tokens, q_width, kv_raw):
     deep, units = packed.shape[0], gate_up_a.shape[1] // 2
-    steps = 4
+    steps = 8
     rows = lambda array: (array[0] // steps, array[1])
     spec = lambda array: pl.BlockSpec(rows(array), lambda i: (i, 0))
-    early = pl.BlockSpec((deep // steps, 2 * units), lambda i: (jnp.minimum(i, steps - 2), 0))
-    late = pl.BlockSpec((deep // steps, 2 * units), lambda i: (0, 0))
+    early = pl.BlockSpec((deep // steps, 2 * units), lambda i: (jnp.minimum(i, steps * 3 // 4 - 1), 0))
+    late = pl.BlockSpec((deep // steps, 2 * units), lambda i: (jnp.maximum(i - steps * 3 // 4, 0), 0))
     flat = (
         (down.shape, F32), ((deep, units), F32), ((deep, units), F32),
         ((deep, q_width), F32), ((deep, kv_raw), F32), ((deep, kv_raw), F32),

time: 465 us -> 472 us (1.015)
  Pallas kernels: 454 us -> 462 us
where the time goes in v5:
time: 472 us; the launch traced here: 463 us
  Pallas kernels  462 us (98%)
    pallas_call x1, Pallas kernels, attend_back(): pl.pallas_call(attend_back_kernel, out_shape=(jax.ShapeDtypeStruct((rows,...  116 us
    pallas_call x1, Pallas kernels, front(): pl.pallas_call(front_kernel, out_shape=(low(group, depth), *[low(*shape)...  103 us
    pallas_call x1, Pallas kernels, layer_output(): pl.pallas_call(output_kernel, out_shape=(jax.ShapeDtypeStruct((rows, dept...  92.1 us
    pallas_call x1, Pallas kernels, hidden_back(): pl.pallas_call(hidden_back_kernel, out_shape=(jax.ShapeDtypeStruct((rows,...  76.5 us
    pallas_call x1, Pallas kernels, hidden_units(): pl.pallas_call(hidden_kernel, out_shape=(wide(depth), wide(units), wide(u...  65.1 us

profile of v5, /device:TPU:0, one launch (start us, length us, event | category | flops | bytes accessed | tf_op | source)
XLA Modules:
  0.0 463.2 jit_solution(7357166373828042845)
XLA Ops:
  0.6 103.4 %shard_map.221 = (bf16[1024,2048]{1,0:T(8,128)(2,1)}, bf16[1024,512]{1,0:T(8,128)(2,1)}, bf16[1024,256]{1,0:T(8,128)(2,1)}, bf16[1024,256]{1,0:T(8,128)(2,1)}, f...) custom-call(s32[1,3]{1,0:T(1,128)} %lengths.3, ...), custom_call_target="tpu_custom_call" | custom-call | flops 6442450944 | bytes 62914560 | tf_op jit(solution)/shard_map/pallas_call | solution.py:881
  104.0 65.1 %shard_map.222 = (bf16[1024,2048]{1,0:T(8,128)(2,1)}, bf16[1024,2048]{1,0:T(8,128)(2,1)}, bf16[1024,2048]{1,0:T(8,128)(2,1)}, bf16[1024,2048]{1,0:T(8,128)(2,1)}...) custom-call(bf16[256,2048]{1,0:T(8,128)(2,1)} %get-tuple-element.51.normed, bf16[256,2048]{1,0:T(8,128)(2,1)} %cotangent.5, ...), custom_call_target="tpu_custom_call" | custom-call | flops 25769803776 | bytes 62914560 | tf_op jit(solution)/shard_map/pallas_call | solution.py:1073
  169.1 76.5 %shard_map.223 = (f32[256,2048]{1,0:T(8,128)}, bf16[256,2048]{1,0:T(8,128)(2,1)}, f32[8,2048]{1,0:T(8,128)}, bf16[1024,4096]{1,0:T(8,128)(2,1)}, bf16[2,3,2048,2...) custom-call(bf16[1024,2048]{1,0:T(8,128)(2,1)} %get-tuple-element.54.slope_gate, ...), custom_call_target="tpu_custom_call" | custom-call | flops 42949672960 | bytes 83886080 | tf_op jit(solution)/shard_map/pallas_call | solution.py:1256
  245.5 116.5 %shard_map.224 = (bf16[256,2048]{1,0:T(8,128)(2,1)}, f32[8,2048]{1,0:T(8,128)}, bf16[1024,1280]{1,0:T(8,128)(2,1)}, bf16[192,4096]{1,0:T(8,128)(2,1)}) custom-call(s32[1,3]{1,0:T(1,128)} %lengths.3, f32[1,2048]{1,0:T(1,128)} %bitcast.11, bf16[256,2048]{1,0:T(8,128)(2,1)} %get-tuple-element.61.grad_mixed, bf16[1024,512]{1,0:T(8,128)(2,1)} %get-tuple-element.62.query_in, ...), custom_call_target="tpu_custom_call" | custom-call | flops 25769803776 | bytes 62914560 | tf_op jit(solution)/shard_map/pallas_call | solution.py:1497
  362.0 92.1 %shard_map.225 = (bf16[256,2048]{1,0:T(8,128)(2,1)}, f32[2,8,128]{2,1,0:T(8,128)}, bf16[64,4096]{1,0:T(8,128)(2,1)}, bf16[256,1280]{1,0:T(8,128)(2,1)}) custom-call(bf16[1024,2048]{1,0:T(8,128)(2,1)} %get-tuple-element.73.hidden_in, bf16[2048,2048]{1,0:T(8,128)(2,1)} %w_down.3, f32[256,2048]{1,0:T(8,128)} %get-tuple-element.58.state, ...), custom_call_target="tpu_custom_call" | custom-call | flops 8589934592 | bytes 20971520 | tf_op jit(solution)/shard_map/pallas_call | solution.py:1674
  454.2 0.0 copy-start
  454.2 8.1 %shard_map.226 = (f32[2048,256]{1,0:T(8,128)}, f32[256,2048]{1,0:T(8,128)}, f32[256,2048]{1,0:T(8,128)}, f32[256,512]{1,0:T(8,128)}, f32[256,128]{1,0:T(8,128)},...) custom-call(bf16[2048,256]{1,0:T(8,128)(2,1)} %get-tuple-element.60.down, ...), custom_call_target="tpu_custom_call" | custom-call | tf_op jit(solution)/shard_map/pallas_call | solution.py:1748
  462.3 0.0 copy-done
  462.4 0.1 constant_dynamic-slice_fusion
  462.4 0.5 slice_bitcast_fusion
  (1 shorter events, 0.0 us)
Async XLA Ops:
  454.2 8.2 %copy-start = (f32[2,8,128]{2,1,0:T(8,128)S(1)}, f32[2,8,128]{2,1,0:T(8,128)}, u32[]{:S(2)}) copy-start(f32[2,8,128]{2,1,0:T(8,128)} %get-tuple-element.83) | copy-start | bytes 24580
